TPU v7x, 32 devices: a whole 2x2x4 slice. The times are simulated.
32 devices in a mesh: bx: 8 (over z, core), by: 4 (over y, x).
Axes of the slice: x: 2, y: 2, z: 4, core: 2. Of those that a mesh axis runs over, the one named last changes fastest.
Arguments:
- tracers: float32 [2, 20, 64, 512], P(None, None, 'bx', 'by'), may hold values from -6 to 6
- velocity: float32 [2, 20, 64, 512], P(None, None, 'bx', 'by'), may hold values from -6 to 6
- wet_levels: int32 [64, 512], P('bx', 'by'), may hold values from 0 to 20, as said below
- thickness: float32 [20], replicated, may hold values from 0.1 to 1
- diagonal: float32 [64, 512], P('bx'), may hold values from 0.05 to 1
Outputs:
- new_tracers: float32 [2, 20, 64, 512], P(None, None, 'bx', 'by')
- new_velocity: float32 [2, 20, 64, 512], P(None, None, 'bx', 'by')
- surface_pressure: float32 [64, 512], P('bx', 'by')
Inputs may be any that keep to these rules, and one draw needn't show every extreme that they name: `wet_levels`: 0 marks land; a column of 20 is wet to the bottom; land covers whole blocks of 8 x 128 columns (aligned at multiples of 8 and 128), and inside ocean blocks columns may also be land.
All inputs are finite; a program needn't handle non-finite values.
Results may differ from a plain program's by a relative error of at most 0.0001.
Values sent between devices are 32-bit elements; how exact they have to be, the bound alone decides.
No kernel may reach another device: no remote copies, remote signals or barrier semaphores. Data moves between devices by JAX's collectives and lax.ppermute only.
A program may use at most 64 MiB of HBM per device.

v0:
```python
import math

import jax
import jax.numpy as jnp
from jax import lax
from jax.sharding import PartitionSpec as P

CY = 128
ITERS = 3


HEAT_ALPHA = 0.5
SALINITY_BETA = 0.8
KAPPA_SPREAD = 0.15
VISCOSITY = 0.1
TIME_INCREMENT = 0.2
GRAVITY = 1.0


def extended(array, sides, width):
    for axis, dim in sides:
        devices, length = (lax.axis_size(axis), array.shape[dim])
        up = [(i, (i + 1) % devices) for i in range(devices - 1)]
        down = [(j, i) for i, j in up]
        last = lax.slice_in_dim(array, length - width, length, axis=dim)
        first = lax.slice_in_dim(array, 0, width, axis=dim)
        before = lax.ppermute(last, axis, up)
        after = lax.ppermute(first, axis, down)
        array = jnp.concatenate([before, array, after], axis=dim)
    return array


def latitude_rate(positions, total_rows):
    return 1.5 * jnp.sin(math.pi * ((positions + 0.5) / total_rows - 0.5))


def second_derivative_sum(values, wet_indicator):
    middle = values[:, 1:-1, 1:-1]
    summed = wet_indicator[:, 2:, 1:-1] * (values[:, 2:, 1:-1] - middle)
    summed = summed + wet_indicator[:, :-2, 1:-1] * (values[:, :-2, 1:-1] - middle)
    summed = summed + wet_indicator[:, 1:-1, 2:] * (values[:, 1:-1, 2:] - middle)
    summed = summed + wet_indicator[:, 1:-1, :-2] * (values[:, 1:-1, :-2] - middle)
    return wet_indicator[:, 1:-1, 1:-1] * summed


def clinic(haloed_array, thickness, coriolis):
    theta_heat = haloed_array[0]
    salinity_amount = haloed_array[1]
    zonal_flow = haloed_array[2]
    meridional = haloed_array[3]
    wet_indicator = haloed_array[4]
    seawater_rho = SALINITY_BETA * salinity_amount - HEAT_ALPHA * theta_heat
    pressure = jnp.cumsum(thickness[:, None, None] * wet_indicator * seawater_rho, axis=0)
    wet_mid = wet_indicator[:, 1:-1, 1:-1]
    grad_x = (
        wet_mid
        * wet_indicator[:, 2:, 1:-1]
        * wet_indicator[:, :-2, 1:-1]
        * (pressure[:, 2:, 1:-1] - pressure[:, :-2, 1:-1])
        * 0.5
    )
    grad_y = (
        wet_mid
        * wet_indicator[:, 1:-1, 2:]
        * wet_indicator[:, 1:-1, :-2]
        * (pressure[:, 1:-1, 2:] - pressure[:, 1:-1, :-2])
        * 0.5
    )
    zonal_mid = zonal_flow[:, 1:-1, 1:-1]
    merid_mid = meridional[:, 1:-1, 1:-1]
    zonal_rate = wet_mid * (
        coriolis * merid_mid - grad_x + VISCOSITY * second_derivative_sum(zonal_flow, wet_indicator)
    )
    merid_rate = wet_mid * (
        -coriolis * zonal_mid
        - grad_y
        + VISCOSITY * second_derivative_sum(meridional, wet_indicator)
    )
    next_theta = theta_heat[:, 1:-1, 1:-1] + TIME_INCREMENT * KAPPA_SPREAD * second_derivative_sum(
        theta_heat, wet_indicator
    )
    next_salinity = salinity_amount[
        :, 1:-1, 1:-1
    ] + TIME_INCREMENT * KAPPA_SPREAD * second_derivative_sum(salinity_amount, wet_indicator)
    next_eastward_speed = zonal_mid + TIME_INCREMENT * zonal_rate
    next_northward_speed = merid_mid + TIME_INCREMENT * merid_rate
    weights = thickness[:, None, None] * wet_mid
    eastward_current = jnp.sum(weights * next_eastward_speed, axis=0)
    northward_current = jnp.sum(weights * next_northward_speed, axis=0)
    return (
        jnp.stack([next_theta, next_salinity]),
        jnp.stack([next_eastward_speed, next_northward_speed]),
        eastward_current,
        northward_current,
    )


def divergence(flow_x_wide, flow_y_wide, ocean_mask):
    return ocean_mask * (
        (
            flow_x_wide[2:, 1:-1]
            - flow_x_wide[:-2, 1:-1]
            + (flow_y_wide[1:-1, 2:] - flow_y_wide[1:-1, :-2])
        )
        * 0.5
    )


def stencil(padded, values, ocean_mask, diagonal):
    neighbours = padded[2:, 1:-1] + padded[:-2, 1:-1] + padded[1:-1, 2:] + padded[1:-1, :-2]
    return ocean_mask * ((4.0 + diagonal) * values - neighbours)


def block_sum(values, block_x, block_y):
    blocked = values.reshape(
        values.shape[0] // block_x, block_x, values.shape[1] // block_y, block_y
    )
    padded = jnp.pad(blocked, ((0, 0), (1, 1), (0, 0), (1, 1)))
    summed = (
        padded[:, 2:, :, 1:-1]
        + padded[:, :-2, :, 1:-1]
        + padded[:, 1:-1, :, 2:]
        + padded[:, 1:-1, :, :-2]
    )
    return summed.reshape(values.shape)


def schwarz(residual, ocean_mask, diagonal, block_x, block_y):
    centre_coef = 4.0 + diagonal
    inverse = ocean_mask / centre_coef
    first_sweep = inverse * residual
    local_image = ocean_mask * (
        centre_coef * first_sweep - block_sum(first_sweep, block_x, block_y)
    )
    return inverse * (2.0 * residual - local_image)


def widened_strip(values):
    rimmed = extended(values, (("bx", 0),), 1)
    return jnp.pad(rimmed, ((0, 0), (1, 1)))


def apply_operator(values, ocean_mask, diagonal):
    return stencil(widened_strip(values), values, ocean_mask, diagonal)


def body(tracers, velocity, wet_levels, thickness, diagonal):
    levels = tracers.shape[1]
    cols_x = wet_levels.shape[0]
    rows_y = wet_levels.shape[1]
    wet_indicator = (jnp.arange(levels, dtype=jnp.int32)[:, None, None] < wet_levels[None]).astype(
        jnp.float32
    )
    state_stack = jnp.concatenate([tracers, velocity, wet_indicator[None]], axis=0)
    row_start = lax.axis_index("by") * rows_y
    total_rows = lax.axis_size("by") * rows_y
    haloed_array = extended(state_stack, (("bx", 2), ("by", 3)), 2)
    positions = (row_start + jnp.arange(-1, rows_y + 1, dtype=jnp.int32)).astype(jnp.float32)
    cycle_tracers, cycle_velocity, eastward_current, northward_current = clinic(
        haloed_array, thickness, latitude_rate(positions, total_rows)
    )
    new_tracers = cycle_tracers[:, :, 1:-1, 1:-1]
    moved_velocity = cycle_velocity[:, :, 1:-1, 1:-1]
    forcing = divergence(eastward_current, northward_current, wet_indicator[0])
    forcing_all, ocean_all = (
        lax.all_gather(forcing, "by", axis=1, tiled=True),
        lax.all_gather(wet_indicator[0], "by", axis=1, tiled=True),
    )
    residual = forcing_all
    solution = jnp.zeros_like(forcing_all)
    direction = jnp.zeros_like(forcing_all)
    direction_image = jnp.zeros_like(forcing_all)
    inner_old = jnp.float32(1.0)
    step_old = jnp.float32(1.0)
    for iteration in range(ITERS):
        smoothed = schwarz(residual, ocean_all, diagonal, cols_x, CY)
        operator_image = apply_operator(smoothed, ocean_all, diagonal)
        inner_now, curvature = lax.psum(
            (jnp.sum(residual * smoothed), jnp.sum(smoothed * operator_image)), "bx"
        )
        if iteration == 0:
            step_size = inner_now / curvature
            direction = smoothed
            direction_image = operator_image
        else:
            conjugacy = inner_now / inner_old
            step_size = inner_now / (curvature - conjugacy * inner_now / step_old)
            direction = smoothed + conjugacy * direction
            direction_image = operator_image + conjugacy * direction_image
        solution = solution + step_size * direction
        residual = residual - step_size * direction_image
        inner_old = inner_now
        step_old = step_size
    padded_surface = widened_strip(solution)
    slope_x = (padded_surface[2:, 1:-1] - padded_surface[:-2, 1:-1]) * 0.5
    slope_y = (padded_surface[1:-1, 2:] - padded_surface[1:-1, :-2]) * 0.5
    own_x = lax.dynamic_slice_in_dim(slope_x, row_start, rows_y, axis=1)
    own_y = lax.dynamic_slice_in_dim(slope_y, row_start, rows_y, axis=1)
    slopes = jnp.stack([own_x, own_y])
    new_velocity = moved_velocity - GRAVITY * (wet_indicator[None] * slopes[:, None])
    surface_pressure = lax.dynamic_slice_in_dim(solution, row_start, rows_y, axis=1)
    return (new_tracers, new_velocity, surface_pressure)


def solution(mesh):
    placed = (
        P(None, None, "bx", "by"),
        P(None, None, "bx", "by"),
        P("bx", "by"),
        P(),
        P("bx", None),
    )
    return jax.shard_map(
        body,
        mesh=mesh,
        in_specs=placed,
        out_specs=(P(None, None, "bx", "by"), P(None, None, "bx", "by"), P("bx", "by")),
        check_vma=False,
    )
```

profile of v0, /device:TPU:0, one launch (start us, length us, event | category | flops | bytes accessed | tf_op | source)
XLA Modules:
  0.0 122.8 jit_solution(17677801461141941955)
XLA Ops:
  0.6 0.7 fusion.64
  1.3 1.2 pad_maximum_fusion.6
  2.6 2.4 %collective-permute-start = (f32[5,20,2,128]{3,2,1,0:T(2,128)S(1)}, f32[5,20,2,128]{3,2,1,0:T(2,128)S(1)}, u32[]{:S(2)}, u32[]{:S(2)}) collective-permute-start(f32[5,20,2,128]{3,2,1,0:T(2,128)S(1)} %get-tuple-element.32), channel_id=1, source_target_pairs={{0,4},{4,8},{8,12},{12,16},{16,20},{20,24},{24,28},{1,5},{5,9},{9,... | collective-permute-start | bytes 307208 | tf_op jit(solution)/shard_map/ppermute | solution.py:27
  4.9 1.3 %collective-permute-start.1 = (f32[5,20,2,128]{3,2,1,0:T(2,128)S(1)}, f32[5,20,2,128]{3,2,1,0:T(2,128)S(1)}, u32[]{:S(2)}, u32[]{:S(2)}) collective-permute-start(f32[5,20,2,128]{3,2,1,0:T(2,128)S(1)} %get-tuple-element.33), channel_id=1, source_target_pairs={{4,0},{8,4},{12,8},{16,12},{20,16},{24,20},{28,24},{5,1},{9,5},{13... | collective-permute-start | bytes 307208 | tf_op jit(solution)/shard_map/ppermute | solution.py:28
  6.2 0.7 fusion.65
  6.9 3.4 %collective-permute-done.1 = f32[5,20,2,128]{3,2,1,0:T(2,128)S(1)} collective-permute-done((f32[5,20,2,128]{3,2,1,0:T(2,128)S(1)}, f32[5,20,2,128]{3,2,1,0:T(2,128)S(1)}, u32[]{:S(2)}, u32[]{:S(2)}) %collective-permute-start.1) | collective-permute-done | bytes 102432 | tf_op jit(solution)/shard_map/ppermute | solution.py:28
  10.3 1.2 pad_maximum_fusion.1
  11.5 0.3 fusion.119
  11.8 0.5 copy.8
  12.3 3.4 %collective-permute-start.2 = (f32[5,20,12,2]{1,3,2,0:T(2,128)S(1)}, f32[5,20,12,2]{1,3,2,0:T(2,128)S(1)}, u32[]{:S(2)}, u32[]{:S(2)}) collective-permute-start(f32[5,20,12,2]{1,3,2,0:T(2,128)S(1)} %copy.8), channel_id=1, source_target_pairs={{0,1},{1,2},{2,3},{4,5},{5,6},{6,7},{8,9},{9,10},{10,11},{12,13},{... | collective-permute-start | bytes 28808 | tf_op jit(solution)/shard_map/ppermute | solution.py:27
  15.6 0.5 copy.9
  16.1 1.3 %collective-permute-start.3 = (f32[5,20,12,2]{1,3,2,0:T(2,128)S(1)}, f32[5,20,12,2]{1,3,2,0:T(2,128)S(1)}, u32[]{:S(2)}, u32[]{:S(2)}) collective-permute-start(f32[5,20,12,2]{1,3,2,0:T(2,128)S(1)} %copy.9), channel_id=1, source_target_pairs={{1,0},{2,1},{3,2},{5,4},{6,5},{7,6},{9,8},{10,9},{11,10},{13,12},{... | collective-permute-start | bytes 28808 | tf_op jit(solution)/shard_map/ppermute | solution.py:28
  17.5 10.2 %all-gather = f32[1,8,512]{2,1,0:T(8,128)S(1)} all-gather(f32[1,8,128]{2,1,0:T(8,128)S(1)} %slice.401), channel_id=2, replica_groups=mesh['bx'=8,'by'=4] {'by'}, dimensions={2}, use_global_device_ids=true | all-gather | bytes 20480 | tf_op jit(solution)/shard_map/all_gather | solution.py:167
  27.7 0.7 copy.10
  28.4 0.7 copy.11
  29.0 1.1 pad_maximum_fusion
  30.2 0.1 slice_bitcast_fusion
  30.3 0.5 copy-done.3
  30.8 0.1 fusion.54
  31.0 1.4 %multiply_reduce_fusion.1 = (f32[10,130]{1,0:T(8,128)S(1)}, f32[10,130]{1,0:T(8,128)S(1)}, f32[20,10,130]{2,1,0:T(8,128)S(1)}, f32[20,10,130]{2,1,0:T(8,128)S(1)}) fusion(f32[20,12,132]{2,1,0:T(8,128)S(1)} %get-tuple-element.28, f32[20]{0:T(128)S(1)} %copy-done.3, f32[20,12,132]{2,1,0:T(8,128)S(1)} %get-tuple-element.26, f32[20,12,132]{2,1,0:T(8,128)S(1)} %fusion.54, ...), kind=kLoop, calls=%fused_computation.80 | loop fusion | flops 1375400 | bytes 2195520 | tf_op jit(solution)/shard_map/reduce_sum | solution.py:88
  32.4 7.2 %all_gather.6 = f32[8,512]{1,0:T(8,128)S(1)} all-gather(f32[8,128]{1,0:T(8,128)S(1)} %fusion.111), channel_id=1, replica_groups=mesh['bx'=8,'by'=4] {'by'}, dimensions={1}, use_global_device_ids=true | all-gather | bytes 20480 | tf_op jit(solution)/shard_map/all_gather | solution.py:166
  39.7 0.1 fusion.74
  39.8 1.3 %collective-permute-start.4 = (f32[1,512]{1,0:T(1,128)S(1)}, f32[1,512]{1,0:T(1,128)S(1)}, u32[]{:S(2)}, u32[]{:S(2)}) collective-permute-start(f32[1,512]{1,0:T(1,128)S(1)} %get-tuple-element.45), channel_id=1, source_target_pairs={{4,0},{8,4},{12,8},{16,12},{20,16},{24,20},{28,24},{5,1},{9,5},{13... | collective-permute-start | bytes 6152 | tf_op jit(solution)/shard_map/ppermute | solution.py:28
  41.1 3.0 %collective-permute-start.5 = (f32[1,512]{1,0:T(1,128)S(1)}, f32[1,512]{1,0:T(1,128)S(1)}, u32[]{:S(2)}, u32[]{:S(2)}) collective-permute-start(f32[1,512]{1,0:T(1,128)S(1)} %get-tuple-element.44), channel_id=1, source_target_pairs={{0,4},{4,8},{8,12},{12,16},{16,20},{20,24},{24,28},{1,5},{5,9},{9,... | collective-permute-start | bytes 6152 | tf_op jit(solution)/shard_map/ppermute | solution.py:27
  44.1 0.8 collective-permute-done.5
  44.9 0.1 select_maximum_fusion.6
  45.0 0.7 multiply_reduce_fusion.5
  45.7 19.3 %all-reduce.9 = (f32[]{:T(128)}, f32[]{:T(128)}) all-reduce(f32[]{:T(128)} %get-tuple-element.10, f32[]{:T(128)} %get-tuple-element.9), channel_id=1, replica_groups=mesh['bx'=8,'by'=4] {'bx'}, use_global_device_ids=true, to_apply=%region_4.5 | all-reduce | flops 2 | bytes 16 | tf_op jit(solution)/shard_map/psum | solution.py:178
  66.3 0.1 fusion.82
  66.4 1.3 %collective-permute-start.6 = (f32[1,512]{1,0:T(1,128)S(1)}, f32[1,512]{1,0:T(1,128)S(1)}, u32[]{:S(2)}, u32[]{:S(2)}) collective-permute-start(f32[1,512]{1,0:T(1,128)S(1)} %get-tuple-element.43), channel_id=1, source_target_pairs={{4,0},{8,4},{12,8},{16,12},{20,16},{24,20},{28,24},{5,1},{9,5},{13... | collective-permute-start | bytes 6152 | tf_op jit(solution)/shard_map/ppermute | solution.py:28
  67.7 3.0 %collective-permute-start.7 = (f32[1,512]{1,0:T(1,128)S(1)}, f32[1,512]{1,0:T(1,128)S(1)}, u32[]{:S(2)}, u32[]{:S(2)}) collective-permute-start(f32[1,512]{1,0:T(1,128)S(1)} %get-tuple-element.42), channel_id=1, source_target_pairs={{0,4},{4,8},{8,12},{12,16},{16,20},{20,24},{24,28},{1,5},{5,9},{9,... | collective-permute-start | bytes 6152 | tf_op jit(solution)/shard_map/ppermute | solution.py:27
  70.7 0.7 fusion.48
  71.5 0.1 select_maximum_fusion.4
  71.6 0.8 multiply_reduce_fusion.3
  72.4 14.5 %all-reduce.8 = (f32[]{:T(128)}, f32[]{:T(128)}) all-reduce(f32[]{:T(128)} %get-tuple-element.8, f32[]{:T(128)} %get-tuple-element.7), channel_id=1, replica_groups=mesh['bx'=8,'by'=4] {'bx'}, use_global_device_ids=true, to_apply=%region_8.9 | all-reduce | flops 2 | bytes 16 | tf_op jit(solution)/shard_map/psum | solution.py:178
  91.3 0.1 fusion.90
  91.4 1.3 %collective-permute-start.8 = (f32[1,512]{1,0:T(1,128)S(1)}, f32[1,512]{1,0:T(1,128)S(1)}, u32[]{:S(2)}, u32[]{:S(2)}) collective-permute-start(f32[1,512]{1,0:T(1,128)S(1)} %get-tuple-element.41), channel_id=1, source_target_pairs={{4,0},{8,4},{12,8},{16,12},{20,16},{24,20},{28,24},{5,1},{9,5},{13... | collective-permute-start | bytes 6152 | tf_op jit(solution)/shard_map/ppermute | solution.py:28
  92.7 3.0 %collective-permute-start.9 = (f32[1,512]{1,0:T(1,128)S(1)}, f32[1,512]{1,0:T(1,128)S(1)}, u32[]{:S(2)}, u32[]{:S(2)}) collective-permute-start(f32[1,512]{1,0:T(1,128)S(1)} %get-tuple-element.40), channel_id=1, source_target_pairs={{0,4},{4,8},{8,12},{12,16},{16,20},{20,24},{24,28},{1,5},{5,9},{9,... | collective-permute-start | bytes 6152 | tf_op jit(solution)/shard_map/ppermute | solution.py:27
  95.7 0.7 fusion.37
  96.5 0.1 select_maximum_fusion.2
  96.6 0.7 fusion.94
  97.3 15.0 %all-reduce.7 = (f32[]{:T(128)}, f32[]{:T(128)}) all-reduce(f32[]{:T(128)} %get-tuple-element.6, f32[]{:T(128)} %get-tuple-element.5), channel_id=1, replica_groups=mesh['bx'=8,'by'=4] {'bx'}, use_global_device_ids=true, to_apply=%region_12.13 | all-reduce | flops 2 | bytes 16 | tf_op jit(solution)/shard_map/psum | solution.py:178
  116.1 1.3 %collective-permute-start.10 = (f32[1,512]{1,0:T(1,128)S(1)}, f32[1,512]{1,0:T(1,128)S(1)}, u32[]{:S(2)}, u32[]{:S(2)}) collective-permute-start(f32[1,512]{1,0:T(1,128)S(1)} %get-tuple-element.39), channel_id=1, source_target_pairs={{4,0},{8,4},{12,8},{16,12},{20,16},{24,20},{28,24},{5,1},{9,5},{13... | collective-permute-start | bytes 6152 | tf_op jit(solution)/shard_map/ppermute | solution.py:28
  117.4 3.0 %collective-permute-start.11 = (f32[1,512]{1,0:T(1,128)S(1)}, f32[1,512]{1,0:T(1,128)S(1)}, u32[]{:S(2)}, u32[]{:S(2)}) collective-permute-start(f32[1,512]{1,0:T(1,128)S(1)} %get-tuple-element.38), channel_id=1, source_target_pairs={{0,4},{4,8},{8,12},{12,16},{16,20},{20,24},{24,28},{1,5},{5,9},{9,... | collective-permute-start | bytes 6152 | tf_op jit(solution)/shard_map/ppermute | solution.py:27
  120.4 0.8 pad_maximum_fusion.3
  121.2 0.1 select_maximum_fusion
  121.4 0.6 constant_dynamic-slice_fusion
  122.0 0.8 fusion.60
  (31 shorter events, 0.4 us)
Async XLA Ops:
  2.6 4.4 %collective-permute-start = (f32[5,20,2,128]{3,2,1,0:T(2,128)S(1)}, f32[5,20,2,128]{3,2,1,0:T(2,128)S(1)}, u32[]{:S(2)}, u32[]{:S(2)}) collective-permute-start(f32[5,20,2,128]{3,2,1,0:T(2,128)S(1)} %get-tuple-element.32), channel_id=1, source_target_pairs={{0,4},{4,8},{8,12},{12,16},{16,20},{20,24},{24,28},{1,5},{5,9},{9,... | collective-permute-start | bytes 307208 | tf_op jit(solution)/shard_map/ppermute | solution.py:27
  4.9 5.4 %collective-permute-start.1 = (f32[5,20,2,128]{3,2,1,0:T(2,128)S(1)}, f32[5,20,2,128]{3,2,1,0:T(2,128)S(1)}, u32[]{:S(2)}, u32[]{:S(2)}) collective-permute-start(f32[5,20,2,128]{3,2,1,0:T(2,128)S(1)} %get-tuple-element.33), channel_id=1, source_target_pairs={{4,0},{8,4},{12,8},{16,12},{20,16},{24,20},{28,24},{5,1},{9,5},{13... | collective-permute-start | bytes 307208 | tf_op jit(solution)/shard_map/ppermute | solution.py:28
  11.7 17.3 %copy-start = (f32[2,20,8,128]{3,2,1,0:T(8,128)S(1)}, f32[2,20,8,128]{3,2,1,0:T(8,128)}, u32[]{:S(2)}) copy-start(f32[2,20,8,128]{3,2,1,0:T(8,128)} %param.6) | copy-start | bytes 491524
  11.8 17.3 %copy-start.1 = (f32[2,20,8,128]{3,2,1,0:T(8,128)S(1)}, f32[2,20,8,128]{3,2,1,0:T(8,128)}, u32[]{:S(2)}) copy-start(f32[2,20,8,128]{3,2,1,0:T(8,128)} %param.5) | copy-start | bytes 491524
  12.3 15.4 %collective-permute-start.2 = (f32[5,20,12,2]{1,3,2,0:T(2,128)S(1)}, f32[5,20,12,2]{1,3,2,0:T(2,128)S(1)}, u32[]{:S(2)}, u32[]{:S(2)}) collective-permute-start(f32[5,20,12,2]{1,3,2,0:T(2,128)S(1)} %copy.8), channel_id=1, source_target_pairs={{0,1},{1,2},{2,3},{4,5},{5,6},{6,7},{8,9},{9,10},{10,11},{12,13},{... | collective-permute-start | bytes 28808 | tf_op jit(solution)/shard_map/ppermute | solution.py:27
  16.1 12.2 %collective-permute-start.3 = (f32[5,20,12,2]{1,3,2,0:T(2,128)S(1)}, f32[5,20,12,2]{1,3,2,0:T(2,128)S(1)}, u32[]{:S(2)}, u32[]{:S(2)}) collective-permute-start(f32[5,20,12,2]{1,3,2,0:T(2,128)S(1)} %copy.9), channel_id=1, source_target_pairs={{1,0},{2,1},{3,2},{5,4},{6,5},{7,6},{9,8},{10,9},{11,10},{13,12},{... | collective-permute-start | bytes 28808 | tf_op jit(solution)/shard_map/ppermute | solution.py:28
  30.2 0.7 copy-start.3
  30.9 8.7 %copy-start.2 = (f32[8,512]{1,0:T(8,128)S(1)}, f32[8,512]{1,0:T(8,128)}, u32[]{:S(2)}) copy-start(f32[8,512]{1,0:T(8,128)} %param.9) | copy-start | bytes 49156
  39.8 4.3 %collective-permute-start.4 = (f32[1,512]{1,0:T(1,128)S(1)}, f32[1,512]{1,0:T(1,128)S(1)}, u32[]{:S(2)}, u32[]{:S(2)}) collective-permute-start(f32[1,512]{1,0:T(1,128)S(1)} %get-tuple-element.45), channel_id=1, source_target_pairs={{4,0},{8,4},{12,8},{16,12},{20,16},{24,20},{28,24},{5,1},{9,5},{13... | collective-permute-start | bytes 6152 | tf_op jit(solution)/shard_map/ppermute | solution.py:28
  41.1 3.8 %collective-permute-start.5 = (f32[1,512]{1,0:T(1,128)S(1)}, f32[1,512]{1,0:T(1,128)S(1)}, u32[]{:S(2)}, u32[]{:S(2)}) collective-permute-start(f32[1,512]{1,0:T(1,128)S(1)} %get-tuple-element.44), channel_id=1, source_target_pairs={{0,4},{4,8},{8,12},{12,16},{16,20},{20,24},{24,28},{1,5},{5,9},{9,... | collective-permute-start | bytes 6152 | tf_op jit(solution)/shard_map/ppermute | solution.py:27
  66.4 5.1 %collective-permute-start.6 = (f32[1,512]{1,0:T(1,128)S(1)}, f32[1,512]{1,0:T(1,128)S(1)}, u32[]{:S(2)}, u32[]{:S(2)}) collective-permute-start(f32[1,512]{1,0:T(1,128)S(1)} %get-tuple-element.43), channel_id=1, source_target_pairs={{4,0},{8,4},{12,8},{16,12},{20,16},{24,20},{28,24},{5,1},{9,5},{13... | collective-permute-start | bytes 6152 | tf_op jit(solution)/shard_map/ppermute | solution.py:28
  67.7 3.8 %collective-permute-start.7 = (f32[1,512]{1,0:T(1,128)S(1)}, f32[1,512]{1,0:T(1,128)S(1)}, u32[]{:S(2)}, u32[]{:S(2)}) collective-permute-start(f32[1,512]{1,0:T(1,128)S(1)} %get-tuple-element.42), channel_id=1, source_target_pairs={{0,4},{4,8},{8,12},{12,16},{16,20},{20,24},{24,28},{1,5},{5,9},{9,... | collective-permute-start | bytes 6152 | tf_op jit(solution)/shard_map/ppermute | solution.py:27
  91.4 5.1 %collective-permute-start.8 = (f32[1,512]{1,0:T(1,128)S(1)}, f32[1,512]{1,0:T(1,128)S(1)}, u32[]{:S(2)}, u32[]{:S(2)}) collective-permute-start(f32[1,512]{1,0:T(1,128)S(1)} %get-tuple-element.41), channel_id=1, source_target_pairs={{4,0},{8,4},{12,8},{16,12},{20,16},{24,20},{28,24},{5,1},{9,5},{13... | collective-permute-start | bytes 6152 | tf_op jit(solution)/shard_map/ppermute | solution.py:28
  92.7 3.8 %collective-permute-start.9 = (f32[1,512]{1,0:T(1,128)S(1)}, f32[1,512]{1,0:T(1,128)S(1)}, u32[]{:S(2)}, u32[]{:S(2)}) collective-permute-start(f32[1,512]{1,0:T(1,128)S(1)} %get-tuple-element.40), channel_id=1, source_target_pairs={{0,4},{4,8},{8,12},{12,16},{16,20},{20,24},{24,28},{1,5},{5,9},{9,... | collective-permute-start | bytes 6152 | tf_op jit(solution)/shard_map/ppermute | solution.py:27
  116.1 5.1 %collective-permute-start.10 = (f32[1,512]{1,0:T(1,128)S(1)}, f32[1,512]{1,0:T(1,128)S(1)}, u32[]{:S(2)}, u32[]{:S(2)}) collective-permute-start(f32[1,512]{1,0:T(1,128)S(1)} %get-tuple-element.39), channel_id=1, source_target_pairs={{4,0},{8,4},{12,8},{16,12},{20,16},{24,20},{28,24},{5,1},{9,5},{13... | collective-permute-start | bytes 6152 | tf_op jit(solution)/shard_map/ppermute | solution.py:28
  117.4 3.8 %collective-permute-start.11 = (f32[1,512]{1,0:T(1,128)S(1)}, f32[1,512]{1,0:T(1,128)S(1)}, u32[]{:S(2)}, u32[]{:S(2)}) collective-permute-start(f32[1,512]{1,0:T(1,128)S(1)} %get-tuple-element.38), channel_id=1, source_target_pairs={{0,4},{4,8},{8,12},{12,16},{16,20},{20,24},{24,28},{1,5},{5,9},{9,... | collective-permute-start | bytes 6152 | tf_op jit(solution)/shard_map/ppermute | solution.py:27
where the time goes:
time: 124 us; the launch traced here: 123 us
  blocking collectives  66.2 us (53%)
  starting transfers between devices  25.6 us (21%)
  other arithmetic  13 us (10%)
  between operations  10.4 us (8%)
  waiting for transfers between devices  4.29 us (3%)
  local copies, waits for them, and re-layouts  3.33 us (3%)
    psum x3, blocking collectives, body(): lax.psum((jnp.sum(residual * smoothed), jnp.sum(smoothed * operator_image...  48.7 us
    ppermute x6, starting transfers between devices, extended(): before = lax.ppermute(last, axis, up)  17.9 us
    all_gather x1, blocking collectives, body(): lax.all_gather(wet_indicator[0], 'by', axis=1, tiled=True)  10.2 us
    ppermute x6, starting transfers between devices, extended(): after = lax.ppermute(first, axis, down)  7.74 us
    all_gather x1, blocking collectives, body(): lax.all_gather(forcing, 'by', axis=1, tiled=True)  7.22 us
    ppermute x6, waiting for transfers between devices, extended(): after = lax.ppermute(first, axis, down)  3.4 us
    concatenate x6, other arithmetic, extended(): array = jnp.concatenate([before, array, after], axis=dim)  2.63 us
  transfers between devices with their start and end apart: 12, of which 2 were waited for; matrix products, arithmetic and copies ran while one was open for 3% of the time, Pallas kernels for 0%

commit v1 on v0

v1 whole, which is shorter than its diff:
```python
import math

import jax
import jax.numpy as jnp
from jax import lax
from jax.experimental import pallas as pl
from jax.experimental.pallas import tpu as pltpu
from jax.sharding import PartitionSpec as P

ITERS = 3

HEAT_ALPHA = 0.5
SALINITY_BETA = 0.8
KAPPA_SPREAD = 0.15
VISCOSITY = 0.1
TIME_INCREMENT = 0.2
GRAVITY = 1.0

VMEM = pl.BlockSpec(memory_space=pltpu.VMEM)
SMEM = pl.BlockSpec(memory_space=pltpu.SMEM)


def lanes_of(shape):
    return lax.broadcasted_iota(jnp.int32, shape, 1)


def sublanes_of(shape):
    return lax.broadcasted_iota(jnp.int32, shape, 0)


def pack_rims(tracers, velocity, wet, first_rows, last_rows, first_cols, last_cols):
    levels, cols_x, rows_y = tracers.shape[1:]
    lane = lanes_of((cols_x, rows_y))
    counts = wet[...].astype(jnp.float32)
    first, last = jnp.zeros_like(counts), jnp.zeros_like(counts)
    for index in range(4 * levels + 1):
        field, level = divmod(index, levels)
        if field < 4:
            tile = (tracers if field < 2 else velocity)[field % 2, level]
        else:
            tile = counts
        first_rows[index : index + 1, :] = tile[0:1, :]
        last_rows[index : index + 1, :] = tile[cols_x - 1 : cols_x, :]
        first = jnp.where(lane == index, tile[:, 0:1], first)
        last = jnp.where(lane == index, tile[:, rows_y - 1 : rows_y], last)
    first_cols[...] = first
    last_cols[...] = last


def level_kernel(
    tracers, velocity, wet, diagonal, thickness, latitude, x_before, x_after, y_before, y_after,
    new_tracers, moved_velocity, surface,
):
    levels, cols_x, rows_y = tracers.shape[1:]
    shape = (cols_x, rows_y)
    lane, sublane = (lanes_of(shape), sublanes_of(shape))
    low_x, high_x = (sublane == 0, sublane == cols_x - 1)
    low_y, high_y = (lane == 0, lane == rows_y - 1)
    before_cols, after_cols = (y_before[...], y_after[...])

    def neighbours(tile, index):
        return (
            jnp.where(high_x, x_after[index : index + 1, :], pltpu.roll(tile, cols_x - 1, 0)),
            jnp.where(low_x, x_before[index : index + 1, :], pltpu.roll(tile, 1, 0)),
            jnp.where(high_y, after_cols[:, index : index + 1], pltpu.roll(tile, rows_y - 1, 1)),
            jnp.where(low_y, before_cols[:, index : index + 1], pltpu.roll(tile, 1, 1)),
        )

    counts = wet[...].astype(jnp.float32)
    around = neighbours(counts, 4 * levels)
    shared = [jnp.minimum(counts, other) for other in around]
    both_x = jnp.minimum(shared[0], shared[1])
    both_y = jnp.minimum(shared[2], shared[3])
    coriolis = jnp.broadcast_to(latitude[...], shape)
    zero = jnp.zeros(shape, jnp.float32)
    difference_x, difference_y, flow_x, flow_y = (zero, zero, zero, zero)
    for level in range(levels):
        here = counts > level
        open_to = [other > level for other in shared]
        wet_around = [other > level for other in around]
        weight = thickness[level]
        heat, salt = (tracers[0, level], tracers[1, level])
        zonal, merid = (velocity[0, level], velocity[1, level])
        heat_around = neighbours(heat, level)
        salt_around = neighbours(salt, levels + level)

        def laplacian(tile, others):
            total = zero
            for other, passable in zip(others, open_to):
                total = total + jnp.where(passable, other - tile, 0.0)
            return total

        loads = [
            jnp.where(is_wet, SALINITY_BETA * s - HEAT_ALPHA * t, 0.0)
            for is_wet, s, t in zip(wet_around, salt_around, heat_around)
        ]
        difference_x = difference_x + weight * (loads[0] - loads[1])
        difference_y = difference_y + weight * (loads[2] - loads[3])
        gradient_x = jnp.where(both_x > level, difference_x * 0.5, 0.0)
        gradient_y = jnp.where(both_y > level, difference_y * 0.5, 0.0)
        diffusivity = TIME_INCREMENT * KAPPA_SPREAD
        new_tracers[0, level] = heat + diffusivity * laplacian(heat, heat_around)
        new_tracers[1, level] = salt + diffusivity * laplacian(salt, salt_around)
        spread_x = laplacian(zonal, neighbours(zonal, 2 * levels + level))
        spread_y = laplacian(merid, neighbours(merid, 3 * levels + level))
        zonal_rate = coriolis * merid - gradient_x + VISCOSITY * spread_x
        merid_rate = -coriolis * zonal - gradient_y + VISCOSITY * spread_y
        next_zonal = zonal + jnp.where(here, TIME_INCREMENT * zonal_rate, 0.0)
        next_merid = merid + jnp.where(here, TIME_INCREMENT * merid_rate, 0.0)
        moved_velocity[0, level] = next_zonal
        moved_velocity[1, level] = next_merid
        flow_x = flow_x + jnp.where(here, weight * next_zonal, 0.0)
        flow_y = flow_y + jnp.where(here, weight * next_merid, 0.0)
    row_start = pl.multiple_of(lax.axis_index("by") * rows_y, rows_y)
    surface[0] = flow_x
    surface[1] = flow_y
    surface[2] = jnp.where(counts > 0, 1.0, 0.0)
    surface[3] = diagonal[:, pl.ds(row_start, rows_y)]


def solve_kernel(
    blocks_x, blocks_y, gathered, moved_velocity, wet,
    new_velocity, pressure,
    inverse, residual, smooth_0, smooth_1, smooth_2, image_0, image_1, direction_1,
):
    cols_x, rows_y = gathered.shape[2:]
    levels = moved_velocity.shape[1]
    shape = (cols_x, rows_y)
    lane, sublane = (lanes_of(shape), sublanes_of(shape))
    low_x, high_x = (sublane == 0, sublane == cols_x - 1)
    low_y, high_y = (lane == 0, lane == rows_y - 1)
    zero = jnp.zeros(shape, jnp.float32)

    def each_row(step, carry):
        if blocks_x <= 8:
            for row in range(blocks_x):
                carry = step(row, carry)
            return carry
        return lax.fori_loop(0, blocks_x, step, carry)

    def guarded(load, row, column):
        if isinstance(row, int):
            return load(row * blocks_y + column) if 0 <= row < blocks_x else zero
        inside = jnp.logical_and(row >= 0, row < blocks_x)
        return load(jnp.clip(row, 0, blocks_x - 1) * blocks_y + column) * inside.astype(jnp.float32)

    def after_x(load, tile, row, column):
        other = guarded(load, row + 1, column)
        return jnp.where(high_x, pltpu.roll(other, cols_x - 1, 0), pltpu.roll(tile, cols_x - 1, 0))

    def before_x(load, tile, row, column):
        other = guarded(load, row - 1, column)
        return jnp.where(low_x, pltpu.roll(other, 1, 0), pltpu.roll(tile, 1, 0))

    def along_y(tiles):
        ahead = [pltpu.roll(tile, rows_y - 1, 1) for tile in tiles] + [zero]
        behind = [zero] + [pltpu.roll(tile, 1, 1) for tile in tiles]
        after = [jnp.where(high_y, ahead[c + 1], ahead[c]) for c in range(blocks_y)]
        before = [jnp.where(low_y, behind[c], behind[c + 1]) for c in range(blocks_y)]
        return after, before

    def smoothed_by(inv, tile):
        first = inv * tile
        near = jnp.where(high_x, 0.0, pltpu.roll(first, cols_x - 1, 0))
        near = near + jnp.where(low_x, 0.0, pltpu.roll(first, 1, 0))
        near = near + jnp.where(high_y, 0.0, pltpu.roll(first, rows_y - 1, 1))
        near = near + jnp.where(low_y, 0.0, pltpu.roll(first, 1, 1))
        return inv * (tile + near)

    def total(values):
        return jnp.sum(values, axis=(0, 1), keepdims=True)

    def start(row, carry):
        flow_y = [gathered[row * blocks_y + c, 1] for c in range(blocks_y)]
        after, before = along_y(flow_y)
        for column in range(blocks_y):
            index = row * blocks_y + column
            flow = gathered[index, 0]
            load = lambda i: gathered[i, 0]
            slope = after_x(load, flow, row, column) - before_x(load, flow, row, column)
            ocean = gathered[index, 2]
            forcing = ocean * ((slope + (after[column] - before[column])) * 0.5)
            inv = ocean / (4.0 + gathered[index, 3])
            inverse[index] = inv
            residual[index] = forcing
            smooth_0[index] = smoothed_by(inv, forcing)
        return carry

    def operate(smooth, image):
        def step(row, carry):
            inner, curvature = carry
            tiles = [smooth[row * blocks_y + c] for c in range(blocks_y)]
            after, before = along_y(tiles)
            for column in range(blocks_y):
                index = row * blocks_y + column
                tile = tiles[column]
                load = lambda i: smooth[i]
                near = after_x(load, tile, row, column) + before_x(load, tile, row, column)
                near = near + after[column] + before[column]
                centre = 4.0 + gathered[index, 3]
                result = gathered[index, 2] * (centre * tile - near)
                if image is not None:
                    image[index] = result
                inner = inner + residual[index] * tile
                curvature = curvature + tile * result
            return inner, curvature

        inner, curvature = each_row(step, (zero, zero))
        return total(inner), total(curvature)

    each_row(start, 0)
    inner_0, curvature_0 = operate(smooth_0, image_0)
    step_0 = inner_0 / curvature_0

    def advance_0(row, carry):
        for column in range(blocks_y):
            index = row * blocks_y + column
            left = residual[index] - step_0 * image_0[index]
            residual[index] = left
            smooth_1[index] = smoothed_by(inverse[index], left)
        return carry

    each_row(advance_0, 0)
    inner_1, curvature_1 = operate(smooth_1, image_1)
    turn_1 = inner_1 / inner_0
    step_1 = inner_1 / (curvature_1 - turn_1 * inner_1 / step_0)

    def advance_1(row, carry):
        for column in range(blocks_y):
            index = row * blocks_y + column
            direction_1[index] = smooth_1[index] + turn_1 * smooth_0[index]
            image = image_1[index] + turn_1 * image_0[index]
            left = residual[index] - step_1 * image
            residual[index] = left
            smooth_2[index] = smoothed_by(inverse[index], left)
        return carry

    each_row(advance_1, 0)
    inner_2, curvature_2 = operate(smooth_2, None)
    turn_2 = inner_2 / inner_1
    step_2 = inner_2 / (curvature_2 - turn_2 * inner_2 / step_1)

    def iterate(index):
        previous = direction_1[index]
        result = step_0 * smooth_0[index] + step_1 * previous
        return result + step_2 * (smooth_2[index] + turn_2 * previous)

    own_x, own_y = (lax.axis_index("bx"), lax.axis_index("by"))

    def block(shift_x, shift_y):
        row, column = (own_x + shift_x, own_y + shift_y)
        inside = (row >= 0) & (row < blocks_x) & (column >= 0) & (column < blocks_y)
        row, column = (jnp.clip(row, 0, blocks_x - 1), jnp.clip(column, 0, blocks_y - 1))
        return jnp.where(inside, iterate(row * blocks_y + column), 0.0)

    own = iterate(own_x * blocks_y + own_y)
    pressure[...] = own
    upper = jnp.where(high_x, pltpu.roll(block(1, 0), cols_x - 1, 0), pltpu.roll(own, cols_x - 1, 0))
    lower = jnp.where(low_x, pltpu.roll(block(-1, 0), 1, 0), pltpu.roll(own, 1, 0))
    slope_x = GRAVITY * ((upper - lower) * 0.5)
    upper = jnp.where(high_y, pltpu.roll(block(0, 1), rows_y - 1, 1), pltpu.roll(own, rows_y - 1, 1))
    lower = jnp.where(low_y, pltpu.roll(block(0, -1), 1, 1), pltpu.roll(own, 1, 1))
    slope_y = GRAVITY * ((upper - lower) * 0.5)
    counts = wet[...]
    for level in range(levels):
        here = counts > level
        new_velocity[0, level] = moved_velocity[0, level] - jnp.where(here, slope_x, 0.0)
        new_velocity[1, level] = moved_velocity[1, level] - jnp.where(here, slope_y, 0.0)


def latitude_rate(positions, total_rows):
    return 1.5 * jnp.sin(math.pi * ((positions + 0.5) / total_rows - 0.5))


def body(tracers, velocity, wet_levels, thickness, diagonal):
    levels = tracers.shape[1]
    cols_x, rows_y = wet_levels.shape
    blocks_x, blocks_y = (lax.axis_size("bx"), lax.axis_size("by"))
    blocks = blocks_x * blocks_y
    shape = (cols_x, rows_y)
    rim_rows = 4 * levels + 1

    def like(*dims):
        return jax.ShapeDtypeStruct(dims, jnp.float32)

    first_rows, last_rows, first_cols, last_cols = pl.pallas_call(
        pack_rims,
        out_shape=[like(rim_rows, rows_y)] * 2 + [like(*shape)] * 2,
        in_specs=[VMEM] * 3,
        out_specs=[VMEM] * 4,
    )(tracers, velocity, wet_levels)

    def neighbours_of(axis, first, last):
        up = [(i, i + 1) for i in range(lax.axis_size(axis) - 1)]
        down = [(j, i) for i, j in up]
        return lax.ppermute(last, axis, up), lax.ppermute(first, axis, down)

    y_before, y_after = neighbours_of("by", first_cols, last_cols)
    x_before, x_after = neighbours_of("bx", first_rows, last_rows)
    positions = (lax.axis_index("by") * rows_y + jnp.arange(rows_y, dtype=jnp.int32)).astype(jnp.float32)
    latitude = latitude_rate(positions, blocks_y * rows_y)[None]

    new_tracers, moved_velocity, surface = pl.pallas_call(
        level_kernel,
        out_shape=[like(*tracers.shape), like(*velocity.shape), like(4, *shape)],
        in_specs=[VMEM] * 4 + [SMEM] + [VMEM] * 5,
        out_specs=[VMEM] * 3,
    )(
        tracers, velocity, wet_levels, diagonal, thickness, latitude,
        x_before, x_after, y_before, y_after,
    )
    gathered = lax.all_gather(surface, ("bx", "by"), axis=0, tiled=False)

    def solve(*refs):
        solve_kernel(blocks_x, blocks_y, *refs)

    new_velocity, pressure = pl.pallas_call(
        solve,
        out_shape=[like(*velocity.shape), like(*shape)],
        in_specs=[VMEM] * 3,
        out_specs=[VMEM] * 2,
        scratch_shapes=[pltpu.VMEM((blocks, *shape), jnp.float32)] * 8,
        compiler_params=pltpu.CompilerParams(vmem_limit_bytes=(4 + 52 * blocks // 1024) * 2**20),
    )(gathered, moved_velocity, wet_levels)
    return new_tracers, new_velocity, pressure


def solution(mesh):
    placed = (
        P(None, None, "bx", "by"),
        P(None, None, "bx", "by"),
        P("bx", "by"),
        P(),
        P("bx", None),
    )
    return jax.shard_map(
        body,
        mesh=mesh,
        in_specs=placed,
        out_specs=(P(None, None, "bx", "by"), P(None, None, "bx", "by"), P("bx", "by")),
        check_vma=False,
    )
```

time: 124 us -> 91.9 us (0.74)
  starting transfers between devices: 25.6 us -> 8.88 us
  other arithmetic: 13 us -> 0.56 us
  between operations: 10.4 us -> 0.69 us
  Pallas kernels: 0 us -> 5.92 us
  blocking collectives: 66.2 us -> 71.8 us
  local copies, waits for them, and re-layouts: 3.33 us -> 0.63 us
    all_gather x2 -> x1, blocking collectives: 17.4 us -> 71.8 us  [body(): gathered = lax.all_gather(surface, ('bx', 'by'), axis=0, tiled=False)]
    psum x3 -> x0, blocking collectives: 48.7 us -> none  [body(): lax.psum((jnp.sum(residual * smoothed), jnp.sum(smoothed * operator_image...]
    ppermute x12 -> x4, starting transfers between devices: 25.6 us -> 8.88 us  [neighbours_of(): return (lax.ppermute(last, axis, up), lax.ppermute(first, axis, down))]
    pallas_call x0 -> x3, Pallas kernels: none -> 5.92 us  [the longest x1 2.22 us: body(): pl.pallas_call(level_kernel, out_shape=[like(*tracers.shape), like(*veloc...]
    reduce_sum x4 -> x0, other arithmetic: 3.53 us -> none  [the longest x3 2.14 us: body(): jnp.sum(smoothed * operator_image)]
    concatenate x6 -> x0, other arithmetic: 2.63 us -> none  [extended(): array = jnp.concatenate([before, array, after], axis=dim)]
    another operation x6 -> x0, other arithmetic: 2.39 us -> none  [the longest x3 2.28 us: clinic(): jnp.stack([next_theta, next_salinity])]
    convert_element_type x2 -> x0, other arithmetic: 1.39 us -> none  [body(): (jnp.arange(levels, dtype=jnp.int32)[:, None, None] < wet_levels[None]).a...]
  transfers between devices with their start and end apart: 12 -> 4, of which waited for: 2 -> 2; matrix products, arithmetic and copies ran while one was open for 3% -> 1% of each run, Pallas kernels for 0% -> 0%
where the time goes in v1:
time: 91.9 us; the launch traced here: 91.6 us
  blocking collectives  71.8 us (78%)
  starting transfers between devices  8.88 us (10%)
  Pallas kernels  5.92 us (6%)
  waiting for transfers between devices  3.09 us (3%)
    all_gather x1, blocking collectives, body(): gathered = lax.all_gather(surface, ('bx', 'by'), axis=0, tiled=False)  71.8 us
    ppermute x4, starting transfers between devices, neighbours_of(): return (lax.ppermute(last, axis, up), lax.ppermute(first, axis, down))  8.88 us
    ppermute x4, waiting for transfers between devices, neighbours_of(): return (lax.ppermute(last, axis, up), lax.ppermute(first, axis, down))  3.09 us
    pallas_call x1, Pallas kernels, body(): pl.pallas_call(level_kernel, out_shape=[like(*tracers.shape), like(*veloc...  2.22 us
    pallas_call x1, Pallas kernels, body(): pl.pallas_call(solve, out_shape=[like(*velocity.shape), like(*shape)], in...  1.87 us
  transfers between devices with their start and end apart: 4, of which 2 were waited for; matrix products, arithmetic and copies ran while one was open for 1% of the time, Pallas kernels for 0%

profile of v1, /device:TPU:0, one launch (start us, length us, event | category | flops | bytes accessed | tf_op | source)
XLA Modules:
  0.0 91.6 jit_solution(13007874779818456980)
XLA Ops:
  0.6 1.8 %shard_map.76 = (f32[81,128]{1,0:T(8,128)}, f32[81,128]{1,0:T(8,128)}, f32[8,128]{1,0:T(8,128)}, f32[8,128]{1,0:T(8,128)}) custom-call(f32[2,20,8,128]{3,2,1,0:T(8,128)} %tracers.3, f32[2,20,8,128]{3,2,1,0:T(8,128)} %velocity.3, s32[8,128]{1,0:T(8,128)} %refs_2_.1), custom_call_target="tpu_custom_call" | custom-call | tf_op jit(solution)/shard_map/pallas_call | solution.py:286
  2.5 4.8 %collective-permute-start.2 = (f32[8,128]{1,0:T(8,128)}, f32[8,128]{1,0:T(8,128)S(1)}, u32[]{:S(2)}, u32[]{:S(2)}) collective-permute-start(f32[8,128]{1,0:T(8,128)} %get-tuple-element.14), channel_id=1, source_target_pairs={{0,1},{1,2},{2,3},{4,5},{5,6},{6,7},{8,9},{9,10},{10,11},{12,13},{... | collective-permute-start | bytes 12296 | tf_op jit(solution)/shard_map/ppermute | solution.py:296
  7.3 1.3 %collective-permute-start.3 = (f32[8,128]{1,0:T(8,128)}, f32[8,128]{1,0:T(8,128)S(1)}, u32[]{:S(2)}, u32[]{:S(2)}) collective-permute-start(f32[8,128]{1,0:T(8,128)} %get-tuple-element.15), channel_id=1, source_target_pairs={{1,0},{2,1},{3,2},{5,4},{6,5},{7,6},{9,8},{10,9},{11,10},{13,12},{... | collective-permute-start | bytes 12296 | tf_op jit(solution)/shard_map/ppermute | solution.py:296
  8.6 1.5 %collective-permute-start = (f32[81,128]{1,0:T(8,128)}, f32[81,128]{1,0:T(8,128)S(1)}, u32[]{:S(2)}, u32[]{:S(2)}) collective-permute-start(f32[81,128]{1,0:T(8,128)} %get-tuple-element.12), channel_id=1, source_target_pairs={{0,4},{4,8},{8,12},{12,16},{16,20},{20,24},{24,28},{1,5},{5,9},{9,... | collective-permute-start | bytes 124424 | tf_op jit(solution)/shard_map/ppermute | solution.py:296
  10.1 1.3 %collective-permute-start.1 = (f32[81,128]{1,0:T(8,128)}, f32[81,128]{1,0:T(8,128)S(1)}, u32[]{:S(2)}, u32[]{:S(2)}) collective-permute-start(f32[81,128]{1,0:T(8,128)} %get-tuple-element.13), channel_id=1, source_target_pairs={{4,0},{8,4},{12,8},{16,12},{20,16},{24,20},{28,24},{5,1},{9,5},{13... | collective-permute-start | bytes 124424 | tf_op jit(solution)/shard_map/ppermute | solution.py:296
  11.4 0.6 sine_multiply_fusion.latitude
  11.9 0.0 collective-permute-done.2.y_before
  11.9 0.0 copy-start.4
  11.9 1.1 %collective-permute-done.3.y_after = f32[8,128]{1,0:T(8,128)S(1)} collective-permute-done((f32[8,128]{1,0:T(8,128)}, f32[8,128]{1,0:T(8,128)S(1)}, u32[]{:S(2)}, u32[]{:S(2)}) %collective-permute-start.3) | collective-permute-done | bytes 4128 | tf_op jit(solution)/shard_map/ppermute | solution.py:296
  13.0 0.0 copy-start.5
  13.0 0.0 collective-permute-done.x_before
  13.0 0.0 copy-start.2
  13.0 2.0 %collective-permute-done.1.x_after = f32[81,128]{1,0:T(8,128)S(1)} collective-permute-done((f32[81,128]{1,0:T(8,128)}, f32[81,128]{1,0:T(8,128)S(1)}, u32[]{:S(2)}, u32[]{:S(2)}) %collective-permute-start.1) | collective-permute-done | bytes 41504 | tf_op jit(solution)/shard_map/ppermute | solution.py:296
  15.0 0.0 copy-done.4
  15.0 0.0 copy-done.5
  15.0 0.0 copy-done.2
  15.1 0.0 copy-start.3
  15.1 0.6 copy-done.3
  15.7 2.2 %shard_map.77 = (f32[2,20,8,128]{3,2,1,0:T(8,128)}, f32[2,20,8,128]{3,2,1,0:T(8,128)}, f32[4,8,128]{2,1,0:T(8,128)}) custom-call(f32[2,20,8,128]{3,2,1,0:T(8,128)} %tracers.3, f32[2,20,8,128]{3,2,1,0:T(8,128)} %velocity.3, s32[8,128]{1,0:T(8,128)} %refs_2_.1, f32[8,512]{1,0:T(8,128)} %diagonal.1, f32[20]{0:T(128)} %thickness.1, ...), custom_call_target="tpu_custom_call" | custom-call | tf_op jit(solution)/shard_map/pallas_call | solution.py:303
  17.9 0.0 copy-start
  17.9 0.0 copy-start.1
  17.9 71.8 %all-gather = f32[128,8,128]{2,1,0:T(8,128)S(1)} all-gather(f32[4,8,128]{2,1,0:T(8,128)} %get-tuple-element.17), channel_id=2, replica_groups=mesh['bx'=8,'by'=4] {'bx','by'}, dimensions={0}, use_global_device_ids=true | all-gather | bytes 540672 | tf_op jit(solution)/shard_map/all_gather | solution.py:312
  89.7 0.0 copy-done
  89.7 0.0 copy-done.1
  89.7 1.9 %shard_map.78 = (f32[2,20,8,128]{3,2,1,0:T(8,128)}, f32[8,128]{1,0:T(8,128)}) custom-call(f32[32,4,8,128]{3,2,1,0:T(8,128)S(1)} %bitcast.1, f32[2,20,8,128]{3,2,1,0:T(8,128)S(1)} %copy-done, s32[8,128]{1,0:T(8,128)S(1)} %copy-done.1), custom_call_target="tpu_custom_call" | custom-call | tf_op jit(solution)/shard_map/pallas_call | solution.py:317
Async XLA Ops:
  2.5 9.5 %collective-permute-start.2 = (f32[8,128]{1,0:T(8,128)}, f32[8,128]{1,0:T(8,128)S(1)}, u32[]{:S(2)}, u32[]{:S(2)}) collective-permute-start(f32[8,128]{1,0:T(8,128)} %get-tuple-element.14), channel_id=1, source_target_pairs={{0,1},{1,2},{2,3},{4,5},{5,6},{6,7},{8,9},{9,10},{10,11},{12,13},{... | collective-permute-start | bytes 12296 | tf_op jit(solution)/shard_map/ppermute | solution.py:296
  7.3 5.7 %collective-permute-start.3 = (f32[8,128]{1,0:T(8,128)}, f32[8,128]{1,0:T(8,128)S(1)}, u32[]{:S(2)}, u32[]{:S(2)}) collective-permute-start(f32[8,128]{1,0:T(8,128)} %get-tuple-element.15), channel_id=1, source_target_pairs={{1,0},{2,1},{3,2},{5,4},{6,5},{7,6},{9,8},{10,9},{11,10},{13,12},{... | collective-permute-start | bytes 12296 | tf_op jit(solution)/shard_map/ppermute | solution.py:296
  8.6 4.4 %collective-permute-start = (f32[81,128]{1,0:T(8,128)}, f32[81,128]{1,0:T(8,128)S(1)}, u32[]{:S(2)}, u32[]{:S(2)}) collective-permute-start(f32[81,128]{1,0:T(8,128)} %get-tuple-element.12), channel_id=1, source_target_pairs={{0,4},{4,8},{8,12},{12,16},{16,20},{20,24},{24,28},{1,5},{5,9},{9,... | collective-permute-start | bytes 124424 | tf_op jit(solution)/shard_map/ppermute | solution.py:296
  10.1 5.0 %collective-permute-start.1 = (f32[81,128]{1,0:T(8,128)}, f32[81,128]{1,0:T(8,128)S(1)}, u32[]{:S(2)}, u32[]{:S(2)}) collective-permute-start(f32[81,128]{1,0:T(8,128)} %get-tuple-element.13), channel_id=1, source_target_pairs={{4,0},{8,4},{12,8},{16,12},{20,16},{24,20},{28,24},{5,1},{9,5},{13... | collective-permute-start | bytes 124424 | tf_op jit(solution)/shard_map/ppermute | solution.py:296
  11.9 3.1 %copy-start.4 = (f32[8,128]{1,0:T(8,128)}, f32[8,128]{1,0:T(8,128)S(1)}, u32[]{:S(2)}) copy-start(f32[8,128]{1,0:T(8,128)S(1)} %collective-permute-done.2.y_before) | copy-start | bytes 12292
  13.0 2.0 %copy-start.5 = (f32[8,128]{1,0:T(8,128)}, f32[8,128]{1,0:T(8,128)S(1)}, u32[]{:S(2)}) copy-start(f32[8,128]{1,0:T(8,128)S(1)} %collective-permute-done.3.y_after) | copy-start | bytes 12292
  13.0 2.0 %copy-start.2 = (f32[81,128]{1,0:T(8,128)}, f32[81,128]{1,0:T(8,128)S(1)}, u32[]{:S(2)}) copy-start(f32[81,128]{1,0:T(8,128)S(1)} %collective-permute-done.x_before) | copy-start | bytes 124420
  15.1 0.6 copy-start.3
  17.9 71.9 %copy-start = (f32[2,20,8,128]{3,2,1,0:T(8,128)S(1)}, f32[2,20,8,128]{3,2,1,0:T(8,128)}, u32[]{:S(2)}) copy-start(f32[2,20,8,128]{3,2,1,0:T(8,128)} %get-tuple-element.18.refs_1_) | copy-start | bytes 491524
  17.9 71.9 %copy-start.1 = (s32[8,128]{1,0:T(8,128)S(1)}, s32[8,128]{1,0:T(8,128)}, u32[]{:S(2)}) copy-start(s32[8,128]{1,0:T(8,128)} %refs_2_.1) | copy-start | bytes 12292

commit v2 on v1

--- a/solution.py
+++ b/solution.py
@@ -112,10 +112,16 @@
         flow_x = flow_x + jnp.where(here, weight * next_zonal, 0.0)
         flow_y = flow_y + jnp.where(here, weight * next_merid, 0.0)
     row_start = pl.multiple_of(lax.axis_index("by") * rows_y, rows_y)
-    surface[0] = flow_x
-    surface[1] = flow_y
-    surface[2] = jnp.where(counts > 0, 1.0, 0.0)
-    surface[3] = diagonal[:, pl.ds(row_start, rows_y)]
+    ocean = jnp.where(counts > 0, 1.0, 0.0)
+    own_diagonal = diagonal[:, pl.ds(row_start, rows_y)]
+
+    def place(target):
+        surface[target, 0] = flow_x
+        surface[target, 1] = flow_y
+        surface[target, 2] = ocean
+        surface[target, 3] = own_diagonal
+
+    pl.loop(0, surface.shape[0], unroll=8)(place)
 
 
 def solve_kernel(
@@ -302,14 +308,14 @@
 
     new_tracers, moved_velocity, surface = pl.pallas_call(
         level_kernel,
-        out_shape=[like(*tracers.shape), like(*velocity.shape), like(4, *shape)],
+        out_shape=[like(*tracers.shape), like(*velocity.shape), like(blocks, 4, *shape)],
         in_specs=[VMEM] * 4 + [SMEM] + [VMEM] * 5,
         out_specs=[VMEM] * 3,
     )(
         tracers, velocity, wet_levels, diagonal, thickness, latitude,
         x_before, x_after, y_before, y_after,
     )
-    gathered = lax.all_gather(surface, ("bx", "by"), axis=0, tiled=False)
+    gathered = lax.all_to_all(surface, ("bx", "by"), split_axis=0, concat_axis=0, tiled=True)
 
     def solve(*refs):
         solve_kernel(blocks_x, blocks_y, *refs)

time: 91.9 us -> 45 us (0.49)
  blocking collectives: 71.8 us -> 24.6 us
    all_gather x1 -> x0, blocking collectives: 71.8 us -> none  [body(): gathered = lax.all_gather(surface, ('bx', 'by'), axis=0, tiled=False)]
    all_to_all x0 -> x1, blocking collectives: none -> 24.6 us  [body(): lax.all_to_all(surface, ('bx', 'by'), split_axis=0, concat_axis=0, tiled=...]
where the time goes in v2:
time: 45 us; the launch traced here: 44.6 us
  blocking collectives  24.6 us (55%)
  starting transfers between devices  8.88 us (20%)
  Pallas kernels  6.18 us (14%)
  waiting for transfers between devices  3.07 us (7%)
  between operations  0.69 us (2%)
  local copies, waits for them, and re-layouts  0.63 us (1%)
  other arithmetic  0.59 us (1%)
    all_to_all x1, blocking collectives, body(): lax.all_to_all(surface, ('bx', 'by'), split_axis=0, concat_axis=0, tiled=...  24.6 us
    ppermute x4, starting transfers between devices, neighbours_of(): return (lax.ppermute(last, axis, up), lax.ppermute(first, axis, down))  8.88 us
    ppermute x4, waiting for transfers between devices, neighbours_of(): return (lax.ppermute(last, axis, up), lax.ppermute(first, axis, down))  3.07 us
    pallas_call x1, Pallas kernels, body(): pl.pallas_call(level_kernel, out_shape=[like(*tracers.shape), like(*veloc...  2.47 us
    pallas_call x1, Pallas kernels, body(): pl.pallas_call(solve, out_shape=[like(*velocity.shape), like(*shape)], in...  1.87 us
    pallas_call x1, Pallas kernels, body(): pl.pallas_call(pack_rims, out_shape=[like(rim_rows, rows_y)] * 2 + [like(...  1.84 us
  transfers between devices with their start and end apart: 4, of which 2 were waited for; matrix products, arithmetic and copies ran while one was open for 1% of the time, Pallas kernels for 0%

profile of v2, /device:TPU:0, one launch (start us, length us, event | category | flops | bytes accessed | tf_op | source)
XLA Modules:
  0.0 44.6 jit_solution(8226268029467174619)
XLA Ops:
  0.6 1.8 %shard_map.76 = (f32[81,128]{1,0:T(8,128)}, f32[81,128]{1,0:T(8,128)}, f32[8,128]{1,0:T(8,128)}, f32[8,128]{1,0:T(8,128)}) custom-call(f32[2,20,8,128]{3,2,1,0:T(8,128)} %tracers.3, f32[2,20,8,128]{3,2,1,0:T(8,128)} %velocity.3, s32[8,128]{1,0:T(8,128)} %refs_2_.1), custom_call_target="tpu_custom_call" | custom-call | tf_op jit(solution)/shard_map/pallas_call | solution.py:292
  2.5 4.8 %collective-permute-start.2 = (f32[8,128]{1,0:T(8,128)}, f32[8,128]{1,0:T(8,128)S(1)}, u32[]{:S(2)}, u32[]{:S(2)}) collective-permute-start(f32[8,128]{1,0:T(8,128)} %get-tuple-element.14), channel_id=1, source_target_pairs={{0,1},{1,2},{2,3},{4,5},{5,6},{6,7},{8,9},{9,10},{10,11},{12,13},{... | collective-permute-start | bytes 12296 | tf_op jit(solution)/shard_map/ppermute | solution.py:302
  7.3 1.3 %collective-permute-start.3 = (f32[8,128]{1,0:T(8,128)}, f32[8,128]{1,0:T(8,128)S(1)}, u32[]{:S(2)}, u32[]{:S(2)}) collective-permute-start(f32[8,128]{1,0:T(8,128)} %get-tuple-element.15), channel_id=1, source_target_pairs={{1,0},{2,1},{3,2},{5,4},{6,5},{7,6},{9,8},{10,9},{11,10},{13,12},{... | collective-permute-start | bytes 12296 | tf_op jit(solution)/shard_map/ppermute | solution.py:302
  8.6 1.5 %collective-permute-start = (f32[81,128]{1,0:T(8,128)}, f32[81,128]{1,0:T(8,128)S(1)}, u32[]{:S(2)}, u32[]{:S(2)}) collective-permute-start(f32[81,128]{1,0:T(8,128)} %get-tuple-element.12), channel_id=1, source_target_pairs={{0,4},{4,8},{8,12},{12,16},{16,20},{20,24},{24,28},{1,5},{5,9},{9,... | collective-permute-start | bytes 124424 | tf_op jit(solution)/shard_map/ppermute | solution.py:302
  10.1 1.3 %collective-permute-start.1 = (f32[81,128]{1,0:T(8,128)}, f32[81,128]{1,0:T(8,128)S(1)}, u32[]{:S(2)}, u32[]{:S(2)}) collective-permute-start(f32[81,128]{1,0:T(8,128)} %get-tuple-element.13), channel_id=1, source_target_pairs={{4,0},{8,4},{12,8},{16,12},{20,16},{24,20},{28,24},{5,1},{9,5},{13... | collective-permute-start | bytes 124424 | tf_op jit(solution)/shard_map/ppermute | solution.py:302
  11.4 0.6 %sine_multiply_fusion.latitude = f32[1,128]{1,0:T(1,128)} fusion(s32[]{:T(128)S(6)} %mul.29), kind=kLoop, calls=%fused_computation | loop fusion | flops 896 | bytes 516 | tf_op jit(solution)/shard_map/mul | solution.py:278
  12.0 0.0 collective-permute-done.2.y_before
  12.0 0.0 copy-start.4
  12.0 1.0 %collective-permute-done.3.y_after = f32[8,128]{1,0:T(8,128)S(1)} collective-permute-done((f32[8,128]{1,0:T(8,128)}, f32[8,128]{1,0:T(8,128)S(1)}, u32[]{:S(2)}, u32[]{:S(2)}) %collective-permute-start.3) | collective-permute-done | bytes 4128 | tf_op jit(solution)/shard_map/ppermute | solution.py:302
  13.0 0.0 copy-start.5
  13.0 0.0 collective-permute-done.x_before
  13.0 0.0 copy-start.2
  13.0 2.0 %collective-permute-done.1.x_after = f32[81,128]{1,0:T(8,128)S(1)} collective-permute-done((f32[81,128]{1,0:T(8,128)}, f32[81,128]{1,0:T(8,128)S(1)}, u32[]{:S(2)}, u32[]{:S(2)}) %collective-permute-start.1) | collective-permute-done | bytes 41504 | tf_op jit(solution)/shard_map/ppermute | solution.py:302
  15.0 0.0 copy-done.4
  15.0 0.0 copy-done.5
  15.0 0.0 copy-done.2
  15.1 0.0 copy-start.3
  15.1 0.6 %copy-done.3 = f32[81,128]{1,0:T(8,128)} copy-done((f32[81,128]{1,0:T(8,128)}, f32[81,128]{1,0:T(8,128)S(1)}, u32[]{:S(2)}) %copy-start.3) | copy-done | bytes 41496
  15.7 2.5 %shard_map.77 = (f32[2,20,8,128]{3,2,1,0:T(8,128)}, f32[2,20,8,128]{3,2,1,0:T(8,128)}, f32[32,4,8,128]{3,2,1,0:T(8,128)}) custom-call(f32[2,20,8,128]{3,2,1,0:T(8,128)} %tracers.3, f32[2,20,8,128]{3,2,1,0:T(8,128)} %velocity.3, s32[8,128]{1,0:T(8,128)} %refs_2_.1, f32[8,512]{1,0:T(8,128)} %diagonal.1, f32[20]{0:T(128)} %thickness.1, ...), custom_call_target="tpu_custom_call" | custom-call | tf_op jit(solution)/shard_map/pallas_call | solution.py:309
  18.1 0.0 copy-start
  18.1 0.0 copy-start.1
  18.1 24.6 %all_to_all.5.refs_0_ = f32[32,4,8,128]{3,2,1,0:T(8,128)S(1)} all-to-all(f32[32,4,8,128]{3,2,1,0:T(8,128)} %get-tuple-element.17), channel_id=1, replica_groups=mesh['bx'=8,'by'=4] {'bx','by'}, dimensions={0} | all-to-all | bytes 1048576 | tf_op jit(solution)/shard_map/all_to_all | solution.py:318
  42.7 0.0 copy-done
  42.7 0.0 copy-done.1
  42.8 1.9 %shard_map.78 = (f32[2,20,8,128]{3,2,1,0:T(8,128)}, f32[8,128]{1,0:T(8,128)}) custom-call(f32[32,4,8,128]{3,2,1,0:T(8,128)S(1)} %all_to_all.5.refs_0_, f32[2,20,8,128]{3,2,1,0:T(8,128)S(1)} %copy-done, s32[8,128]{1,0:T(8,128)S(1)} %copy-done.1), custom_call_target="tpu_custom_call" | custom-call | tf_op jit(solution)/shard_map/pallas_call | solution.py:323
Async XLA Ops:
  2.5 9.5 %collective-permute-start.2 = (f32[8,128]{1,0:T(8,128)}, f32[8,128]{1,0:T(8,128)S(1)}, u32[]{:S(2)}, u32[]{:S(2)}) collective-permute-start(f32[8,128]{1,0:T(8,128)} %get-tuple-element.14), channel_id=1, source_target_pairs={{0,1},{1,2},{2,3},{4,5},{5,6},{6,7},{8,9},{9,10},{10,11},{12,13},{... | collective-permute-start | bytes 12296 | tf_op jit(solution)/shard_map/ppermute | solution.py:302
  7.3 5.7 %collective-permute-start.3 = (f32[8,128]{1,0:T(8,128)}, f32[8,128]{1,0:T(8,128)S(1)}, u32[]{:S(2)}, u32[]{:S(2)}) collective-permute-start(f32[8,128]{1,0:T(8,128)} %get-tuple-element.15), channel_id=1, source_target_pairs={{1,0},{2,1},{3,2},{5,4},{6,5},{7,6},{9,8},{10,9},{11,10},{13,12},{... | collective-permute-start | bytes 12296 | tf_op jit(solution)/shard_map/ppermute | solution.py:302
  8.6 4.4 %collective-permute-start = (f32[81,128]{1,0:T(8,128)}, f32[81,128]{1,0:T(8,128)S(1)}, u32[]{:S(2)}, u32[]{:S(2)}) collective-permute-start(f32[81,128]{1,0:T(8,128)} %get-tuple-element.12), channel_id=1, source_target_pairs={{0,4},{4,8},{8,12},{12,16},{16,20},{20,24},{24,28},{1,5},{5,9},{9,... | collective-permute-start | bytes 124424 | tf_op jit(solution)/shard_map/ppermute | solution.py:302
  10.1 5.0 %collective-permute-start.1 = (f32[81,128]{1,0:T(8,128)}, f32[81,128]{1,0:T(8,128)S(1)}, u32[]{:S(2)}, u32[]{:S(2)}) collective-permute-start(f32[81,128]{1,0:T(8,128)} %get-tuple-element.13), channel_id=1, source_target_pairs={{4,0},{8,4},{12,8},{16,12},{20,16},{24,20},{28,24},{5,1},{9,5},{13... | collective-permute-start | bytes 124424 | tf_op jit(solution)/shard_map/ppermute | solution.py:302
  12.0 3.1 %copy-start.4 = (f32[8,128]{1,0:T(8,128)}, f32[8,128]{1,0:T(8,128)S(1)}, u32[]{:S(2)}) copy-start(f32[8,128]{1,0:T(8,128)S(1)} %collective-permute-done.2.y_before) | copy-start | bytes 12292
  13.0 2.0 %copy-start.5 = (f32[8,128]{1,0:T(8,128)}, f32[8,128]{1,0:T(8,128)S(1)}, u32[]{:S(2)}) copy-start(f32[8,128]{1,0:T(8,128)S(1)} %collective-permute-done.3.y_after) | copy-start | bytes 12292
  13.0 2.0 %copy-start.2 = (f32[81,128]{1,0:T(8,128)}, f32[81,128]{1,0:T(8,128)S(1)}, u32[]{:S(2)}) copy-start(f32[81,128]{1,0:T(8,128)S(1)} %collective-permute-done.x_before) | copy-start | bytes 124420
  15.1 0.6 %copy-start.3 = (f32[81,128]{1,0:T(8,128)}, f32[81,128]{1,0:T(8,128)S(1)}, u32[]{:S(2)}) copy-start(f32[81,128]{1,0:T(8,128)S(1)} %collective-permute-done.1.x_after) | copy-start | bytes 124420
  18.1 24.6 %copy-start = (f32[2,20,8,128]{3,2,1,0:T(8,128)S(1)}, f32[2,20,8,128]{3,2,1,0:T(8,128)}, u32[]{:S(2)}) copy-start(f32[2,20,8,128]{3,2,1,0:T(8,128)} %get-tuple-element.18.refs_1_) | copy-start | bytes 491524
  18.1 24.6 %copy-start.1 = (s32[8,128]{1,0:T(8,128)S(1)}, s32[8,128]{1,0:T(8,128)}, u32[]{:S(2)}) copy-start(s32[8,128]{1,0:T(8,128)} %refs_2_.1) | copy-start | bytes 12292

commit v3 on v2

--- a/solution.py
+++ b/solution.py
@@ -28,8 +28,9 @@
     return lax.broadcasted_iota(jnp.int32, shape, 0)
 
 
-def pack_rims(tracers, velocity, wet, first_rows, last_rows, first_cols, last_cols):
+def pack_rims(tracers, velocity, wet, rows_a, rows_b, cols_a, cols_b):
     levels, cols_x, rows_y = tracers.shape[1:]
+    even_x, even_y = (lax.axis_index("bx") % 2 == 0, lax.axis_index("by") % 2 == 0)
     lane = lanes_of((cols_x, rows_y))
     counts = wet[...].astype(jnp.float32)
     first, last = jnp.zeros_like(counts), jnp.zeros_like(counts)
@@ -39,16 +40,17 @@
             tile = (tracers if field < 2 else velocity)[field % 2, level]
         else:
             tile = counts
-        first_rows[index : index + 1, :] = tile[0:1, :]
-        last_rows[index : index + 1, :] = tile[cols_x - 1 : cols_x, :]
+        top, bottom = (tile[0:1, :], tile[cols_x - 1 : cols_x, :])
+        rows_a[index : index + 1, :] = jnp.where(even_x, bottom, top)
+        rows_b[index : index + 1, :] = jnp.where(even_x, top, bottom)
         first = jnp.where(lane == index, tile[:, 0:1], first)
         last = jnp.where(lane == index, tile[:, rows_y - 1 : rows_y], last)
-    first_cols[...] = first
-    last_cols[...] = last
+    cols_a[...] = jnp.where(even_y, last, first)
+    cols_b[...] = jnp.where(even_y, first, last)
 
 
 def level_kernel(
-    tracers, velocity, wet, diagonal, thickness, latitude, x_before, x_after, y_before, y_after,
+    tracers, velocity, wet, diagonal, thickness, latitude, rows_a, rows_b, cols_a, cols_b,
     new_tracers, moved_velocity, surface,
 ):
     levels, cols_x, rows_y = tracers.shape[1:]
@@ -56,12 +58,16 @@
     lane, sublane = (lanes_of(shape), sublanes_of(shape))
     low_x, high_x = (sublane == 0, sublane == cols_x - 1)
     low_y, high_y = (lane == 0, lane == rows_y - 1)
-    before_cols, after_cols = (y_before[...], y_after[...])
+    even_x, even_y = (lax.axis_index("bx") % 2 == 0, lax.axis_index("by") % 2 == 0)
+    after_cols = jnp.where(even_y, cols_a[...], cols_b[...])
+    before_cols = jnp.where(even_y, cols_b[...], cols_a[...])
 
     def neighbours(tile, index):
+        row_a, row_b = (rows_a[index : index + 1, :], rows_b[index : index + 1, :])
+        after_row, before_row = (jnp.where(even_x, row_a, row_b), jnp.where(even_x, row_b, row_a))
         return (
-            jnp.where(high_x, x_after[index : index + 1, :], pltpu.roll(tile, cols_x - 1, 0)),
-            jnp.where(low_x, x_before[index : index + 1, :], pltpu.roll(tile, 1, 0)),
+            jnp.where(high_x, after_row, pltpu.roll(tile, cols_x - 1, 0)),
+            jnp.where(low_x, before_row, pltpu.roll(tile, 1, 0)),
             jnp.where(high_y, after_cols[:, index : index + 1], pltpu.roll(tile, rows_y - 1, 1)),
             jnp.where(low_y, before_cols[:, index : index + 1], pltpu.roll(tile, 1, 1)),
         )
@@ -112,14 +118,25 @@
         flow_x = flow_x + jnp.where(here, weight * next_zonal, 0.0)
         flow_y = flow_y + jnp.where(here, weight * next_merid, 0.0)
     row_start = pl.multiple_of(lax.axis_index("by") * rows_y, rows_y)
-    ocean = jnp.where(counts > 0, 1.0, 0.0)
-    own_diagonal = diagonal[:, pl.ds(row_start, rows_y)]
+    inverse = jnp.where(counts > 0, 1.0, 0.0) / (4.0 + diagonal[:, pl.ds(row_start, rows_y)])
+    ahead = jnp.where(high_x, 0.0, pltpu.roll(flow_x, cols_x - 1, 0))
+    behind = jnp.where(low_x, 0.0, pltpu.roll(flow_x, 1, 0))
+    slope = ahead - behind
+    ahead = jnp.where(high_y, 0.0, pltpu.roll(flow_y, rows_y - 1, 1))
+    behind = jnp.where(low_y, 0.0, pltpu.roll(flow_y, 1, 1))
+    inner = (slope + (ahead - behind)) * 0.5
+    edge_x = flow_x * 0.5
+    edge_y = flow_y * 0.5
+    first = jnp.where(lane == sublane, edge_y[:, 0:1], 0.0)
+    last = jnp.where(lane == sublane + cols_x, edge_y[:, rows_y - 1 : rows_y], 0.0)
+    corner = jnp.sum(first + last, axis=0, keepdims=True)
 
     def place(target):
-        surface[target, 0] = flow_x
-        surface[target, 1] = flow_y
-        surface[target, 2] = ocean
-        surface[target, 3] = own_diagonal
+        surface[target, 0:cols_x, 0, :] = inner
+        surface[target, cols_x : 2 * cols_x, 0, :] = inverse
+        surface[target, 2 * cols_x : 2 * cols_x + 1, 0, :] = edge_x[0:1, :]
+        surface[target, 2 * cols_x + 1 : 2 * cols_x + 2, 0, :] = edge_x[cols_x - 1 : cols_x, :]
+        surface[target, 2 * cols_x + 2 : 2 * cols_x + 3, 0, :] = corner
 
     pl.loop(0, surface.shape[0], unroll=8)(place)
 
@@ -127,10 +144,9 @@
 def solve_kernel(
     blocks_x, blocks_y, gathered, moved_velocity, wet,
     new_velocity, pressure,
-    inverse, residual, smooth_0, smooth_1, smooth_2, image_0, image_1, direction_1,
+    residual, lifted_0, lifted_1, smooth_0, smooth_1, smooth_2, image_0, direction_1,
 ):
-    cols_x, rows_y = gathered.shape[2:]
-    levels = moved_velocity.shape[1]
+    levels, cols_x, rows_y = moved_velocity.shape[1:]
     shape = (cols_x, rows_y)
     lane, sublane = (lanes_of(shape), sublanes_of(shape))
     low_x, high_x = (sublane == 0, sublane == cols_x - 1)
@@ -146,88 +162,103 @@
 
     def guarded(load, row, column):
         if isinstance(row, int):
-            return load(row * blocks_y + column) if 0 <= row < blocks_x else zero
+            return load(row * blocks_y + column) if 0 <= row < blocks_x else 0.0
         inside = jnp.logical_and(row >= 0, row < blocks_x)
         return load(jnp.clip(row, 0, blocks_x - 1) * blocks_y + column) * inside.astype(jnp.float32)
 
-    def after_x(load, tile, row, column):
-        other = guarded(load, row + 1, column)
-        return jnp.where(high_x, pltpu.roll(other, cols_x - 1, 0), pltpu.roll(tile, cols_x - 1, 0))
-
-    def before_x(load, tile, row, column):
-        other = guarded(load, row - 1, column)
-        return jnp.where(low_x, pltpu.roll(other, 1, 0), pltpu.roll(tile, 1, 0))
+    def along_x(load, row, column):
+        tile = load(row * blocks_y + column)
+        other = guarded(lambda i: load(i, slice(0, 1)), row + 1, column)
+        after = jnp.where(high_x, other, pltpu.roll(tile, cols_x - 1, 0))
+        other = guarded(lambda i: load(i, slice(cols_x - 1, cols_x)), row - 1, column)
+        before = jnp.where(low_x, other, pltpu.roll(tile, 1, 0))
+        return after + before
 
     def along_y(tiles):
-        ahead = [pltpu.roll(tile, rows_y - 1, 1) for tile in tiles] + [zero]
-        behind = [zero] + [pltpu.roll(tile, 1, 1) for tile in tiles]
-        after = [jnp.where(high_y, ahead[c + 1], ahead[c]) for c in range(blocks_y)]
-        before = [jnp.where(low_y, behind[c], behind[c + 1]) for c in range(blocks_y)]
-        return after, before
-
-    def smoothed_by(inv, tile):
-        first = inv * tile
+        ahead = [pltpu.roll(tile, rows_y - 1, 1) for tile in tiles] + [0.0]
+        behind = [0.0] + [pltpu.roll(tile, 1, 1) for tile in tiles]
+        return [
+            jnp.where(high_y, ahead[c + 1], ahead[c]) + jnp.where(low_y, behind[c], behind[c + 1])
+            for c in range(blocks_y)
+        ]
+
+    def inverse_of(index):
+        return gathered[index, cols_x : 2 * cols_x, 0, :]
+
+    def lift(inverse, tile):
+        first = inverse * tile
         near = jnp.where(high_x, 0.0, pltpu.roll(first, cols_x - 1, 0))
         near = near + jnp.where(low_x, 0.0, pltpu.roll(first, 1, 0))
         near = near + jnp.where(high_y, 0.0, pltpu.roll(first, rows_y - 1, 1))
         near = near + jnp.where(low_y, 0.0, pltpu.roll(first, 1, 1))
-        return inv * (tile + near)
+        return tile + near
 
     def total(values):
         return jnp.sum(values, axis=(0, 1), keepdims=True)
 
+    def edge_rows(which):
+        place = 2 * cols_x + which
+        return lambda index: gathered[index, place : place + 1, 0, :]
+
+    def edge_column(index, which):
+        corner = jnp.where(lane == sublane + which * cols_x, edge_rows(2)(index), 0.0)
+        return jnp.sum(corner, axis=1, keepdims=True)
+
     def start(row, carry):
-        flow_y = [gathered[row * blocks_y + c, 1] for c in range(blocks_y)]
-        after, before = along_y(flow_y)
         for column in range(blocks_y):
             index = row * blocks_y + column
-            flow = gathered[index, 0]
-            load = lambda i: gathered[i, 0]
-            slope = after_x(load, flow, row, column) - before_x(load, flow, row, column)
-            ocean = gathered[index, 2]
-            forcing = ocean * ((slope + (after[column] - before[column])) * 0.5)
-            inv = ocean / (4.0 + gathered[index, 3])
-            inverse[index] = inv
+            forcing = gathered[index, 0:cols_x, 0, :]
+            forcing = forcing + jnp.where(high_x, guarded(edge_rows(0), row + 1, column), 0.0)
+            forcing = forcing - jnp.where(low_x, guarded(edge_rows(1), row - 1, column), 0.0)
+            if column + 1 < blocks_y:
+                forcing = forcing + jnp.where(high_y, edge_column(index + 1, 0), 0.0)
+            if column > 0:
+                forcing = forcing - jnp.where(low_y, edge_column(index - 1, 1), 0.0)
+            inverse = inverse_of(index)
+            lifted = lift(inverse, forcing)
             residual[index] = forcing
-            smooth_0[index] = smoothed_by(inv, forcing)
+            lifted_0[index] = lifted
+            smooth_0[index] = inverse * lifted
         return carry
 
-    def operate(smooth, image):
+    def operate(lifted, smooth, image):
+        def load(index, rows=slice(None)):
+            return smooth[index, rows]
+
         def step(row, carry):
             inner, curvature = carry
             tiles = [smooth[row * blocks_y + c] for c in range(blocks_y)]
-            after, before = along_y(tiles)
+            beside = along_y(tiles)
             for column in range(blocks_y):
                 index = row * blocks_y + column
-                tile = tiles[column]
-                load = lambda i: smooth[i]
-                near = after_x(load, tile, row, column) + before_x(load, tile, row, column)
-                near = near + after[column] + before[column]
-                centre = 4.0 + gathered[index, 3]
-                result = gathered[index, 2] * (centre * tile - near)
+                result = lifted[index] - (along_x(load, row, column) + beside[column])
                 if image is not None:
                     image[index] = result
-                inner = inner + residual[index] * tile
-                curvature = curvature + tile * result
+                inner = inner + residual[index] * tiles[column]
+                curvature = curvature + tiles[column] * result
             return inner, curvature
 
         inner, curvature = each_row(step, (zero, zero))
         return total(inner), total(curvature)
 
     each_row(start, 0)
-    inner_0, curvature_0 = operate(smooth_0, image_0)
+    inner_0, curvature_0 = operate(lifted_0, smooth_0, image_0)
     step_0 = inner_0 / curvature_0
 
     def advance_0(row, carry):
         for column in range(blocks_y):
             index = row * blocks_y + column
             left = residual[index] - step_0 * image_0[index]
+            inverse = inverse_of(index)
+            lifted = lift(inverse, left)
             residual[index] = left
-            smooth_1[index] = smoothed_by(inverse[index], left)
+            lifted_1[index] = lifted
+            smooth_1[index] = inverse * lifted
         return carry
 
     each_row(advance_0, 0)
-    inner_1, curvature_1 = operate(smooth_1, image_1)
+    image_1 = lifted_1
+    inner_1, curvature_1 = operate(lifted_1, smooth_1, image_1)
     turn_1 = inner_1 / inner_0
     step_1 = inner_1 / (curvature_1 - turn_1 * inner_1 / step_0)
 
@@ -235,14 +266,16 @@
         for column in range(blocks_y):
             index = row * blocks_y + column
             direction_1[index] = smooth_1[index] + turn_1 * smooth_0[index]
-            image = image_1[index] + turn_1 * image_0[index]
-            left = residual[index] - step_1 * image
+            left = residual[index] - step_1 * (image_1[index] + turn_1 * image_0[index])
+            inverse = inverse_of(index)
+            lifted = lift(inverse, left)
             residual[index] = left
-            smooth_2[index] = smoothed_by(inverse[index], left)
+            lifted_0[index] = lifted
+            smooth_2[index] = inverse * lifted
         return carry
 
     each_row(advance_1, 0)
-    inner_2, curvature_2 = operate(smooth_2, None)
+    inner_2, curvature_2 = operate(lifted_0, smooth_2, None)
     turn_2 = inner_2 / inner_1
     step_2 = inner_2 / (curvature_2 - turn_2 * inner_2 / step_1)
 
@@ -289,31 +322,33 @@
     def like(*dims):
         return jax.ShapeDtypeStruct(dims, jnp.float32)
 
-    first_rows, last_rows, first_cols, last_cols = pl.pallas_call(
+    def held(*dims):
+        return pltpu.VMEM(dims, jnp.float32)
+
+    rows_a, rows_b, cols_a, cols_b = pl.pallas_call(
         pack_rims,
-        out_shape=[like(rim_rows, rows_y)] * 2 + [like(*shape)] * 2,
+        out_shape=[held(rim_rows, rows_y)] * 2 + [held(*shape)] * 2,
         in_specs=[VMEM] * 3,
         out_specs=[VMEM] * 4,
     )(tracers, velocity, wet_levels)
 
-    def neighbours_of(axis, first, last):
-        up = [(i, i + 1) for i in range(lax.axis_size(axis) - 1)]
-        down = [(j, i) for i, j in up]
-        return lax.ppermute(last, axis, up), lax.ppermute(first, axis, down)
-
-    y_before, y_after = neighbours_of("by", first_cols, last_cols)
-    x_before, x_after = neighbours_of("bx", first_rows, last_rows)
+    def exchange(message, axis, first):
+        pairs = [(i, i + 1) for i in range(first, lax.axis_size(axis) - 1, 2)]
+        return lax.ppermute(message, axis, pairs + [(j, i) for i, j in pairs])
+
+    cols_a, cols_b = (exchange(cols_a, "by", 0), exchange(cols_b, "by", 1))
+    rows_a, rows_b = (exchange(rows_a, "bx", 0), exchange(rows_b, "bx", 1))
     positions = (lax.axis_index("by") * rows_y + jnp.arange(rows_y, dtype=jnp.int32)).astype(jnp.float32)
     latitude = latitude_rate(positions, blocks_y * rows_y)[None]
 
     new_tracers, moved_velocity, surface = pl.pallas_call(
         level_kernel,
-        out_shape=[like(*tracers.shape), like(*velocity.shape), like(blocks, 4, *shape)],
+        out_shape=[like(*tracers.shape), held(*velocity.shape), held(blocks, 2 * cols_x + 3, 1, rows_y)],
         in_specs=[VMEM] * 4 + [SMEM] + [VMEM] * 5,
         out_specs=[VMEM] * 3,
     )(
         tracers, velocity, wet_levels, diagonal, thickness, latitude,
-        x_before, x_after, y_before, y_after,
+        rows_a, rows_b, cols_a, cols_b,
     )
     gathered = lax.all_to_all(surface, ("bx", "by"), split_axis=0, concat_axis=0, tiled=True)
 

time: 45 us -> 36.7 us (0.82)
  starting transfers between devices: 8.88 us -> 4.39 us
  waiting for transfers between devices: 3.07 us -> 0.01 us
  blocking collectives: 24.6 us -> 22.8 us
  local copies, waits for them, and re-layouts: 0.63 us -> 1.22 us
  Pallas kernels: 6.18 us -> 6.69 us
    ppermute x4, starting transfers between devices: 8.88 us -> 4.39 us  [exchange(): return lax.ppermute(message, axis, pairs + [(j, i) for i, j in pairs])]
    ppermute x4, waiting for transfers between devices: 3.07 us -> 0.01 us  [exchange(): return lax.ppermute(message, axis, pairs + [(j, i) for i, j in pairs])]
    all_to_all x1, blocking collectives: 24.6 us -> 22.8 us  [body(): lax.all_to_all(surface, ('bx', 'by'), split_axis=0, concat_axis=0, tiled=...]
    pallas_call x1, Pallas kernels: 1.87 us -> 3.01 us  [body(): pl.pallas_call(solve, out_shape=[like(*velocity.shape), like(*shape)], in...]
    pallas_call x2, Pallas kernels: 4.31 us -> 3.68 us  [the longest x1 2.45 us: body(): pl.pallas_call(level_kernel, out_shape=[like(*tracers.shape), held(*veloc...]
    unnamed x12 -> x10, local copies, waits for them, and re-layouts: 0.63 us -> 1.22 us
  transfers between devices with their start and end apart: 4 -> 4, of which waited for: 2 -> 0; matrix products, arithmetic and copies ran while one was open for 1% -> 2% of each run, Pallas kernels for 0% -> 0%
where the time goes in v3:
time: 36.7 us; the launch traced here: 36.4 us
  blocking collectives  22.8 us (62%)
  Pallas kernels  6.69 us (18%)
  starting transfers between devices  4.39 us (12%)
  local copies, waits for them, and re-layouts  1.22 us (3%)
  between operations  0.7 us (2%)
  other arithmetic  0.62 us (2%)
    all_to_all x1, blocking collectives, body(): lax.all_to_all(surface, ('bx', 'by'), split_axis=0, concat_axis=0, tiled=...  22.8 us
    ppermute x4, starting transfers between devices, exchange(): return lax.ppermute(message, axis, pairs + [(j, i) for i, j in pairs])  4.39 us
    pallas_call x1, Pallas kernels, body(): pl.pallas_call(solve, out_shape=[like(*velocity.shape), like(*shape)], in...  3.01 us
    pallas_call x1, Pallas kernels, body(): pl.pallas_call(level_kernel, out_shape=[like(*tracers.shape), held(*veloc...  2.45 us
    pallas_call x1, Pallas kernels, body(): pl.pallas_call(pack_rims, out_shape=[held(rim_rows, rows_y)] * 2 + [held(...  1.24 us
    unnamed x10, local copies, waits for them, and re-layouts  1.22 us
  transfers between devices with their start and end apart: 4, of which 0 were waited for; matrix products, arithmetic and copies ran while one was open for 2% of the time, Pallas kernels for 0%

profile of v3, /device:TPU:0, one launch (start us, length us, event | category | flops | bytes accessed | tf_op | source)
XLA Modules:
  0.0 36.4 jit_solution(15663427217747511652)
XLA Ops:
  0.6 1.2 %shard_map.76 = (f32[81,128]{1,0:T(8,128)S(1)}, f32[81,128]{1,0:T(8,128)S(1)}, f32[8,128]{1,0:T(8,128)S(1)}, f32[8,128]{1,0:T(8,128)S(1)}) custom-call(f32[2,20,8,128]{3,2,1,0:T(8,128)} %tracers.3, f32[2,20,8,128]{3,2,1,0:T(8,128)} %velocity.3, s32[8,128]{1,0:T(8,128)} %refs_2_.1), custom_call_target="tpu_custom_call" | custom-call | tf_op jit(solution)/shard_map/pallas_call | solution.py:328
  1.9 3.0 %collective-permute-start.2 = (f32[8,128]{1,0:T(8,128)S(1)}, f32[8,128]{1,0:T(8,128)S(1)}, u32[]{:S(2)}, u32[]{:S(2)}) collective-permute-start(f32[8,128]{1,0:T(8,128)S(1)} %get-tuple-element.14), channel_id=1, source_target_pairs={{0,1},{2,3},{1,0},{3,2},{4,5},{6,7},{5,4},{7,6},{8,9},{10,11},{9,8... | collective-permute-start | bytes 12296 | tf_op jit(solution)/shard_map/ppermute | solution.py:337
  4.9 0.6 %collective-permute-start.3 = (f32[8,128]{1,0:T(8,128)S(1)}, f32[8,128]{1,0:T(8,128)S(1)}, u32[]{:S(2)}, u32[]{:S(2)}) collective-permute-start(f32[8,128]{1,0:T(8,128)S(1)} %get-tuple-element.15), channel_id=1, source_target_pairs={{1,2},{2,1},{5,6},{6,5},{9,10},{10,9},{13,14},{14,13},{17,18},{18,... | collective-permute-start | bytes 12296 | tf_op jit(solution)/shard_map/ppermute | solution.py:337
  5.5 0.1 collective-permute-start
  5.6 0.7 %collective-permute-start.1 = (f32[81,128]{1,0:T(8,128)S(1)}, f32[81,128]{1,0:T(8,128)S(1)}, u32[]{:S(2)}, u32[]{:S(2)}) collective-permute-start(f32[81,128]{1,0:T(8,128)S(1)} %get-tuple-element.13), channel_id=1, source_target_pairs={{4,8},{12,16},{20,24},{8,4},{16,12},{24,20},{5,9},{13,17},{21,25},... | collective-permute-start | bytes 124424 | tf_op jit(solution)/shard_map/ppermute | solution.py:337
  6.3 0.6 %sine_multiply_fusion.latitude = f32[1,128]{1,0:T(1,128)} fusion(s32[]{:T(128)S(6)} %mul.29), kind=kLoop, calls=%fused_computation | loop fusion | flops 896 | bytes 516 | tf_op jit(solution)/shard_map/mul | solution.py:311
  6.9 0.0 collective-permute-done.2.cols_a
  6.9 0.0 copy-start.3
  6.9 0.0 collective-permute-done.3.cols_b
  6.9 0.0 copy-start.4
  6.9 0.0 collective-permute-done.rows_a
  6.9 0.0 copy-start.1
  7.0 0.0 collective-permute-done.1.rows_b
  7.0 0.5 %copy-done.3 = f32[8,128]{1,0:T(8,128)} copy-done((f32[8,128]{1,0:T(8,128)}, f32[8,128]{1,0:T(8,128)S(1)}, u32[]{:S(2)}) %copy-start.3) | copy-done | bytes 4120
  7.5 0.0 copy-done.4
  7.5 0.0 copy-done.1
  7.6 0.0 copy-start.2
  7.6 0.6 %copy-done.2 = f32[81,128]{1,0:T(8,128)} copy-done((f32[81,128]{1,0:T(8,128)}, f32[81,128]{1,0:T(8,128)S(1)}, u32[]{:S(2)}) %copy-start.2) | copy-done | bytes 41496
  8.2 2.4 %shard_map.77 = (f32[2,20,8,128]{3,2,1,0:T(8,128)}, f32[2,20,8,128]{3,2,1,0:T(8,128)S(1)}, f32[32,19,1,128]{3,2,1,0:T(1,128)S(1)}) custom-call(f32[2,20,8,128]{3,2,1,0:T(8,128)} %tracers.3, f32[2,20,8,128]{3,2,1,0:T(8,128)} %velocity.3, s32[8,128]{1,0:T(8,128)} %refs_2_.1, f32[8,512]{1,0:T(8,128)} %diagonal.1, f32[20]{0:T(128)} %thickness.1, ...), custom_call_target="tpu_custom_call" | custom-call | tf_op jit(solution)/shard_map/pallas_call | solution.py:344
  10.6 0.0 copy-start
  10.6 22.8 %all_to_all.5.refs_0_ = f32[32,19,1,128]{3,2,1,0:T(1,128)S(1)} all-to-all(f32[32,19,1,128]{3,2,1,0:T(1,128)S(1)} %get-tuple-element.17), channel_id=1, replica_groups=mesh['bx'=8,'by'=4] {'bx','by'}, dimensions={0} | all-to-all | bytes 622592 | tf_op jit(solution)/shard_map/all_to_all | solution.py:353
  33.4 0.0 copy-done
  33.4 3.0 %shard_map.78 = (f32[2,20,8,128]{3,2,1,0:T(8,128)}, f32[8,128]{1,0:T(8,128)}) custom-call(f32[32,19,1,128]{3,2,1,0:T(1,128)S(1)} %all_to_all.5.refs_0_, f32[2,20,8,128]{3,2,1,0:T(8,128)S(1)} %get-tuple-element.18.refs_1_, s32[8,128]{1,0:T(8,128)S(1)} %copy-done), custom_call_target="tpu_custom_call" | custom-call | tf_op jit(solution)/shard_map/pallas_call | solution.py:358
Async XLA Ops:
  1.9 5.0 %collective-permute-start.2 = (f32[8,128]{1,0:T(8,128)S(1)}, f32[8,128]{1,0:T(8,128)S(1)}, u32[]{:S(2)}, u32[]{:S(2)}) collective-permute-start(f32[8,128]{1,0:T(8,128)S(1)} %get-tuple-element.14), channel_id=1, source_target_pairs={{0,1},{2,3},{1,0},{3,2},{4,5},{6,7},{5,4},{7,6},{8,9},{10,11},{9,8... | collective-permute-start | bytes 12296 | tf_op jit(solution)/shard_map/ppermute | solution.py:337
  4.9 2.0 %collective-permute-start.3 = (f32[8,128]{1,0:T(8,128)S(1)}, f32[8,128]{1,0:T(8,128)S(1)}, u32[]{:S(2)}, u32[]{:S(2)}) collective-permute-start(f32[8,128]{1,0:T(8,128)S(1)} %get-tuple-element.15), channel_id=1, source_target_pairs={{1,2},{2,1},{5,6},{6,5},{9,10},{10,9},{13,14},{14,13},{17,18},{18,... | collective-permute-start | bytes 12296 | tf_op jit(solution)/shard_map/ppermute | solution.py:337
  5.5 1.4 %collective-permute-start = (f32[81,128]{1,0:T(8,128)S(1)}, f32[81,128]{1,0:T(8,128)S(1)}, u32[]{:S(2)}, u32[]{:S(2)}) collective-permute-start(f32[81,128]{1,0:T(8,128)S(1)} %get-tuple-element.12), channel_id=1, source_target_pairs={{0,4},{8,12},{16,20},{24,28},{4,0},{12,8},{20,16},{28,24},{1,5},{9... | collective-permute-start | bytes 124424 | tf_op jit(solution)/shard_map/ppermute | solution.py:337
  5.6 1.3 %collective-permute-start.1 = (f32[81,128]{1,0:T(8,128)S(1)}, f32[81,128]{1,0:T(8,128)S(1)}, u32[]{:S(2)}, u32[]{:S(2)}) collective-permute-start(f32[81,128]{1,0:T(8,128)S(1)} %get-tuple-element.13), channel_id=1, source_target_pairs={{4,8},{12,16},{20,24},{8,4},{16,12},{24,20},{5,9},{13,17},{21,25},... | collective-permute-start | bytes 124424 | tf_op jit(solution)/shard_map/ppermute | solution.py:337
  6.9 0.6 %copy-start.3 = (f32[8,128]{1,0:T(8,128)}, f32[8,128]{1,0:T(8,128)S(1)}, u32[]{:S(2)}) copy-start(f32[8,128]{1,0:T(8,128)S(1)} %collective-permute-done.2.cols_a) | copy-start | bytes 12292
  6.9 0.6 %copy-start.4 = (f32[8,128]{1,0:T(8,128)}, f32[8,128]{1,0:T(8,128)S(1)}, u32[]{:S(2)}) copy-start(f32[8,128]{1,0:T(8,128)S(1)} %collective-permute-done.3.cols_b) | copy-start | bytes 12292
  6.9 0.6 %copy-start.1 = (f32[81,128]{1,0:T(8,128)}, f32[81,128]{1,0:T(8,128)S(1)}, u32[]{:S(2)}) copy-start(f32[81,128]{1,0:T(8,128)S(1)} %collective-permute-done.rows_a) | copy-start | bytes 124420
  7.6 0.6 %copy-start.2 = (f32[81,128]{1,0:T(8,128)}, f32[81,128]{1,0:T(8,128)S(1)}, u32[]{:S(2)}) copy-start(f32[81,128]{1,0:T(8,128)S(1)} %collective-permute-done.1.rows_b) | copy-start | bytes 124420
  10.6 22.8 %copy-start = (s32[8,128]{1,0:T(8,128)S(1)}, s32[8,128]{1,0:T(8,128)}, u32[]{:S(2)}) copy-start(s32[8,128]{1,0:T(8,128)} %refs_2_.1) | copy-start | bytes 12292

commit v4 on v3

--- a/solution.py
+++ b/solution.py
@@ -15,6 +15,8 @@
 VISCOSITY = 0.1
 TIME_INCREMENT = 0.2
 GRAVITY = 1.0
+
+HELD_SIZE = 2**18
 
 VMEM = pl.BlockSpec(memory_space=pltpu.VMEM)
 SMEM = pl.BlockSpec(memory_space=pltpu.SMEM)
@@ -144,7 +146,7 @@
 def solve_kernel(
     blocks_x, blocks_y, gathered, moved_velocity, wet,
     new_velocity, pressure,
-    residual, lifted_0, lifted_1, smooth_0, smooth_1, smooth_2, image_0, direction_1,
+    residual, inverses, lifted_0, lifted_1, smooth_0, smooth_1, smooth_2, image_0, direction_1,
 ):
     levels, cols_x, rows_y = moved_velocity.shape[1:]
     shape = (cols_x, rows_y)
@@ -181,9 +183,6 @@
             jnp.where(high_y, ahead[c + 1], ahead[c]) + jnp.where(low_y, behind[c], behind[c + 1])
             for c in range(blocks_y)
         ]
-
-    def inverse_of(index):
-        return gathered[index, cols_x : 2 * cols_x, 0, :]
 
     def lift(inverse, tile):
         first = inverse * tile
@@ -214,8 +213,9 @@
                 forcing = forcing + jnp.where(high_y, edge_column(index + 1, 0), 0.0)
             if column > 0:
                 forcing = forcing - jnp.where(low_y, edge_column(index - 1, 1), 0.0)
-            inverse = inverse_of(index)
+            inverse = gathered[index, cols_x : 2 * cols_x, 0, :]
             lifted = lift(inverse, forcing)
+            inverses[index] = inverse
             residual[index] = forcing
             lifted_0[index] = lifted
             smooth_0[index] = inverse * lifted
@@ -249,7 +249,7 @@
         for column in range(blocks_y):
             index = row * blocks_y + column
             left = residual[index] - step_0 * image_0[index]
-            inverse = inverse_of(index)
+            inverse = inverses[index]
             lifted = lift(inverse, left)
             residual[index] = left
             lifted_1[index] = lifted
@@ -267,7 +267,7 @@
             index = row * blocks_y + column
             direction_1[index] = smooth_1[index] + turn_1 * smooth_0[index]
             left = residual[index] - step_1 * (image_1[index] + turn_1 * image_0[index])
-            inverse = inverse_of(index)
+            inverse = inverses[index]
             lifted = lift(inverse, left)
             residual[index] = left
             lifted_0[index] = lifted
@@ -323,8 +323,14 @@
         return jax.ShapeDtypeStruct(dims, jnp.float32)
 
     def held(*dims):
-        return pltpu.VMEM(dims, jnp.float32)
-
+        return pltpu.VMEM(dims, jnp.float32) if math.prod(dims) <= HELD_SIZE else like(*dims)
+
+    def kept(array):
+        if array.size > HELD_SIZE:
+            return array
+        return pltpu.with_memory_space_constraint(array, pltpu.VMEM)
+
+    tracers, velocity, wet_levels = (kept(tracers), kept(velocity), kept(wet_levels))
     rows_a, rows_b, cols_a, cols_b = pl.pallas_call(
         pack_rims,
         out_shape=[held(rim_rows, rows_y)] * 2 + [held(*shape)] * 2,
@@ -336,8 +342,8 @@
         pairs = [(i, i + 1) for i in range(first, lax.axis_size(axis) - 1, 2)]
         return lax.ppermute(message, axis, pairs + [(j, i) for i, j in pairs])
 
-    cols_a, cols_b = (exchange(cols_a, "by", 0), exchange(cols_b, "by", 1))
-    rows_a, rows_b = (exchange(rows_a, "bx", 0), exchange(rows_b, "bx", 1))
+    rows_b, rows_a = (exchange(rows_b, "bx", 1), exchange(rows_a, "bx", 0))
+    cols_b, cols_a = (exchange(cols_b, "by", 1), exchange(cols_a, "by", 0))
     positions = (lax.axis_index("by") * rows_y + jnp.arange(rows_y, dtype=jnp.int32)).astype(jnp.float32)
     latitude = latitude_rate(positions, blocks_y * rows_y)[None]
 
@@ -347,8 +353,8 @@
         in_specs=[VMEM] * 4 + [SMEM] + [VMEM] * 5,
         out_specs=[VMEM] * 3,
     )(
-        tracers, velocity, wet_levels, diagonal, thickness, latitude,
-        rows_a, rows_b, cols_a, cols_b,
+        tracers, velocity, wet_levels, kept(diagonal), thickness, kept(latitude),
+        kept(rows_a), kept(rows_b), kept(cols_a), kept(cols_b),
     )
     gathered = lax.all_to_all(surface, ("bx", "by"), split_axis=0, concat_axis=0, tiled=True)
 
@@ -360,9 +366,9 @@
         out_shape=[like(*velocity.shape), like(*shape)],
         in_specs=[VMEM] * 3,
         out_specs=[VMEM] * 2,
-        scratch_shapes=[pltpu.VMEM((blocks, *shape), jnp.float32)] * 8,
+        scratch_shapes=[pltpu.VMEM((blocks, *shape), jnp.float32)] * 9,
         compiler_params=pltpu.CompilerParams(vmem_limit_bytes=(4 + 52 * blocks // 1024) * 2**20),
-    )(gathered, moved_velocity, wet_levels)
+    )(kept(gathered), kept(moved_velocity), wet_levels)
     return new_tracers, new_velocity, pressure
 
 

time: 36.7 us -> 37.2 us (1.014)
  Pallas kernels: 6.69 us -> 5.28 us
  local copies, waits for them, and re-layouts: 1.22 us -> 2.52 us
  blocking collectives: 22.8 us -> 23.5 us
  other arithmetic: 0.62 us -> 0.05 us
  waiting for transfers between devices: 0.01 us -> 0.49 us
    unnamed x10 -> x8, local copies, waits for them, and re-layouts: 1.22 us -> 2.52 us
    pallas_call x1, Pallas kernels: 1.24 us -> 0.24 us  [body(): pl.pallas_call(pack_rims, out_shape=[held(rim_rows, rows_y)] * 2 + [held(...]
    all_to_all x1, blocking collectives: 22.8 us -> 23.5 us  [body(): lax.all_to_all(surface, ('bx', 'by'), split_axis=0, concat_axis=0, tiled=...]
    mul x1, other arithmetic: 0.62 us -> 0.05 us  [latitude_rate(): return 1.5 * jnp.sin(math.pi * ((positions + 0.5) / total_rows - 0.5))]
    ppermute x4, waiting for transfers between devices: 0.01 us -> 0.49 us  [exchange(): return lax.ppermute(message, axis, pairs + [(j, i) for i, j in pairs])]
    pallas_call x1, Pallas kernels: 2.45 us -> 2.05 us  [body(): pl.pallas_call(level_kernel, out_shape=[like(*tracers.shape), held(*veloc...]
  transfers between devices with their start and end apart: 4 -> 4, of which waited for: 0 -> 2; matrix products, arithmetic and copies ran while one was open for 2% -> 0% of each run, Pallas kernels for 0% -> 0%
where the time goes in v4:
time: 37.2 us; the launch traced here: 36.9 us
  blocking collectives  23.5 us (63%)
  Pallas kernels  5.28 us (14%)
  starting transfers between devices  4.39 us (12%)
  local copies, waits for them, and re-layouts  2.52 us (7%)
  between operations  0.69 us (2%)
  waiting for transfers between devices  0.49 us (1%)
    all_to_all x1, blocking collectives, body(): lax.all_to_all(surface, ('bx', 'by'), split_axis=0, concat_axis=0, tiled=...  23.5 us
    ppermute x4, starting transfers between devices, exchange(): return lax.ppermute(message, axis, pairs + [(j, i) for i, j in pairs])  4.39 us
    pallas_call x1, Pallas kernels, body(): pl.pallas_call(solve, out_shape=[like(*velocity.shape), like(*shape)], in...  2.99 us
    unnamed x8, local copies, waits for them, and re-layouts  2.52 us
    pallas_call x1, Pallas kernels, body(): pl.pallas_call(level_kernel, out_shape=[like(*tracers.shape), held(*veloc...  2.05 us
  transfers between devices with their start and end apart: 4, of which 2 were waited for; matrix products, arithmetic and copies ran while one was open for 0% of the time, Pallas kernels for 0%

profile of v4, /device:TPU:0, one launch (start us, length us, event | category | flops | bytes accessed | tf_op | source)
XLA Modules:
  0.0 36.9 jit_solution(17642553084226305781)
XLA Ops:
  0.6 0.0 copy-start
  0.6 0.9 %copy-done = f32[2,20,8,128]{3,2,1,0:T(8,128)S(1)} copy-done((f32[2,20,8,128]{3,2,1,0:T(8,128)S(1)}, f32[2,20,8,128]{3,2,1,0:T(8,128)}, u32[]{:S(2)}) %copy-start) | copy-done | bytes 163864
  1.5 0.0 copy-start.1
  1.5 0.9 %copy-done.1 = f32[2,20,8,128]{3,2,1,0:T(8,128)S(1)} copy-done((f32[2,20,8,128]{3,2,1,0:T(8,128)S(1)}, f32[2,20,8,128]{3,2,1,0:T(8,128)}, u32[]{:S(2)}) %copy-start.1) | copy-done | bytes 163864
  2.5 0.0 copy-start.2
  2.5 0.7 %copy-done.2 = s32[8,128]{1,0:T(8,128)S(1)} copy-done((s32[8,128]{1,0:T(8,128)S(1)}, s32[8,128]{1,0:T(8,128)}, u32[]{:S(2)}) %copy-start.2) | copy-done | bytes 4120
  3.2 0.2 shard_map.76
  3.4 0.0 copy-start.3
  3.4 3.0 %collective-permute-start.2 = (f32[8,128]{1,0:T(8,128)S(1)}, f32[8,128]{1,0:T(8,128)S(1)}, u32[]{:S(2)}, u32[]{:S(2)}) collective-permute-start(f32[8,128]{1,0:T(8,128)S(1)} %get-tuple-element.14), channel_id=1, source_target_pairs={{0,1},{2,3},{1,0},{3,2},{4,5},{6,7},{5,4},{7,6},{8,9},{10,11},{9,8... | collective-permute-start | bytes 12296 | tf_op jit(solution)/shard_map/ppermute | solution.py:343
  6.4 0.6 %collective-permute-start.3 = (f32[8,128]{1,0:T(8,128)S(1)}, f32[8,128]{1,0:T(8,128)S(1)}, u32[]{:S(2)}, u32[]{:S(2)}) collective-permute-start(f32[8,128]{1,0:T(8,128)S(1)} %get-tuple-element.15), channel_id=1, source_target_pairs={{1,2},{2,1},{5,6},{6,5},{9,10},{10,9},{13,14},{14,13},{17,18},{18,... | collective-permute-start | bytes 12296 | tf_op jit(solution)/shard_map/ppermute | solution.py:343
  7.1 0.1 collective-permute-start
  7.1 0.7 %collective-permute-start.1 = (f32[81,128]{1,0:T(8,128)S(1)}, f32[81,128]{1,0:T(8,128)S(1)}, u32[]{:S(2)}, u32[]{:S(2)}) collective-permute-start(f32[81,128]{1,0:T(8,128)S(1)} %get-tuple-element.13), channel_id=1, source_target_pairs={{4,8},{12,16},{20,24},{8,4},{16,12},{24,20},{5,9},{13,17},{21,25},... | collective-permute-start | bytes 124424 | tf_op jit(solution)/shard_map/ppermute | solution.py:343
  7.9 0.1 collective-permute-done.2.cols_a
  8.0 0.0 collective-permute-done.3.cols_b
  8.0 0.4 collective-permute-done.rows_a
  8.4 0.0 collective-permute-done.1.rows_b
  8.4 0.0 copy-done.3
  8.4 2.1 %shard_map.77 = (f32[2,20,8,128]{3,2,1,0:T(8,128)}, f32[2,20,8,128]{3,2,1,0:T(8,128)S(1)}, f32[32,19,1,128]{3,2,1,0:T(1,128)S(1)}) custom-call(f32[2,20,8,128]{3,2,1,0:T(8,128)S(1)} %copy-done, f32[2,20,8,128]{3,2,1,0:T(8,128)S(1)} %copy-done.1, s32[8,128]{1,0:T(8,128)S(1)} %copy-done.2, f32[8,512]{1,0:T(8,128)S(1)} %copy-done.3, f32[20]{0:T(128)} %thickness.1, ...), custom_call_target="tpu_custom_call" | custom-call | tf_op jit(solution)/shard_map/pallas_call | solution.py:350
  10.4 23.5 %all_to_all.5.refs_0_ = f32[32,19,1,128]{3,2,1,0:T(1,128)S(1)} all-to-all(f32[32,19,1,128]{3,2,1,0:T(1,128)S(1)} %get-tuple-element.17), channel_id=1, replica_groups=mesh['bx'=8,'by'=4] {'bx','by'}, dimensions={0} | all-to-all | bytes 622592 | tf_op jit(solution)/shard_map/all_to_all | solution.py:359
  33.9 3.0 %shard_map.78 = (f32[2,20,8,128]{3,2,1,0:T(8,128)}, f32[8,128]{1,0:T(8,128)}) custom-call(f32[32,19,1,128]{3,2,1,0:T(1,128)S(1)} %all_to_all.5.refs_0_, f32[2,20,8,128]{3,2,1,0:T(8,128)S(1)} %get-tuple-element.18.refs_1_, s32[8,128]{1,0:T(8,128)S(1)} %copy-done.2), custom_call_target="tpu_custom_call" | custom-call | tf_op jit(solution)/shard_map/pallas_call | solution.py:364
  (1 shorter events, 0.0 us)
Async XLA Ops:
  0.6 0.9 %copy-start = (f32[2,20,8,128]{3,2,1,0:T(8,128)S(1)}, f32[2,20,8,128]{3,2,1,0:T(8,128)}, u32[]{:S(2)}) copy-start(f32[2,20,8,128]{3,2,1,0:T(8,128)} %tracers.3) | copy-start | bytes 491524
  1.5 0.9 %copy-start.1 = (f32[2,20,8,128]{3,2,1,0:T(8,128)S(1)}, f32[2,20,8,128]{3,2,1,0:T(8,128)}, u32[]{:S(2)}) copy-start(f32[2,20,8,128]{3,2,1,0:T(8,128)} %velocity.3) | copy-start | bytes 491524
  2.5 0.7 %copy-start.2 = (s32[8,128]{1,0:T(8,128)S(1)}, s32[8,128]{1,0:T(8,128)}, u32[]{:S(2)}) copy-start(s32[8,128]{1,0:T(8,128)} %refs_2_.1) | copy-start | bytes 12292
  3.4 5.0 %copy-start.3 = (f32[8,512]{1,0:T(8,128)S(1)}, f32[8,512]{1,0:T(8,128)}, u32[]{:S(2)}) copy-start(f32[8,512]{1,0:T(8,128)} %diagonal.1) | copy-start | bytes 49156
  3.4 4.6 %collective-permute-start.2 = (f32[8,128]{1,0:T(8,128)S(1)}, f32[8,128]{1,0:T(8,128)S(1)}, u32[]{:S(2)}, u32[]{:S(2)}) collective-permute-start(f32[8,128]{1,0:T(8,128)S(1)} %get-tuple-element.14), channel_id=1, source_target_pairs={{0,1},{2,3},{1,0},{3,2},{4,5},{6,7},{5,4},{7,6},{8,9},{10,11},{9,8... | collective-permute-start | bytes 12296 | tf_op jit(solution)/shard_map/ppermute | solution.py:343
  6.4 1.6 %collective-permute-start.3 = (f32[8,128]{1,0:T(8,128)S(1)}, f32[8,128]{1,0:T(8,128)S(1)}, u32[]{:S(2)}, u32[]{:S(2)}) collective-permute-start(f32[8,128]{1,0:T(8,128)S(1)} %get-tuple-element.15), channel_id=1, source_target_pairs={{1,2},{2,1},{5,6},{6,5},{9,10},{10,9},{13,14},{14,13},{17,18},{18,... | collective-permute-start | bytes 12296 | tf_op jit(solution)/shard_map/ppermute | solution.py:343
  7.1 1.3 %collective-permute-start = (f32[81,128]{1,0:T(8,128)S(1)}, f32[81,128]{1,0:T(8,128)S(1)}, u32[]{:S(2)}, u32[]{:S(2)}) collective-permute-start(f32[81,128]{1,0:T(8,128)S(1)} %get-tuple-element.12), channel_id=1, source_target_pairs={{0,4},{8,12},{16,20},{24,28},{4,0},{12,8},{20,16},{28,24},{1,5},{9... | collective-permute-start | bytes 124424 | tf_op jit(solution)/shard_map/ppermute | solution.py:343
  7.1 1.2 %collective-permute-start.1 = (f32[81,128]{1,0:T(8,128)S(1)}, f32[81,128]{1,0:T(8,128)S(1)}, u32[]{:S(2)}, u32[]{:S(2)}) collective-permute-start(f32[81,128]{1,0:T(8,128)S(1)} %get-tuple-element.13), channel_id=1, source_target_pairs={{4,8},{12,16},{20,24},{8,4},{16,12},{24,20},{5,9},{13,17},{21,25},... | collective-permute-start | bytes 124424 | tf_op jit(solution)/shard_map/ppermute | solution.py:343

commit v5 on v4

--- a/solution.py
+++ b/solution.py
@@ -19,6 +19,7 @@
 HELD_SIZE = 2**18
 
 VMEM = pl.BlockSpec(memory_space=pltpu.VMEM)
+ANY = pl.BlockSpec(memory_space=pl.ANY)
 SMEM = pl.BlockSpec(memory_space=pltpu.SMEM)
 
 
@@ -30,10 +31,34 @@
     return lax.broadcasted_iota(jnp.int32, shape, 0)
 
 
-def pack_rims(tracers, velocity, wet, rows_a, rows_b, cols_a, cols_b):
+def position_x():
+    return lax.axis_index("z") * lax.axis_size("core") + lax.axis_index("core")
+
+
+def pack_rims(
+    tracers_in, velocity_in, wet_in, diagonal_in, thickness,
+    rows_a, rows_b, cols_a, cols_b, tracers, velocity, wet, diagonal, weights,
+    semaphores,
+):
     levels, cols_x, rows_y = tracers.shape[1:]
-    even_x, even_y = (lax.axis_index("bx") % 2 == 0, lax.axis_index("by") % 2 == 0)
+    row_start = pl.multiple_of(lax.axis_index("by") * rows_y, rows_y)
+    copies = [
+        pltpu.make_async_copy(source, target, semaphores.at[number])
+        for number, (source, target) in enumerate((
+            (tracers_in, tracers),
+            (velocity_in, velocity),
+            (wet_in, wet),
+            (diagonal_in.at[:, pl.ds(row_start, rows_y)], diagonal),
+        ))
+    ]
+    for copy in copies:
+        copy.start()
+    for level in range(levels):
+        weights[level : level + 1, :] = jnp.full((1, rows_y), thickness[level], jnp.float32)
+    even_x, even_y = (lax.axis_index("core") == 0, lax.axis_index("by") % 2 == 0)
     lane = lanes_of((cols_x, rows_y))
+    for copy in copies:
+        copy.wait()
     counts = wet[...].astype(jnp.float32)
     first, last = jnp.zeros_like(counts), jnp.zeros_like(counts)
     for index in range(4 * levels + 1):
@@ -52,15 +77,16 @@
 
 
 def level_kernel(
-    tracers, velocity, wet, diagonal, thickness, latitude, rows_a, rows_b, cols_a, cols_b,
+    tracers, velocity, wet, diagonal, weights, latitude, rows_a, rows_b, cols_a, cols_b,
     new_tracers, moved_velocity, surface,
+    next_tracers, gradients, semaphore,
 ):
     levels, cols_x, rows_y = tracers.shape[1:]
     shape = (cols_x, rows_y)
     lane, sublane = (lanes_of(shape), sublanes_of(shape))
     low_x, high_x = (sublane == 0, sublane == cols_x - 1)
     low_y, high_y = (lane == 0, lane == rows_y - 1)
-    even_x, even_y = (lax.axis_index("bx") % 2 == 0, lax.axis_index("by") % 2 == 0)
+    even_x, even_y = (lax.axis_index("core") == 0, lax.axis_index("by") % 2 == 0)
     after_cols = jnp.where(even_y, cols_a[...], cols_b[...])
     before_cols = jnp.where(even_y, cols_b[...], cols_a[...])
 
@@ -79,48 +105,51 @@
     shared = [jnp.minimum(counts, other) for other in around]
     both_x = jnp.minimum(shared[0], shared[1])
     both_y = jnp.minimum(shared[2], shared[3])
-    coriolis = jnp.broadcast_to(latitude[...], shape)
     zero = jnp.zeros(shape, jnp.float32)
-    difference_x, difference_y, flow_x, flow_y = (zero, zero, zero, zero)
+
+    def laplacian(tile, others, level):
+        total = zero
+        for other, limit in zip(others, shared):
+            total = total + jnp.where(limit > level, other - tile, 0.0)
+        return total
+
+    difference_x, difference_y = (zero, zero)
     for level in range(levels):
-        here = counts > level
-        open_to = [other > level for other in shared]
-        wet_around = [other > level for other in around]
-        weight = thickness[level]
+        weight = weights[level : level + 1, :]
         heat, salt = (tracers[0, level], tracers[1, level])
-        zonal, merid = (velocity[0, level], velocity[1, level])
         heat_around = neighbours(heat, level)
         salt_around = neighbours(salt, levels + level)
-
-        def laplacian(tile, others):
-            total = zero
-            for other, passable in zip(others, open_to):
-                total = total + jnp.where(passable, other - tile, 0.0)
-            return total
-
         loads = [
-            jnp.where(is_wet, SALINITY_BETA * s - HEAT_ALPHA * t, 0.0)
-            for is_wet, s, t in zip(wet_around, salt_around, heat_around)
+            jnp.where(count > level, SALINITY_BETA * s - HEAT_ALPHA * t, 0.0)
+            for count, s, t in zip(around, salt_around, heat_around)
         ]
         difference_x = difference_x + weight * (loads[0] - loads[1])
         difference_y = difference_y + weight * (loads[2] - loads[3])
-        gradient_x = jnp.where(both_x > level, difference_x * 0.5, 0.0)
-        gradient_y = jnp.where(both_y > level, difference_y * 0.5, 0.0)
+        gradients[0, level] = jnp.where(both_x > level, difference_x * 0.5, 0.0)
+        gradients[1, level] = jnp.where(both_y > level, difference_y * 0.5, 0.0)
         diffusivity = TIME_INCREMENT * KAPPA_SPREAD
-        new_tracers[0, level] = heat + diffusivity * laplacian(heat, heat_around)
-        new_tracers[1, level] = salt + diffusivity * laplacian(salt, salt_around)
-        spread_x = laplacian(zonal, neighbours(zonal, 2 * levels + level))
-        spread_y = laplacian(merid, neighbours(merid, 3 * levels + level))
-        zonal_rate = coriolis * merid - gradient_x + VISCOSITY * spread_x
-        merid_rate = -coriolis * zonal - gradient_y + VISCOSITY * spread_y
+        next_tracers[0, level] = heat + diffusivity * laplacian(heat, heat_around, level)
+        next_tracers[1, level] = salt + diffusivity * laplacian(salt, salt_around, level)
+    leaving = pltpu.make_async_copy(next_tracers, new_tracers, semaphore)
+    leaving.start()
+
+    coriolis = jnp.broadcast_to(latitude[...], shape)
+    flow_x, flow_y = (zero, zero)
+    for level in range(levels):
+        here = counts > level
+        weight = weights[level : level + 1, :]
+        zonal, merid = (velocity[0, level], velocity[1, level])
+        spread_x = laplacian(zonal, neighbours(zonal, 2 * levels + level), level)
+        spread_y = laplacian(merid, neighbours(merid, 3 * levels + level), level)
+        zonal_rate = coriolis * merid - gradients[0, level] + VISCOSITY * spread_x
+        merid_rate = -coriolis * zonal - gradients[1, level] + VISCOSITY * spread_y
         next_zonal = zonal + jnp.where(here, TIME_INCREMENT * zonal_rate, 0.0)
         next_merid = merid + jnp.where(here, TIME_INCREMENT * merid_rate, 0.0)
         moved_velocity[0, level] = next_zonal
         moved_velocity[1, level] = next_merid
         flow_x = flow_x + jnp.where(here, weight * next_zonal, 0.0)
         flow_y = flow_y + jnp.where(here, weight * next_merid, 0.0)
-    row_start = pl.multiple_of(lax.axis_index("by") * rows_y, rows_y)
-    inverse = jnp.where(counts > 0, 1.0, 0.0) / (4.0 + diagonal[:, pl.ds(row_start, rows_y)])
+    inverse = jnp.where(counts > 0, 1.0, 0.0) / (4.0 + diagonal[...])
     ahead = jnp.where(high_x, 0.0, pltpu.roll(flow_x, cols_x - 1, 0))
     behind = jnp.where(low_x, 0.0, pltpu.roll(flow_x, 1, 0))
     slope = ahead - behind
@@ -141,10 +170,11 @@
         surface[target, 2 * cols_x + 2 : 2 * cols_x + 3, 0, :] = corner
 
     pl.loop(0, surface.shape[0], unroll=8)(place)
+    leaving.wait()
 
 
 def solve_kernel(
-    blocks_x, blocks_y, gathered, moved_velocity, wet,
+    blocks_x, blocks_y, gathered, swapped, moved_velocity, wet,
     new_velocity, pressure,
     residual, inverses, lifted_0, lifted_1, smooth_0, smooth_1, smooth_2, image_0, direction_1,
 ):
@@ -195,31 +225,49 @@
     def total(values):
         return jnp.sum(values, axis=(0, 1), keepdims=True)
 
-    def edge_rows(which):
-        place = 2 * cols_x + which
-        return lambda index: gathered[index, place : place + 1, 0, :]
-
-    def edge_column(index, which):
-        corner = jnp.where(lane == sublane + which * cols_x, edge_rows(2)(index), 0.0)
-        return jnp.sum(corner, axis=1, keepdims=True)
-
-    def start(row, carry):
-        for column in range(blocks_y):
-            index = row * blocks_y + column
-            forcing = gathered[index, 0:cols_x, 0, :]
-            forcing = forcing + jnp.where(high_x, guarded(edge_rows(0), row + 1, column), 0.0)
-            forcing = forcing - jnp.where(low_x, guarded(edge_rows(1), row - 1, column), 0.0)
-            if column + 1 < blocks_y:
-                forcing = forcing + jnp.where(high_y, edge_column(index + 1, 0), 0.0)
-            if column > 0:
-                forcing = forcing - jnp.where(low_y, edge_column(index - 1, 1), 0.0)
-            inverse = gathered[index, cols_x : 2 * cols_x, 0, :]
-            lifted = lift(inverse, forcing)
-            inverses[index] = inverse
-            residual[index] = forcing
-            lifted_0[index] = lifted
-            smooth_0[index] = inverse * lifted
-        return carry
+    height = 2 * cols_x + 3
+
+    def start_from(by_core):
+        def rows_of(row, column, first, count):
+            if isinstance(row, int):
+                place = (row // 2 * blocks_y + column) * height + first
+                return by_core[row % 2][place : place + count, :]
+            place = (row // 2 * blocks_y + column) * height + first
+            found = [blocks[pl.ds(place, count), :] for blocks in by_core]
+            return jnp.where(row % 2 == 0, *found)
+
+        def edge_row(which, row, column):
+            if isinstance(row, int):
+                inside = 0 <= row < blocks_x
+                return rows_of(row, column, 2 * cols_x + which, 1) if inside else 0.0
+            inside = jnp.logical_and(row >= 0, row < blocks_x).astype(jnp.float32)
+            row = jnp.clip(row, 0, blocks_x - 1)
+            return rows_of(row, column, 2 * cols_x + which, 1) * inside
+
+        def step(row, carry):
+            corners = [rows_of(row, c, 2 * cols_x + 2, 1) for c in range(blocks_y)]
+            filler = [jnp.zeros((1, rows_y), jnp.float32)] * (-blocks_y % 8)
+            corners = jnp.transpose(jnp.concatenate(corners + filler, axis=0))
+            for column in range(blocks_y):
+                index = row * blocks_y + column
+                forcing = rows_of(row, column, 0, cols_x)
+                forcing = forcing + jnp.where(high_x, edge_row(0, row + 1, column), 0.0)
+                forcing = forcing - jnp.where(low_x, edge_row(1, row - 1, column), 0.0)
+                if column + 1 < blocks_y:
+                    beyond = corners[0:cols_x, column + 1 : column + 2]
+                    forcing = forcing + jnp.where(high_y, beyond, 0.0)
+                if column > 0:
+                    beyond = corners[cols_x : 2 * cols_x, column - 1 : column]
+                    forcing = forcing - jnp.where(low_y, beyond, 0.0)
+                inverse = rows_of(row, column, cols_x, cols_x)
+                lifted = lift(inverse, forcing)
+                inverses[index] = inverse
+                residual[index] = forcing
+                lifted_0[index] = lifted
+                smooth_0[index] = inverse * lifted
+            return carry
+
+        each_row(step, 0)
 
     def operate(lifted, smooth, image):
         def load(index, rows=slice(None)):
@@ -241,7 +289,9 @@
         inner, curvature = each_row(step, (zero, zero))
         return total(inner), total(curvature)
 
-    each_row(start, 0)
+    own_core = lax.axis_index("core")
+    pl.when(own_core == 0)(lambda: start_from((gathered, swapped)))
+    pl.when(own_core == 1)(lambda: start_from((swapped, gathered)))
     inner_0, curvature_0 = operate(lifted_0, smooth_0, image_0)
     step_0 = inner_0 / curvature_0
 
@@ -284,7 +334,7 @@
         result = step_0 * smooth_0[index] + step_1 * previous
         return result + step_2 * (smooth_2[index] + turn_2 * previous)
 
-    own_x, own_y = (lax.axis_index("bx"), lax.axis_index("by"))
+    own_x, own_y = (position_x(), lax.axis_index("by"))
 
     def block(shift_x, shift_y):
         row, column = (own_x + shift_x, own_y + shift_y)
@@ -314,9 +364,10 @@
 def body(tracers, velocity, wet_levels, thickness, diagonal):
     levels = tracers.shape[1]
     cols_x, rows_y = wet_levels.shape
-    blocks_x, blocks_y = (lax.axis_size("bx"), lax.axis_size("by"))
-    blocks = blocks_x * blocks_y
+    chips_z, cores, blocks_y = (lax.axis_size("z"), lax.axis_size("core"), lax.axis_size("by"))
+    blocks_x = chips_z * cores
     shape = (cols_x, rows_y)
+    height = 2 * cols_x + 3
     rim_rows = 4 * levels + 1
 
     def like(*dims):
@@ -330,17 +381,25 @@
             return array
         return pltpu.with_memory_space_constraint(array, pltpu.VMEM)
 
-    tracers, velocity, wet_levels = (kept(tracers), kept(velocity), kept(wet_levels))
-    rows_a, rows_b, cols_a, cols_b = pl.pallas_call(
+    fields = (tracers, velocity, wet_levels, diagonal)
+    rows_a, rows_b, cols_a, cols_b, *block = pl.pallas_call(
         pack_rims,
-        out_shape=[held(rim_rows, rows_y)] * 2 + [held(*shape)] * 2,
-        in_specs=[VMEM] * 3,
-        out_specs=[VMEM] * 4,
-    )(tracers, velocity, wet_levels)
+        out_shape=[
+            held(rim_rows, rows_y), held(rim_rows, rows_y), held(*shape), held(*shape),
+            held(*tracers.shape), held(*velocity.shape), pltpu.VMEM(shape, wet_levels.dtype),
+            held(*shape), held(levels, rows_y),
+        ],
+        in_specs=[ANY] * 4 + [SMEM],
+        out_specs=[VMEM] * 9,
+        scratch_shapes=[pltpu.SemaphoreType.DMA((4,))],
+    )(*(pltpu.with_memory_space_constraint(array, pltpu.HBM) for array in fields), thickness)
+    block = [kept(array) for array in block]
 
     def exchange(message, axis, first):
-        pairs = [(i, i + 1) for i in range(first, lax.axis_size(axis) - 1, 2)]
-        return lax.ppermute(message, axis, pairs + [(j, i) for i, j in pairs])
+        size = blocks_x if axis == "bx" else blocks_y
+        pairs = [(i, i + 1) for i in range(first, size - 1, 2)]
+        axes = ("z", "core") if axis == "bx" else axis
+        return lax.ppermute(message, axes, pairs + [(j, i) for i, j in pairs])
 
     rows_b, rows_a = (exchange(rows_b, "bx", 1), exchange(rows_a, "bx", 0))
     cols_b, cols_a = (exchange(cols_b, "by", 1), exchange(cols_a, "by", 0))
@@ -349,41 +408,53 @@
 
     new_tracers, moved_velocity, surface = pl.pallas_call(
         level_kernel,
-        out_shape=[like(*tracers.shape), held(*velocity.shape), held(blocks, 2 * cols_x + 3, 1, rows_y)],
-        in_specs=[VMEM] * 4 + [SMEM] + [VMEM] * 5,
-        out_specs=[VMEM] * 3,
-    )(
-        tracers, velocity, wet_levels, kept(diagonal), thickness, kept(latitude),
-        kept(rows_a), kept(rows_b), kept(cols_a), kept(cols_b),
-    )
-    gathered = lax.all_to_all(surface, ("bx", "by"), split_axis=0, concat_axis=0, tiled=True)
+        out_shape=[
+            like(*tracers.shape), held(*velocity.shape),
+            held(chips_z * blocks_y, height, 1, rows_y),
+        ],
+        in_specs=[VMEM] * 10,
+        out_specs=[ANY, VMEM, VMEM],
+        scratch_shapes=[
+            pltpu.VMEM(tracers.shape, jnp.float32),
+            pltpu.VMEM((2, levels, *shape), jnp.float32),
+            pltpu.SemaphoreType.DMA,
+        ],
+    )(*block, kept(latitude), kept(rows_a), kept(rows_b), kept(cols_a), kept(cols_b))
+
+    gathered = lax.all_to_all(surface, ("z", "by"), split_axis=0, concat_axis=0, tiled=True)
+    swapped = lax.ppermute(gathered, "core", [(0, 1), (1, 0)])
+    gathered, swapped = (array.reshape(-1, rows_y) for array in (gathered, swapped))
 
     def solve(*refs):
         solve_kernel(blocks_x, blocks_y, *refs)
 
+    blocks = blocks_x * blocks_y
     new_velocity, pressure = pl.pallas_call(
         solve,
         out_shape=[like(*velocity.shape), like(*shape)],
-        in_specs=[VMEM] * 3,
+        in_specs=[VMEM] * 4,
         out_specs=[VMEM] * 2,
         scratch_shapes=[pltpu.VMEM((blocks, *shape), jnp.float32)] * 9,
         compiler_params=pltpu.CompilerParams(vmem_limit_bytes=(4 + 52 * blocks // 1024) * 2**20),
-    )(kept(gathered), kept(moved_velocity), wet_levels)
+    )(kept(gathered), kept(swapped), kept(moved_velocity), block[2])
     return new_tracers, new_velocity, pressure
 
 
 def solution(mesh):
+    size_x, size_y = (mesh.shape["bx"], mesh.shape["by"])
+    chips = jax.sharding.Mesh(mesh.devices.reshape(size_x // 2, 2, size_y), ("z", "core", "by"))
+    along_x = ("z", "core")
     placed = (
-        P(None, None, "bx", "by"),
-        P(None, None, "bx", "by"),
-        P("bx", "by"),
+        P(None, None, along_x, "by"),
+        P(None, None, along_x, "by"),
+        P(along_x, "by"),
         P(),
-        P("bx", None),
+        P(along_x, None),
     )
     return jax.shard_map(
         body,
-        mesh=mesh,
+        mesh=chips,
         in_specs=placed,
-        out_specs=(P(None, None, "bx", "by"), P(None, None, "bx", "by"), P("bx", "by")),
+        out_specs=(P(None, None, along_x, "by"), P(None, None, along_x, "by"), P(along_x, "by")),
         check_vma=False,
     )

time: 37.2 us -> 33.3 us (0.90)
  blocking collectives: 23.5 us -> 20.5 us
  local copies, waits for them, and re-layouts: 2.52 us -> 0 us
  waiting for transfers between devices: 0.49 us -> 1.87 us
    all_to_all x1, blocking collectives: 23.5 us -> 20.5 us  [body(): lax.all_to_all(surface, ('z', 'by'), split_axis=0, concat_axis=0, tiled=T...]
    unnamed x8 -> x0, local copies, waits for them, and re-layouts: 2.52 us -> none
    pallas_call x1, Pallas kernels: 0.24 us -> 1.94 us  [body(): pl.pallas_call(pack_rims, out_shape=[held(rim_rows, rows_y), held(rim_row...]
    ppermute x4 -> x5, waiting for transfers between devices: 0.49 us -> 1.87 us  [the longest x1 1.38 us: body(): swapped = lax.ppermute(gathered, 'core', [(0, 1), (1, 0)])]
    pallas_call x1, Pallas kernels: 2.05 us -> 1.14 us  [body(): pl.pallas_call(level_kernel, out_shape=[like(*tracers.shape), held(*veloc...]
    pallas_call x1, Pallas kernels: 2.99 us -> 2.56 us  [body(): pl.pallas_call(solve, out_shape=[like(*velocity.shape), like(*shape)], in...]
    ppermute x4 -> x5, starting transfers between devices: 4.39 us -> 4.39 us  [the longest x4 4.39 us: exchange(): return lax.ppermute(message, axes, pairs + [(j, i) for i, j in pairs])]
  transfers between devices with their start and end apart: 4 -> 5, of which waited for: 2 -> 3; matrix products, arithmetic and copies ran while one was open for 0% -> 0% of each run, Pallas kernels for 0% -> 0%
where the time goes in v5:
time: 33.3 us; the launch traced here: 33.1 us
  blocking collectives  20.5 us (62%)
  Pallas kernels  5.64 us (17%)
  starting transfers between devices  4.39 us (13%)
  waiting for transfers between devices  1.87 us (6%)
  between operations  0.68 us (2%)
    all_to_all x1, blocking collectives, body(): lax.all_to_all(surface, ('z', 'by'), split_axis=0, concat_axis=0, tiled=T...  20.5 us
    ppermute x4, starting transfers between devices, exchange(): return lax.ppermute(message, axes, pairs + [(j, i) for i, j in pairs])  4.39 us
    pallas_call x1, Pallas kernels, body(): pl.pallas_call(solve, out_shape=[like(*velocity.shape), like(*shape)], in...  2.56 us
    pallas_call x1, Pallas kernels, body(): pl.pallas_call(pack_rims, out_shape=[held(rim_rows, rows_y), held(rim_row...  1.94 us
    ppermute x1, waiting for transfers between devices, body(): swapped = lax.ppermute(gathered, 'core', [(0, 1), (1, 0)])  1.38 us
    pallas_call x1, Pallas kernels, body(): pl.pallas_call(level_kernel, out_shape=[like(*tracers.shape), held(*veloc...  1.14 us
  transfers between devices with their start and end apart: 5, of which 3 were waited for; matrix products, arithmetic and copies ran while one was open for 0% of the time, Pallas kernels for 0%

profile of v5, /device:TPU:0, one launch (start us, length us, event | category | flops | bytes accessed | tf_op | source)
XLA Modules:
  0.0 33.1 jit_solution(4194914934013976934)
XLA Ops:
  0.6 1.9 %shard_map.76 = (f32[81,128]{1,0:T(8,128)S(1)}, f32[81,128]{1,0:T(8,128)S(1)}, f32[8,128]{1,0:T(8,128)S(1)}, f32[8,128]{1,0:T(8,128)S(1)}, f32[2,20,8,128]{3,2,1...) custom-call(f32[2,20,8,128]{3,2,1,0:T(8,128)} %tracers_in.1, ...), custom_call_target="tpu_custom_call" | custom-call | tf_op jit(solution)/shard_map/pallas_call | solution.py:385
  2.6 3.0 %collective-permute-start.2 = (f32[8,128]{1,0:T(8,128)S(1)}, f32[8,128]{1,0:T(8,128)S(1)}, u32[]{:S(2)}, u32[]{:S(2)}) collective-permute-start(f32[8,128]{1,0:T(8,128)S(1)} %get-tuple-element.24), channel_id=1, source_target_pairs={{0,1},{2,3},{1,0},{3,2},{4,5},{6,7},{5,4},{7,6},{8,9},{10,11},{9,8... | collective-permute-start | bytes 12296 | tf_op jit(solution)/shard_map/ppermute | solution.py:402
  5.6 0.6 %collective-permute-start.3 = (f32[8,128]{1,0:T(8,128)S(1)}, f32[8,128]{1,0:T(8,128)S(1)}, u32[]{:S(2)}, u32[]{:S(2)}) collective-permute-start(f32[8,128]{1,0:T(8,128)S(1)} %get-tuple-element.25), channel_id=1, source_target_pairs={{1,2},{2,1},{5,6},{6,5},{9,10},{10,9},{13,14},{14,13},{17,18},{18,... | collective-permute-start | bytes 12296 | tf_op jit(solution)/shard_map/ppermute | solution.py:402
  6.2 0.1 collective-permute-start
  6.3 0.7 %collective-permute-start.1 = (f32[81,128]{1,0:T(8,128)S(1)}, f32[81,128]{1,0:T(8,128)S(1)}, u32[]{:S(2)}, u32[]{:S(2)}) collective-permute-start(f32[81,128]{1,0:T(8,128)S(1)} %get-tuple-element.23), channel_id=1, source_target_pairs={{4,8},{12,16},{20,24},{8,4},{16,12},{24,20},{5,9},{13,17},{21,25},... | collective-permute-start | bytes 124424 | tf_op jit(solution)/shard_map/ppermute | solution.py:402
  7.0 0.1 collective-permute-done.2.cols_a
  7.2 0.0 collective-permute-done.3.cols_b
  7.2 0.4 %collective-permute-done.rows_a = f32[81,128]{1,0:T(8,128)S(1)} collective-permute-done((f32[81,128]{1,0:T(8,128)S(1)}, f32[81,128]{1,0:T(8,128)S(1)}, u32[]{:S(2)}, u32[]{:S(2)}) %collective-permute-start) | collective-permute-done | bytes 41504 | tf_op jit(solution)/shard_map/ppermute | solution.py:402
  7.5 0.0 collective-permute-done.1.rows_b
  7.5 1.1 %shard_map.77 = (f32[2,20,8,128]{3,2,1,0:T(8,128)}, f32[2,20,8,128]{3,2,1,0:T(8,128)S(1)}, f32[16,19,1,128]{3,2,1,0:T(1,128)S(1)}) custom-call(f32[2,20,8,128]{3,2,1,0:T(8,128)S(1)} %get-tuple-element.17.tracers, f32[2,20,8,128]{3,2,1,0:T(8,128)S(1)} %get-tuple-element.18.velocity, s32[8,128]{1,0:T(8,128)S(1)} %get-tuple-element.19.wet.refs_3_, ...), custom_call_target="tpu_custom_call" | custom-call | tf_op jit(solution)/shard_map/pallas_call | solution.py:409
  8.7 20.5 %all_to_all.5 = f32[16,19,1,128]{3,2,1,0:T(1,128)S(1)} all-to-all(f32[16,19,1,128]{3,2,1,0:T(1,128)S(1)} %get-tuple-element.27), channel_id=1, replica_groups=mesh['z'=4,'core'=2,'by'=4] {'z','by'}, dimensions={0} | all-to-all | bytes 311296 | tf_op jit(solution)/shard_map/all_to_all | solution.py:424
  29.2 0.0 collective-permute-start.4
  29.2 1.4 %collective-permute-done.4 = f32[16,19,1,128]{3,2,1,0:T(1,128)S(1)} collective-permute-done((f32[16,19,1,128]{3,2,1,0:T(1,128)S(1)}, f32[16,19,1,128]{3,2,1,0:T(1,128)S(1)}, u32[]{:S(2)}, u32[]{:S(2)}) %collective-permute-start.4) | collective-permute-done | bytes 155680 | tf_op jit(solution)/shard_map/ppermute | solution.py:425
  30.6 2.6 %shard_map.78 = (f32[2,20,8,128]{3,2,1,0:T(8,128)}, f32[8,128]{1,0:T(8,128)}) custom-call(f32[304,128]{1,0:T(8,128)S(1)} %bitcast.2, f32[304,128]{1,0:T(8,128)S(1)} %bitcast.3, f32[2,20,8,128]{3,2,1,0:T(8,128)S(1)} %get-tuple-element.28.refs_2_, s32[8,128]{1,0:T(8,128)S(1)} %get-tuple-element.19.wet.refs_3_), custom_call_target="tpu_custom_call" | custom-call | tf_op jit(solution)/shard_map/pallas_call | solution.py:432
  (1 shorter events, 0.0 us)
Async XLA Ops:
  2.6 4.6 %collective-permute-start.2 = (f32[8,128]{1,0:T(8,128)S(1)}, f32[8,128]{1,0:T(8,128)S(1)}, u32[]{:S(2)}, u32[]{:S(2)}) collective-permute-start(f32[8,128]{1,0:T(8,128)S(1)} %get-tuple-element.24), channel_id=1, source_target_pairs={{0,1},{2,3},{1,0},{3,2},{4,5},{6,7},{5,4},{7,6},{8,9},{10,11},{9,8... | collective-permute-start | bytes 12296 | tf_op jit(solution)/shard_map/ppermute | solution.py:402
  5.6 1.6 %collective-permute-start.3 = (f32[8,128]{1,0:T(8,128)S(1)}, f32[8,128]{1,0:T(8,128)S(1)}, u32[]{:S(2)}, u32[]{:S(2)}) collective-permute-start(f32[8,128]{1,0:T(8,128)S(1)} %get-tuple-element.25), channel_id=1, source_target_pairs={{1,2},{2,1},{5,6},{6,5},{9,10},{10,9},{13,14},{14,13},{17,18},{18,... | collective-permute-start | bytes 12296 | tf_op jit(solution)/shard_map/ppermute | solution.py:402
  6.2 1.3 %collective-permute-start = (f32[81,128]{1,0:T(8,128)S(1)}, f32[81,128]{1,0:T(8,128)S(1)}, u32[]{:S(2)}, u32[]{:S(2)}) collective-permute-start(f32[81,128]{1,0:T(8,128)S(1)} %get-tuple-element.22), channel_id=1, source_target_pairs={{0,4},{8,12},{16,20},{24,28},{4,0},{12,8},{20,16},{28,24},{1,5},{9... | collective-permute-start | bytes 124424 | tf_op jit(solution)/shard_map/ppermute | solution.py:402
  6.3 1.2 %collective-permute-start.1 = (f32[81,128]{1,0:T(8,128)S(1)}, f32[81,128]{1,0:T(8,128)S(1)}, u32[]{:S(2)}, u32[]{:S(2)}) collective-permute-start(f32[81,128]{1,0:T(8,128)S(1)} %get-tuple-element.23), channel_id=1, source_target_pairs={{4,8},{12,16},{20,24},{8,4},{16,12},{24,20},{5,9},{13,17},{21,25},... | collective-permute-start | bytes 124424 | tf_op jit(solution)/shard_map/ppermute | solution.py:402
  29.2 1.4 %collective-permute-start.4 = (f32[16,19,1,128]{3,2,1,0:T(1,128)S(1)}, f32[16,19,1,128]{3,2,1,0:T(1,128)S(1)}, u32[]{:S(2)}, u32[]{:S(2)}) collective-permute-start(f32[16,19,1,128]{3,2,1,0:T(1,128)S(1)} %all_to_all.5), channel_id=1, source_target_pairs={{0,4},{4,0},{1,5},{5,1},{2,6},{6,2},{3,7},{7,3},{8,12},{12,8},{9,1... | collective-permute-start | bytes 466952 | tf_op jit(solution)/shard_map/ppermute | solution.py:425

commit v6 on v5

--- a/solution.py
+++ b/solution.py
@@ -20,7 +20,6 @@
 
 VMEM = pl.BlockSpec(memory_space=pltpu.VMEM)
 ANY = pl.BlockSpec(memory_space=pl.ANY)
-SMEM = pl.BlockSpec(memory_space=pltpu.SMEM)
 
 
 def lanes_of(shape):
@@ -36,9 +35,9 @@
 
 
 def pack_rims(
-    tracers_in, velocity_in, wet_in, diagonal_in, thickness,
+    tracers_in, velocity_in, wet_in, diagonal_in, thickness_in,
     rows_a, rows_b, cols_a, cols_b, tracers, velocity, wet, diagonal, weights,
-    semaphores,
+    thickness, semaphores,
 ):
     levels, cols_x, rows_y = tracers.shape[1:]
     row_start = pl.multiple_of(lax.axis_index("by") * rows_y, rows_y)
@@ -48,17 +47,18 @@
             (tracers_in, tracers),
             (velocity_in, velocity),
             (wet_in, wet),
+            (thickness_in, thickness),
             (diagonal_in.at[:, pl.ds(row_start, rows_y)], diagonal),
         ))
     ]
     for copy in copies:
         copy.start()
-    for level in range(levels):
-        weights[level : level + 1, :] = jnp.full((1, rows_y), thickness[level], jnp.float32)
     even_x, even_y = (lax.axis_index("core") == 0, lax.axis_index("by") % 2 == 0)
     lane = lanes_of((cols_x, rows_y))
     for copy in copies:
         copy.wait()
+    for level in range(levels):
+        weights[level : level + 1, :] = jnp.full((1, rows_y), thickness[level], jnp.float32)
     counts = wet[...].astype(jnp.float32)
     first, last = jnp.zeros_like(counts), jnp.zeros_like(counts)
     for index in range(4 * levels + 1):
@@ -77,7 +77,7 @@
 
 
 def level_kernel(
-    tracers, velocity, wet, diagonal, weights, latitude, rows_a, rows_b, cols_a, cols_b,
+    tracers, velocity, wet, diagonal, weights, latitude, rows_b, rows_a, cols_b, cols_a,
     new_tracers, moved_velocity, surface,
     next_tracers, gradients, semaphore,
 ):
@@ -381,7 +381,7 @@
             return array
         return pltpu.with_memory_space_constraint(array, pltpu.VMEM)
 
-    fields = (tracers, velocity, wet_levels, diagonal)
+    fields = (tracers, velocity, wet_levels, diagonal, thickness)
     rows_a, rows_b, cols_a, cols_b, *block = pl.pallas_call(
         pack_rims,
         out_shape=[
@@ -389,10 +389,10 @@
             held(*tracers.shape), held(*velocity.shape), pltpu.VMEM(shape, wet_levels.dtype),
             held(*shape), held(levels, rows_y),
         ],
-        in_specs=[ANY] * 4 + [SMEM],
+        in_specs=[ANY] * 5,
         out_specs=[VMEM] * 9,
-        scratch_shapes=[pltpu.SemaphoreType.DMA((4,))],
-    )(*(pltpu.with_memory_space_constraint(array, pltpu.HBM) for array in fields), thickness)
+        scratch_shapes=[pltpu.SMEM(thickness.shape, jnp.float32), pltpu.SemaphoreType.DMA((5,))],
+    )(*(pltpu.with_memory_space_constraint(array, pltpu.HBM) for array in fields))
     block = [kept(array) for array in block]
 
     def exchange(message, axis, first):
@@ -419,7 +419,7 @@
             pltpu.VMEM((2, levels, *shape), jnp.float32),
             pltpu.SemaphoreType.DMA,
         ],
-    )(*block, kept(latitude), kept(rows_a), kept(rows_b), kept(cols_a), kept(cols_b))
+    )(*block, kept(latitude), kept(rows_b), kept(rows_a), kept(cols_b), kept(cols_a))
 
     gathered = lax.all_to_all(surface, ("z", "by"), split_axis=0, concat_axis=0, tiled=True)
     swapped = lax.ppermute(gathered, "core", [(0, 1), (1, 0)])

time: 33.3 us -> 32.5 us (0.976)
  blocking collectives: 20.5 us -> 14.4 us
  starting transfers between devices: 4.39 us -> 10.1 us
  Pallas kernels: 5.64 us -> 4.99 us
    all_to_all x1, blocking collectives: 20.5 us -> 14.4 us  [body(): lax.all_to_all(surface, ('z', 'by'), split_axis=0, concat_axis=0, tiled=T...]
    ppermute x4, starting transfers between devices: 4.39 us -> 10.1 us  [exchange(): return lax.ppermute(message, axes, pairs + [(j, i) for i, j in pairs])]
    pallas_call x1, Pallas kernels: 1.94 us -> 1.29 us  [body(): pl.pallas_call(pack_rims, out_shape=[held(rim_rows, rows_y), held(rim_row...]
  transfers between devices with their start and end apart: 5 -> 5, of which waited for: 3 -> 2; matrix products, arithmetic and copies ran while one was open for 0% -> 0% of each run, Pallas kernels for 0% -> 0%
where the time goes in v6:
time: 32.5 us; the launch traced here: 32.3 us
  blocking collectives  14.4 us (44%)
  starting transfers between devices  10.1 us (31%)
  Pallas kernels  4.99 us (15%)
  waiting for transfers between devices  2.18 us (7%)
  between operations  0.69 us (2%)
    all_to_all x1, blocking collectives, body(): lax.all_to_all(surface, ('z', 'by'), split_axis=0, concat_axis=0, tiled=T...  14.4 us
    ppermute x4, starting transfers between devices, exchange(): return lax.ppermute(message, axes, pairs + [(j, i) for i, j in pairs])  10.1 us
    pallas_call x1, Pallas kernels, body(): pl.pallas_call(solve, out_shape=[like(*velocity.shape), like(*shape)], in...  2.56 us
    ppermute x1, waiting for transfers between devices, body(): swapped = lax.ppermute(gathered, 'core', [(0, 1), (1, 0)])  1.38 us
    pallas_call x1, Pallas kernels, body(): pl.pallas_call(pack_rims, out_shape=[held(rim_rows, rows_y), held(rim_row...  1.29 us
    pallas_call x1, Pallas kernels, body(): pl.pallas_call(level_kernel, out_shape=[like(*tracers.shape), held(*veloc...  1.14 us
    ppermute x4, waiting for transfers between devices, exchange(): return lax.ppermute(message, axes, pairs + [(j, i) for i, j in pairs])  0.8 us
  transfers between devices with their start and end apart: 5, of which 2 were waited for; matrix products, arithmetic and copies ran while one was open for 0% of the time, Pallas kernels for 0%

profile of v6, /device:TPU:0, one launch (start us, length us, event | category | flops | bytes accessed | tf_op | source)
XLA Modules:
  0.0 32.3 jit_solution(12438779705368899295)
XLA Ops:
  0.6 1.3 %shard_map.76 = (f32[81,128]{1,0:T(8,128)S(1)}, f32[81,128]{1,0:T(8,128)S(1)}, f32[8,128]{1,0:T(8,128)S(1)}, f32[8,128]{1,0:T(8,128)S(1)}, f32[2,20,8,128]{3,2,1...) custom-call(f32[2,20,8,128]{3,2,1,0:T(8,128)} %tracers_in.1, ...), custom_call_target="tpu_custom_call" | custom-call | tf_op jit(solution)/shard_map/pallas_call | solution.py:385
  1.9 0.7 %collective-permute-start.2 = (f32[8,128]{1,0:T(8,128)S(1)}, f32[8,128]{1,0:T(8,128)S(1)}, u32[]{:S(2)}, u32[]{:S(2)}) collective-permute-start(f32[8,128]{1,0:T(8,128)S(1)} %get-tuple-element.24), channel_id=1, source_target_pairs={{1,2},{2,1},{5,6},{6,5},{9,10},{10,9},{13,14},{14,13},{17,18},{18,... | collective-permute-start | bytes 12296 | tf_op jit(solution)/shard_map/ppermute | solution.py:402
  2.6 5.7 %collective-permute-start.3 = (f32[8,128]{1,0:T(8,128)S(1)}, f32[8,128]{1,0:T(8,128)S(1)}, u32[]{:S(2)}, u32[]{:S(2)}) collective-permute-start(f32[8,128]{1,0:T(8,128)S(1)} %get-tuple-element.25), channel_id=1, source_target_pairs={{0,1},{2,3},{1,0},{3,2},{4,5},{6,7},{5,4},{7,6},{8,9},{10,11},{9,8... | collective-permute-start | bytes 12296 | tf_op jit(solution)/shard_map/ppermute | solution.py:402
  8.3 0.7 %collective-permute-start = (f32[81,128]{1,0:T(8,128)S(1)}, f32[81,128]{1,0:T(8,128)S(1)}, u32[]{:S(2)}, u32[]{:S(2)}) collective-permute-start(f32[81,128]{1,0:T(8,128)S(1)} %get-tuple-element.22), channel_id=1, source_target_pairs={{4,8},{12,16},{20,24},{8,4},{16,12},{24,20},{5,9},{13,17},{21,25},... | collective-permute-start | bytes 124424 | tf_op jit(solution)/shard_map/ppermute | solution.py:402
  9.0 3.0 %collective-permute-start.1 = (f32[81,128]{1,0:T(8,128)S(1)}, f32[81,128]{1,0:T(8,128)S(1)}, u32[]{:S(2)}, u32[]{:S(2)}) collective-permute-start(f32[81,128]{1,0:T(8,128)S(1)} %get-tuple-element.23), channel_id=1, source_target_pairs={{0,4},{8,12},{16,20},{24,28},{4,0},{12,8},{20,16},{28,24},{1,5},{9... | collective-permute-start | bytes 124424 | tf_op jit(solution)/shard_map/ppermute | solution.py:402
  12.1 0.0 collective-permute-done.2.cols_b
  12.1 0.0 collective-permute-done.3.cols_a
  12.1 0.0 collective-permute-done.rows_b
  12.1 0.8 %collective-permute-done.1.rows_a = f32[81,128]{1,0:T(8,128)S(1)} collective-permute-done((f32[81,128]{1,0:T(8,128)S(1)}, f32[81,128]{1,0:T(8,128)S(1)}, u32[]{:S(2)}, u32[]{:S(2)}) %collective-permute-start.1) | collective-permute-done | bytes 41504 | tf_op jit(solution)/shard_map/ppermute | solution.py:402
  12.9 1.1 %shard_map.77 = (f32[2,20,8,128]{3,2,1,0:T(8,128)}, f32[2,20,8,128]{3,2,1,0:T(8,128)S(1)}, f32[16,19,1,128]{3,2,1,0:T(1,128)S(1)}) custom-call(f32[2,20,8,128]{3,2,1,0:T(8,128)S(1)} %get-tuple-element.17.tracers, f32[2,20,8,128]{3,2,1,0:T(8,128)S(1)} %get-tuple-element.18.velocity, s32[8,128]{1,0:T(8,128)S(1)} %get-tuple-element.19.wet.refs_3_, ...), custom_call_target="tpu_custom_call" | custom-call | tf_op jit(solution)/shard_map/pallas_call | solution.py:409
  14.0 14.4 %all_to_all.5 = f32[16,19,1,128]{3,2,1,0:T(1,128)S(1)} all-to-all(f32[16,19,1,128]{3,2,1,0:T(1,128)S(1)} %get-tuple-element.27), channel_id=1, replica_groups=mesh['z'=4,'core'=2,'by'=4] {'z','by'}, dimensions={0} | all-to-all | bytes 311296 | tf_op jit(solution)/shard_map/all_to_all | solution.py:424
  28.4 0.0 collective-permute-start.4
  28.4 1.4 %collective-permute-done.4 = f32[16,19,1,128]{3,2,1,0:T(1,128)S(1)} collective-permute-done((f32[16,19,1,128]{3,2,1,0:T(1,128)S(1)}, f32[16,19,1,128]{3,2,1,0:T(1,128)S(1)}, u32[]{:S(2)}, u32[]{:S(2)}) %collective-permute-start.4) | collective-permute-done | bytes 155680 | tf_op jit(solution)/shard_map/ppermute | solution.py:425
  29.8 2.6 %shard_map.78 = (f32[2,20,8,128]{3,2,1,0:T(8,128)}, f32[8,128]{1,0:T(8,128)}) custom-call(f32[304,128]{1,0:T(8,128)S(1)} %bitcast.2, f32[304,128]{1,0:T(8,128)S(1)} %bitcast.3, f32[2,20,8,128]{3,2,1,0:T(8,128)S(1)} %get-tuple-element.28.refs_2_, s32[8,128]{1,0:T(8,128)S(1)} %get-tuple-element.19.wet.refs_3_), custom_call_target="tpu_custom_call" | custom-call | tf_op jit(solution)/shard_map/pallas_call | solution.py:432
  (1 shorter events, 0.0 us)
Async XLA Ops:
  1.9 10.1 %collective-permute-start.2 = (f32[8,128]{1,0:T(8,128)S(1)}, f32[8,128]{1,0:T(8,128)S(1)}, u32[]{:S(2)}, u32[]{:S(2)}) collective-permute-start(f32[8,128]{1,0:T(8,128)S(1)} %get-tuple-element.24), channel_id=1, source_target_pairs={{1,2},{2,1},{5,6},{6,5},{9,10},{10,9},{13,14},{14,13},{17,18},{18,... | collective-permute-start | bytes 12296 | tf_op jit(solution)/shard_map/ppermute | solution.py:402
  2.6 9.5 %collective-permute-start.3 = (f32[8,128]{1,0:T(8,128)S(1)}, f32[8,128]{1,0:T(8,128)S(1)}, u32[]{:S(2)}, u32[]{:S(2)}) collective-permute-start(f32[8,128]{1,0:T(8,128)S(1)} %get-tuple-element.25), channel_id=1, source_target_pairs={{0,1},{2,3},{1,0},{3,2},{4,5},{6,7},{5,4},{7,6},{8,9},{10,11},{9,8... | collective-permute-start | bytes 12296 | tf_op jit(solution)/shard_map/ppermute | solution.py:402
  8.3 3.7 %collective-permute-start = (f32[81,128]{1,0:T(8,128)S(1)}, f32[81,128]{1,0:T(8,128)S(1)}, u32[]{:S(2)}, u32[]{:S(2)}) collective-permute-start(f32[81,128]{1,0:T(8,128)S(1)} %get-tuple-element.22), channel_id=1, source_target_pairs={{4,8},{12,16},{20,24},{8,4},{16,12},{24,20},{5,9},{13,17},{21,25},... | collective-permute-start | bytes 124424 | tf_op jit(solution)/shard_map/ppermute | solution.py:402
  9.0 3.9 %collective-permute-start.1 = (f32[81,128]{1,0:T(8,128)S(1)}, f32[81,128]{1,0:T(8,128)S(1)}, u32[]{:S(2)}, u32[]{:S(2)}) collective-permute-start(f32[81,128]{1,0:T(8,128)S(1)} %get-tuple-element.23), channel_id=1, source_target_pairs={{0,4},{8,12},{16,20},{24,28},{4,0},{12,8},{20,16},{28,24},{1,5},{9... | collective-permute-start | bytes 124424 | tf_op jit(solution)/shard_map/ppermute | solution.py:402
  28.4 1.4 %collective-permute-start.4 = (f32[16,19,1,128]{3,2,1,0:T(1,128)S(1)}, f32[16,19,1,128]{3,2,1,0:T(1,128)S(1)}, u32[]{:S(2)}, u32[]{:S(2)}) collective-permute-start(f32[16,19,1,128]{3,2,1,0:T(1,128)S(1)} %all_to_all.5), channel_id=1, source_target_pairs={{0,4},{4,0},{1,5},{5,1},{2,6},{6,2},{3,7},{7,3},{8,12},{12,8},{9,1... | collective-permute-start | bytes 466952 | tf_op jit(solution)/shard_map/ppermute | solution.py:425

commit v7 on v6

--- a/solution.py
+++ b/solution.py
@@ -36,7 +36,7 @@
 
 def pack_rims(
     tracers_in, velocity_in, wet_in, diagonal_in, thickness_in,
-    rows_a, rows_b, cols_a, cols_b, tracers, velocity, wet, diagonal, weights,
+    rows_a, rows_b, cols, tracers, velocity, wet, diagonal, weights,
     thickness, semaphores,
 ):
     levels, cols_x, rows_y = tracers.shape[1:]
@@ -53,7 +53,7 @@
     ]
     for copy in copies:
         copy.start()
-    even_x, even_y = (lax.axis_index("core") == 0, lax.axis_index("by") % 2 == 0)
+    even_x = lax.axis_index("core") == 0
     lane = lanes_of((cols_x, rows_y))
     for copy in copies:
         copy.wait()
@@ -72,12 +72,13 @@
         rows_b[index : index + 1, :] = jnp.where(even_x, top, bottom)
         first = jnp.where(lane == index, tile[:, 0:1], first)
         last = jnp.where(lane == index, tile[:, rows_y - 1 : rows_y], last)
-    cols_a[...] = jnp.where(even_y, last, first)
-    cols_b[...] = jnp.where(even_y, first, last)
+    own_y = lax.axis_index("by")
+    for target in range(cols.shape[0]):
+        cols[target] = jnp.where(target > own_y, last, first)
 
 
 def level_kernel(
-    tracers, velocity, wet, diagonal, weights, latitude, rows_b, rows_a, cols_b, cols_a,
+    tracers, velocity, wet, diagonal, weights, latitude, rows_b, rows_a, cols,
     new_tracers, moved_velocity, surface,
     next_tracers, gradients, semaphore,
 ):
@@ -86,9 +87,9 @@
     lane, sublane = (lanes_of(shape), sublanes_of(shape))
     low_x, high_x = (sublane == 0, sublane == cols_x - 1)
     low_y, high_y = (lane == 0, lane == rows_y - 1)
-    even_x, even_y = (lax.axis_index("core") == 0, lax.axis_index("by") % 2 == 0)
-    after_cols = jnp.where(even_y, cols_a[...], cols_b[...])
-    before_cols = jnp.where(even_y, cols_b[...], cols_a[...])
+    even_x, own_y, blocks_y = (lax.axis_index("core") == 0, lax.axis_index("by"), cols.shape[0])
+    after_cols = jnp.where(own_y < blocks_y - 1, cols[jnp.minimum(own_y + 1, blocks_y - 1)], 0.0)
+    before_cols = jnp.where(own_y > 0, cols[jnp.maximum(own_y - 1, 0)], 0.0)
 
     def neighbours(tile, index):
         row_a, row_b = (rows_a[index : index + 1, :], rows_b[index : index + 1, :])
@@ -174,7 +175,7 @@
 
 
 def solve_kernel(
-    blocks_x, blocks_y, gathered, swapped, moved_velocity, wet,
+    blocks_x, blocks_y, gathered, moved_velocity, wet,
     new_velocity, pressure,
     residual, inverses, lifted_0, lifted_1, smooth_0, smooth_1, smooth_2, image_0, direction_1,
 ):
@@ -227,14 +228,10 @@
 
     height = 2 * cols_x + 3
 
-    def start_from(by_core):
+    def start_all():
         def rows_of(row, column, first, count):
-            if isinstance(row, int):
-                place = (row // 2 * blocks_y + column) * height + first
-                return by_core[row % 2][place : place + count, :]
-            place = (row // 2 * blocks_y + column) * height + first
-            found = [blocks[pl.ds(place, count), :] for blocks in by_core]
-            return jnp.where(row % 2 == 0, *found)
+            place = (column * blocks_x + row) * height + first
+            return gathered[pl.ds(place, count), :]
 
         def edge_row(which, row, column):
             if isinstance(row, int):
@@ -289,9 +286,7 @@
         inner, curvature = each_row(step, (zero, zero))
         return total(inner), total(curvature)
 
-    own_core = lax.axis_index("core")
-    pl.when(own_core == 0)(lambda: start_from((gathered, swapped)))
-    pl.when(own_core == 1)(lambda: start_from((swapped, gathered)))
+    start_all()
     inner_0, curvature_0 = operate(lifted_0, smooth_0, image_0)
     step_0 = inner_0 / curvature_0
 
@@ -382,27 +377,25 @@
         return pltpu.with_memory_space_constraint(array, pltpu.VMEM)
 
     fields = (tracers, velocity, wet_levels, diagonal, thickness)
-    rows_a, rows_b, cols_a, cols_b, *block = pl.pallas_call(
+    rows_a, rows_b, cols, *block = pl.pallas_call(
         pack_rims,
         out_shape=[
-            held(rim_rows, rows_y), held(rim_rows, rows_y), held(*shape), held(*shape),
+            held(rim_rows, rows_y), held(rim_rows, rows_y), held(blocks_y, *shape),
             held(*tracers.shape), held(*velocity.shape), pltpu.VMEM(shape, wet_levels.dtype),
             held(*shape), held(levels, rows_y),
         ],
         in_specs=[ANY] * 5,
-        out_specs=[VMEM] * 9,
+        out_specs=[VMEM] * 8,
         scratch_shapes=[pltpu.SMEM(thickness.shape, jnp.float32), pltpu.SemaphoreType.DMA((5,))],
     )(*(pltpu.with_memory_space_constraint(array, pltpu.HBM) for array in fields))
     block = [kept(array) for array in block]
 
-    def exchange(message, axis, first):
-        size = blocks_x if axis == "bx" else blocks_y
-        pairs = [(i, i + 1) for i in range(first, size - 1, 2)]
-        axes = ("z", "core") if axis == "bx" else axis
-        return lax.ppermute(message, axes, pairs + [(j, i) for i, j in pairs])
-
-    rows_b, rows_a = (exchange(rows_b, "bx", 1), exchange(rows_a, "bx", 0))
-    cols_b, cols_a = (exchange(cols_b, "by", 1), exchange(cols_a, "by", 0))
+    def exchange(message, first):
+        pairs = [(i, i + 1) for i in range(first, blocks_x - 1, 2)]
+        return lax.ppermute(message, ("z", "core"), pairs + [(j, i) for i, j in pairs])
+
+    cols = lax.all_to_all(cols, "by", split_axis=0, concat_axis=0, tiled=True)
+    rows_b, rows_a = (exchange(rows_b, 1), exchange(rows_a, 0))
     positions = (lax.axis_index("by") * rows_y + jnp.arange(rows_y, dtype=jnp.int32)).astype(jnp.float32)
     latitude = latitude_rate(positions, blocks_y * rows_y)[None]
 
@@ -410,20 +403,19 @@
         level_kernel,
         out_shape=[
             like(*tracers.shape), held(*velocity.shape),
-            held(chips_z * blocks_y, height, 1, rows_y),
+            held(blocks_x, height, 1, rows_y),
         ],
-        in_specs=[VMEM] * 10,
+        in_specs=[VMEM] * 9,
         out_specs=[ANY, VMEM, VMEM],
         scratch_shapes=[
             pltpu.VMEM(tracers.shape, jnp.float32),
             pltpu.VMEM((2, levels, *shape), jnp.float32),
             pltpu.SemaphoreType.DMA,
         ],
-    )(*block, kept(latitude), kept(rows_b), kept(rows_a), kept(cols_b), kept(cols_a))
-
-    gathered = lax.all_to_all(surface, ("z", "by"), split_axis=0, concat_axis=0, tiled=True)
-    swapped = lax.ppermute(gathered, "core", [(0, 1), (1, 0)])
-    gathered, swapped = (array.reshape(-1, rows_y) for array in (gathered, swapped))
+    )(*block, kept(latitude), kept(rows_b), kept(rows_a), kept(cols))
+
+    gathered = lax.all_to_all(surface, ("z", "core"), split_axis=0, concat_axis=0, tiled=True)
+    gathered = lax.all_gather(gathered, "by", axis=0, tiled=True).reshape(-1, rows_y)
 
     def solve(*refs):
         solve_kernel(blocks_x, blocks_y, *refs)
@@ -432,11 +424,11 @@
     new_velocity, pressure = pl.pallas_call(
         solve,
         out_shape=[like(*velocity.shape), like(*shape)],
-        in_specs=[VMEM] * 4,
+        in_specs=[VMEM] * 3,
         out_specs=[VMEM] * 2,
         scratch_shapes=[pltpu.VMEM((blocks, *shape), jnp.float32)] * 9,
         compiler_params=pltpu.CompilerParams(vmem_limit_bytes=(4 + 52 * blocks // 1024) * 2**20),
-    )(kept(gathered), kept(swapped), kept(moved_velocity), block[2])
+    )(kept(gathered), kept(moved_velocity), block[2])
     return new_tracers, new_velocity, pressure
 
 

time: 32.5 us -> 36.9 us (1.14)
  blocking collectives: 14.4 us -> 21.1 us
  starting transfers between devices: 10.1 us -> 8.83 us
  waiting for transfers between devices: 2.18 us -> 1.01 us
    all_gather x0 -> x1, blocking collectives: none -> 9.75 us  [body(): lax.all_gather(gathered, 'by', axis=0, tiled=True).reshape(-1, rows_y)]
    ppermute x5 -> x2, starting transfers between devices: 10.1 us -> 3.65 us  [exchange(): lax.ppermute(message, ('z', 'core'), pairs + [(j, i) for i, j in pairs])]
    all_to_all x0 -> x1, starting transfers between devices: none -> 5.18 us  [body(): cols = lax.all_to_all(cols, 'by', split_axis=0, concat_axis=0, tiled=True)]
    all_to_all x1, blocking collectives: 14.4 us -> 11.4 us  [body(): lax.all_to_all(surface, ('z', 'core'), split_axis=0, concat_axis=0, tiled...]
    ppermute x5 -> x2, waiting for transfers between devices: 2.18 us -> 0.01 us  [exchange(): lax.ppermute(message, ('z', 'core'), pairs + [(j, i) for i, j in pairs])]
    all_to_all x0 -> x1, waiting for transfers between devices: none -> 1 us  [body(): cols = lax.all_to_all(cols, 'by', split_axis=0, concat_axis=0, tiled=True)]
    pallas_call x1, Pallas kernels: 1.29 us -> 1.9 us  [body(): pl.pallas_call(pack_rims, out_shape=[held(rim_rows, rows_y), held(rim_row...]
    pallas_call x1, Pallas kernels: 2.56 us -> 1.97 us  [body(): pl.pallas_call(solve, out_shape=[like(*velocity.shape), like(*shape)], in...]
  transfers between devices with their start and end apart: 5 -> 3, of which waited for: 2 -> 1; matrix products, arithmetic and copies ran while one was open for 0% -> 0% of each run, Pallas kernels for 0% -> 0%
where the time goes in v7:
time: 36.9 us; the launch traced here: 36.6 us
  blocking collectives  21.1 us (57%)
  starting transfers between devices  8.83 us (24%)
  Pallas kernels  4.93 us (13%)
  waiting for transfers between devices  1.01 us (3%)
  between operations  0.66 us (2%)
    all_to_all x1, blocking collectives, body(): lax.all_to_all(surface, ('z', 'core'), split_axis=0, concat_axis=0, tiled...  11.4 us
    all_gather x1, blocking collectives, body(): lax.all_gather(gathered, 'by', axis=0, tiled=True).reshape(-1, rows_y)  9.75 us
    all_to_all x1, starting transfers between devices, body(): cols = lax.all_to_all(cols, 'by', split_axis=0, concat_axis=0, tiled=True)  5.18 us
    ppermute x2, starting transfers between devices, exchange(): lax.ppermute(message, ('z', 'core'), pairs + [(j, i) for i, j in pairs])  3.65 us
    pallas_call x1, Pallas kernels, body(): pl.pallas_call(solve, out_shape=[like(*velocity.shape), like(*shape)], in...  1.97 us
    pallas_call x1, Pallas kernels, body(): pl.pallas_call(pack_rims, out_shape=[held(rim_rows, rows_y), held(rim_row...  1.9 us
    pallas_call x1, Pallas kernels, body(): pl.pallas_call(level_kernel, out_shape=[like(*tracers.shape), held(*veloc...  1.06 us
    all_to_all x1, waiting for transfers between devices, body(): cols = lax.all_to_all(cols, 'by', split_axis=0, concat_axis=0, tiled=True)  1 us
  transfers between devices with their start and end apart: 3, of which 1 were waited for; matrix products, arithmetic and copies ran while one was open for 0% of the time, Pallas kernels for 0%

profile of v7, /device:TPU:0, one launch (start us, length us, event | category | flops | bytes accessed | tf_op | source)
XLA Modules:
  0.0 36.6 jit_solution(7938489813446724354)
XLA Ops:
  0.6 1.9 %shard_map.76 = (f32[81,128]{1,0:T(8,128)S(1)}, f32[81,128]{1,0:T(8,128)S(1)}, f32[4,8,128]{2,1,0:T(8,128)}, f32[2,20,8,128]{3,2,1,0:T(8,128)S(1)}, f32[2,20,8,1...) custom-call(f32[2,20,8,128]{3,2,1,0:T(8,128)} %tracers_in.1, ...), custom_call_target="tpu_custom_call" | custom-call | tf_op jit(solution)/shard_map/pallas_call | solution.py:380
  2.5 5.2 %all-to-all-start = ((f32[4,8,128]{2,1,0:T(8,128)}), f32[4,8,128]{2,1,0:T(8,128)S(1)}, u32[]{:S(2)}, u32[]{:S(2)}) async-start(f32[4,8,128]{2,1,0:T(8,128)} %get-tuple-element.23), calls=%async_computation | async-start | bytes 32768 | tf_op jit(solution)/shard_map/all_to_all | solution.py:397
  7.7 0.7 %collective-permute-start = (f32[81,128]{1,0:T(8,128)S(1)}, f32[81,128]{1,0:T(8,128)S(1)}, u32[]{:S(2)}, u32[]{:S(2)}) collective-permute-start(f32[81,128]{1,0:T(8,128)S(1)} %get-tuple-element.21), channel_id=1, source_target_pairs={{4,8},{12,16},{20,24},{8,4},{16,12},{24,20},{5,9},{13,17},{21,25},... | collective-permute-start | bytes 124424 | tf_op jit(solution)/shard_map/ppermute | solution.py:395
  8.4 3.0 %collective-permute-start.1 = (f32[81,128]{1,0:T(8,128)S(1)}, f32[81,128]{1,0:T(8,128)S(1)}, u32[]{:S(2)}, u32[]{:S(2)}) collective-permute-start(f32[81,128]{1,0:T(8,128)S(1)} %get-tuple-element.22), channel_id=1, source_target_pairs={{0,4},{8,12},{16,20},{24,28},{4,0},{12,8},{20,16},{28,24},{1,5},{9... | collective-permute-start | bytes 124424 | tf_op jit(solution)/shard_map/ppermute | solution.py:395
  11.4 1.0 %all-to-all-done.cols = f32[4,8,128]{2,1,0:T(8,128)S(1)} async-done(((f32[4,8,128]{2,1,0:T(8,128)}), f32[4,8,128]{2,1,0:T(8,128)S(1)}, u32[]{:S(2)}, u32[]{:S(2)}) %all-to-all-start) | async-done | bytes 16416 | tf_op jit(solution)/shard_map/all_to_all | solution.py:397
  12.4 0.0 collective-permute-done.rows_b
  12.4 0.0 collective-permute-done.1.rows_a
  12.4 1.1 %shard_map.77 = (f32[2,20,8,128]{3,2,1,0:T(8,128)}, f32[2,20,8,128]{3,2,1,0:T(8,128)S(1)}, f32[8,19,1,128]{3,2,1,0:T(1,128)S(1)}) custom-call(f32[2,20,8,128]{3,2,1,0:T(8,128)S(1)} %get-tuple-element.16.tracers, f32[2,20,8,128]{3,2,1,0:T(8,128)S(1)} %get-tuple-element.17.velocity, s32[8,128]{1,0:T(8,128)S(1)} %get-tuple-element.18.wet.refs_2_, ...), custom_call_target="tpu_custom_call" | custom-call | tf_op jit(solution)/shard_map/pallas_call | solution.py:402
  13.5 11.4 %all_to_all.10 = f32[8,19,1,128]{3,2,1,0:T(1,128)S(1)} all-to-all(f32[8,19,1,128]{3,2,1,0:T(1,128)S(1)} %get-tuple-element.25), channel_id=1, replica_groups=mesh['z'=4,'core'=2,'by'=4] {'z','core'}, dimensions={0} | all-to-all | bytes 155648 | tf_op jit(solution)/shard_map/all_to_all | solution.py:417
  24.9 9.8 %all_gather.3 = f32[32,19,1,128]{3,2,1,0:T(1,128)S(1)} all-gather(f32[8,19,1,128]{3,2,1,0:T(1,128)S(1)} %all_to_all.10), channel_id=1, replica_groups=mesh['z'=4,'core'=2,'by'=4] {'by'}, dimensions={0}, use_global_device_ids=true | all-gather | bytes 389120 | tf_op jit(solution)/shard_map/all_gather | solution.py:418
  34.6 2.0 %shard_map.78 = (f32[2,20,8,128]{3,2,1,0:T(8,128)}, f32[8,128]{1,0:T(8,128)}) custom-call(f32[608,128]{1,0:T(8,128)S(1)} %bitcast.1, f32[2,20,8,128]{3,2,1,0:T(8,128)S(1)} %get-tuple-element.26.refs_1_, s32[8,128]{1,0:T(8,128)S(1)} %get-tuple-element.18.wet.refs_2_), custom_call_target="tpu_custom_call" | custom-call | tf_op jit(solution)/shard_map/pallas_call | solution.py:424
  (1 shorter events, 0.0 us)
Async XLA Ops:
  2.5 9.9 %all-to-all-start = ((f32[4,8,128]{2,1,0:T(8,128)}), f32[4,8,128]{2,1,0:T(8,128)S(1)}, u32[]{:S(2)}, u32[]{:S(2)}) async-start(f32[4,8,128]{2,1,0:T(8,128)} %get-tuple-element.23), calls=%async_computation | async-start | bytes 32768 | tf_op jit(solution)/shard_map/all_to_all | solution.py:397
  7.7 4.7 %collective-permute-start = (f32[81,128]{1,0:T(8,128)S(1)}, f32[81,128]{1,0:T(8,128)S(1)}, u32[]{:S(2)}, u32[]{:S(2)}) collective-permute-start(f32[81,128]{1,0:T(8,128)S(1)} %get-tuple-element.21), channel_id=1, source_target_pairs={{4,8},{12,16},{20,24},{8,4},{16,12},{24,20},{5,9},{13,17},{21,25},... | collective-permute-start | bytes 124424 | tf_op jit(solution)/shard_map/ppermute | solution.py:395
  8.4 4.1 %collective-permute-start.1 = (f32[81,128]{1,0:T(8,128)S(1)}, f32[81,128]{1,0:T(8,128)S(1)}, u32[]{:S(2)}, u32[]{:S(2)}) collective-permute-start(f32[81,128]{1,0:T(8,128)S(1)} %get-tuple-element.22), channel_id=1, source_target_pairs={{0,4},{8,12},{16,20},{24,28},{4,0},{12,8},{20,16},{28,24},{1,5},{9... | collective-permute-start | bytes 124424 | tf_op jit(solution)/shard_map/ppermute | solution.py:395

commit v8 on v7

--- a/solution.py
+++ b/solution.py
@@ -36,8 +36,8 @@
 
 def pack_rims(
     tracers_in, velocity_in, wet_in, diagonal_in, thickness_in,
-    rows_a, rows_b, cols, tracers, velocity, wet, diagonal, weights,
-    thickness, semaphores,
+    rows_a, rows_b, early, tracers, velocity, wet, weights,
+    diagonal, thickness, semaphores,
 ):
     levels, cols_x, rows_y = tracers.shape[1:]
     row_start = pl.multiple_of(lax.axis_index("by") * rows_y, rows_y)
@@ -72,13 +72,21 @@
         rows_b[index : index + 1, :] = jnp.where(even_x, top, bottom)
         first = jnp.where(lane == index, tile[:, 0:1], first)
         last = jnp.where(lane == index, tile[:, rows_y - 1 : rows_y], last)
+    inverse = jnp.where(counts > 0, 1.0, 0.0) / (4.0 + diagonal[...])
+    blocks_y = lax.axis_size("by")
     own_y = lax.axis_index("by")
-    for target in range(cols.shape[0]):
-        cols[target] = jnp.where(target > own_y, last, first)
+    sides = [jnp.where(column > own_y, last, first) for column in range(blocks_y)]
+
+    def place(row):
+        for column, side in enumerate(sides):
+            early[row * blocks_y + column, 0:cols_x] = inverse
+            early[row * blocks_y + column, cols_x : 2 * cols_x] = side
+
+    pl.loop(0, early.shape[0] // blocks_y, unroll=8)(place)
 
 
 def level_kernel(
-    tracers, velocity, wet, diagonal, weights, latitude, rows_b, rows_a, cols,
+    tracers, velocity, wet, weights, latitude, rows_b, rows_a, early,
     new_tracers, moved_velocity, surface,
     next_tracers, gradients, semaphore,
 ):
@@ -87,9 +95,13 @@
     lane, sublane = (lanes_of(shape), sublanes_of(shape))
     low_x, high_x = (sublane == 0, sublane == cols_x - 1)
     low_y, high_y = (lane == 0, lane == rows_y - 1)
-    even_x, own_y, blocks_y = (lax.axis_index("core") == 0, lax.axis_index("by"), cols.shape[0])
-    after_cols = jnp.where(own_y < blocks_y - 1, cols[jnp.minimum(own_y + 1, blocks_y - 1)], 0.0)
-    before_cols = jnp.where(own_y > 0, cols[jnp.maximum(own_y - 1, 0)], 0.0)
+    even_x = lax.axis_index("core") == 0
+    own_y, blocks_y = (lax.axis_index("by"), lax.axis_size("by"))
+    own = position_x() * blocks_y + own_y
+    after = jnp.minimum(own + 1, early.shape[0] - 1)
+    before = jnp.maximum(own - 1, 0)
+    after_cols = jnp.where(own_y < blocks_y - 1, early[after, cols_x : 2 * cols_x], 0.0)
+    before_cols = jnp.where(own_y > 0, early[before, cols_x : 2 * cols_x], 0.0)
 
     def neighbours(tile, index):
         row_a, row_b = (rows_a[index : index + 1, :], rows_b[index : index + 1, :])
@@ -150,7 +162,6 @@
         moved_velocity[1, level] = next_merid
         flow_x = flow_x + jnp.where(here, weight * next_zonal, 0.0)
         flow_y = flow_y + jnp.where(here, weight * next_merid, 0.0)
-    inverse = jnp.where(counts > 0, 1.0, 0.0) / (4.0 + diagonal[...])
     ahead = jnp.where(high_x, 0.0, pltpu.roll(flow_x, cols_x - 1, 0))
     behind = jnp.where(low_x, 0.0, pltpu.roll(flow_x, 1, 0))
     slope = ahead - behind
@@ -165,19 +176,18 @@
 
     def place(target):
         surface[target, 0:cols_x, 0, :] = inner
-        surface[target, cols_x : 2 * cols_x, 0, :] = inverse
-        surface[target, 2 * cols_x : 2 * cols_x + 1, 0, :] = edge_x[0:1, :]
-        surface[target, 2 * cols_x + 1 : 2 * cols_x + 2, 0, :] = edge_x[cols_x - 1 : cols_x, :]
-        surface[target, 2 * cols_x + 2 : 2 * cols_x + 3, 0, :] = corner
+        surface[target, cols_x : cols_x + 1, 0, :] = edge_x[0:1, :]
+        surface[target, cols_x + 1 : cols_x + 2, 0, :] = edge_x[cols_x - 1 : cols_x, :]
+        surface[target, cols_x + 2 : cols_x + 3, 0, :] = corner
 
     pl.loop(0, surface.shape[0], unroll=8)(place)
     leaving.wait()
 
 
 def solve_kernel(
-    blocks_x, blocks_y, gathered, moved_velocity, wet,
+    blocks_x, blocks_y, gathered, early, moved_velocity, wet,
     new_velocity, pressure,
-    residual, inverses, lifted_0, lifted_1, smooth_0, smooth_1, smooth_2, image_0, direction_1,
+    residual, lifted_0, lifted_1, smooth_0, smooth_1, smooth_2, image_0, direction_1,
 ):
     levels, cols_x, rows_y = moved_velocity.shape[1:]
     shape = (cols_x, rows_y)
@@ -226,23 +236,23 @@
     def total(values):
         return jnp.sum(values, axis=(0, 1), keepdims=True)
 
-    height = 2 * cols_x + 3
+    height = cols_x + 3
 
     def start_all():
         def rows_of(row, column, first, count):
-            place = (column * blocks_x + row) * height + first
+            place = (row * blocks_y + column) * height + first
             return gathered[pl.ds(place, count), :]
 
         def edge_row(which, row, column):
             if isinstance(row, int):
                 inside = 0 <= row < blocks_x
-                return rows_of(row, column, 2 * cols_x + which, 1) if inside else 0.0
+                return rows_of(row, column, cols_x + which, 1) if inside else 0.0
             inside = jnp.logical_and(row >= 0, row < blocks_x).astype(jnp.float32)
             row = jnp.clip(row, 0, blocks_x - 1)
-            return rows_of(row, column, 2 * cols_x + which, 1) * inside
+            return rows_of(row, column, cols_x + which, 1) * inside
 
         def step(row, carry):
-            corners = [rows_of(row, c, 2 * cols_x + 2, 1) for c in range(blocks_y)]
+            corners = [rows_of(row, c, cols_x + 2, 1) for c in range(blocks_y)]
             filler = [jnp.zeros((1, rows_y), jnp.float32)] * (-blocks_y % 8)
             corners = jnp.transpose(jnp.concatenate(corners + filler, axis=0))
             for column in range(blocks_y):
@@ -256,9 +266,8 @@
                 if column > 0:
                     beyond = corners[cols_x : 2 * cols_x, column - 1 : column]
                     forcing = forcing - jnp.where(low_y, beyond, 0.0)
-                inverse = rows_of(row, column, cols_x, cols_x)
+                inverse = early[index, 0:cols_x]
                 lifted = lift(inverse, forcing)
-                inverses[index] = inverse
                 residual[index] = forcing
                 lifted_0[index] = lifted
                 smooth_0[index] = inverse * lifted
@@ -294,7 +303,7 @@
         for column in range(blocks_y):
             index = row * blocks_y + column
             left = residual[index] - step_0 * image_0[index]
-            inverse = inverses[index]
+            inverse = early[index, 0:cols_x]
             lifted = lift(inverse, left)
             residual[index] = left
             lifted_1[index] = lifted
@@ -312,7 +321,7 @@
             index = row * blocks_y + column
             direction_1[index] = smooth_1[index] + turn_1 * smooth_0[index]
             left = residual[index] - step_1 * (image_1[index] + turn_1 * image_0[index])
-            inverse = inverses[index]
+            inverse = early[index, 0:cols_x]
             lifted = lift(inverse, left)
             residual[index] = left
             lifted_0[index] = lifted
@@ -362,7 +371,8 @@
     chips_z, cores, blocks_y = (lax.axis_size("z"), lax.axis_size("core"), lax.axis_size("by"))
     blocks_x = chips_z * cores
     shape = (cols_x, rows_y)
-    height = 2 * cols_x + 3
+    height = cols_x + 3
+    blocks = blocks_x * blocks_y
     rim_rows = 4 * levels + 1
 
     def like(*dims):
@@ -377,16 +387,16 @@
         return pltpu.with_memory_space_constraint(array, pltpu.VMEM)
 
     fields = (tracers, velocity, wet_levels, diagonal, thickness)
-    rows_a, rows_b, cols, *block = pl.pallas_call(
+    rows_a, rows_b, early, *block = pl.pallas_call(
         pack_rims,
         out_shape=[
-            held(rim_rows, rows_y), held(rim_rows, rows_y), held(blocks_y, *shape),
+            held(rim_rows, rows_y), held(rim_rows, rows_y), held(blocks, 2 * cols_x, rows_y),
             held(*tracers.shape), held(*velocity.shape), pltpu.VMEM(shape, wet_levels.dtype),
-            held(*shape), held(levels, rows_y),
+            held(levels, rows_y),
         ],
         in_specs=[ANY] * 5,
-        out_specs=[VMEM] * 8,
-        scratch_shapes=[pltpu.SMEM(thickness.shape, jnp.float32), pltpu.SemaphoreType.DMA((5,))],
+        out_specs=[VMEM] * 7,
+        scratch_shapes=[pltpu.VMEM(shape, jnp.float32), pltpu.SMEM(thickness.shape, jnp.float32), pltpu.SemaphoreType.DMA((5,))],
     )(*(pltpu.with_memory_space_constraint(array, pltpu.HBM) for array in fields))
     block = [kept(array) for array in block]
 
@@ -394,7 +404,8 @@
         pairs = [(i, i + 1) for i in range(first, blocks_x - 1, 2)]
         return lax.ppermute(message, ("z", "core"), pairs + [(j, i) for i, j in pairs])
 
-    cols = lax.all_to_all(cols, "by", split_axis=0, concat_axis=0, tiled=True)
+    everywhere = ("z", "core", "by")
+    early = lax.all_to_all(early, everywhere, split_axis=0, concat_axis=0, tiled=True)
     rows_b, rows_a = (exchange(rows_b, 1), exchange(rows_a, 0))
     positions = (lax.axis_index("by") * rows_y + jnp.arange(rows_y, dtype=jnp.int32)).astype(jnp.float32)
     latitude = latitude_rate(positions, blocks_y * rows_y)[None]
@@ -403,32 +414,31 @@
         level_kernel,
         out_shape=[
             like(*tracers.shape), held(*velocity.shape),
-            held(blocks_x, height, 1, rows_y),
+            held(blocks, height, 1, rows_y),
         ],
-        in_specs=[VMEM] * 9,
+        in_specs=[VMEM] * 8,
         out_specs=[ANY, VMEM, VMEM],
         scratch_shapes=[
             pltpu.VMEM(tracers.shape, jnp.float32),
             pltpu.VMEM((2, levels, *shape), jnp.float32),
             pltpu.SemaphoreType.DMA,
         ],
-    )(*block, kept(latitude), kept(rows_b), kept(rows_a), kept(cols))
-
-    gathered = lax.all_to_all(surface, ("z", "core"), split_axis=0, concat_axis=0, tiled=True)
-    gathered = lax.all_gather(gathered, "by", axis=0, tiled=True).reshape(-1, rows_y)
+    )(*block, kept(latitude), kept(rows_b), kept(rows_a), kept(early))
+
+    gathered = lax.all_to_all(surface, everywhere, split_axis=0, concat_axis=0, tiled=True)
+    gathered = gathered.reshape(-1, rows_y)
 
     def solve(*refs):
         solve_kernel(blocks_x, blocks_y, *refs)
 
-    blocks = blocks_x * blocks_y
     new_velocity, pressure = pl.pallas_call(
         solve,
         out_shape=[like(*velocity.shape), like(*shape)],
-        in_specs=[VMEM] * 3,
+        in_specs=[VMEM] * 4,
         out_specs=[VMEM] * 2,
-        scratch_shapes=[pltpu.VMEM((blocks, *shape), jnp.float32)] * 9,
+        scratch_shapes=[pltpu.VMEM((blocks, *shape), jnp.float32)] * 8,
         compiler_params=pltpu.CompilerParams(vmem_limit_bytes=(4 + 52 * blocks // 1024) * 2**20),
-    )(kept(gathered), kept(moved_velocity), block[2])
+    )(kept(gathered), kept(early), kept(moved_velocity), block[2])
     return new_tracers, new_velocity, pressure
 
 

time: 36.9 us -> 35.2 us (0.954)
  blocking collectives: 21.1 us -> 11.1 us
  waiting for transfers between devices: 1.01 us -> 7.02 us
  starting transfers between devices: 8.83 us -> 11.2 us
    all_gather x1 -> x0, blocking collectives: 9.75 us -> none  [body(): lax.all_gather(gathered, 'by', axis=0, tiled=True).reshape(-1, rows_y)]
    all_to_all x1, waiting for transfers between devices: 1 us -> 6.2 us  [body(): lax.all_to_all(early, everywhere, split_axis=0, concat_axis=0, tiled=True)]
    all_to_all x1, starting transfers between devices: 5.18 us -> 7.3 us  [body(): lax.all_to_all(early, everywhere, split_axis=0, concat_axis=0, tiled=True)]
    ppermute x2, waiting for transfers between devices: 0.01 us -> 0.82 us  [exchange(): lax.ppermute(message, ('z', 'core'), pairs + [(j, i) for i, j in pairs])]
  transfers between devices with their start and end apart: 3 -> 3, of which waited for: 1 -> 2; matrix products, arithmetic and copies ran while one was open for 0% -> 0% of each run, Pallas kernels for 0% -> 0%
where the time goes in v8:
time: 35.2 us; the launch traced here: 35 us
  starting transfers between devices  11.2 us (32%)
  blocking collectives  11.1 us (32%)
  waiting for transfers between devices  7.02 us (20%)
  Pallas kernels  4.94 us (14%)
  between operations  0.67 us (2%)
    all_to_all x1, blocking collectives, body(): lax.all_to_all(surface, everywhere, split_axis=0, concat_axis=0, tiled=True)  11.1 us
    all_to_all x1, starting transfers between devices, body(): lax.all_to_all(early, everywhere, split_axis=0, concat_axis=0, tiled=True)  7.3 us
    all_to_all x1, waiting for transfers between devices, body(): lax.all_to_all(early, everywhere, split_axis=0, concat_axis=0, tiled=True)  6.2 us
    ppermute x2, starting transfers between devices, exchange(): lax.ppermute(message, ('z', 'core'), pairs + [(j, i) for i, j in pairs])  3.86 us
    pallas_call x1, Pallas kernels, body(): pl.pallas_call(pack_rims, out_shape=[held(rim_rows, rows_y), held(rim_row...  2 us
    pallas_call x1, Pallas kernels, body(): pl.pallas_call(solve, out_shape=[like(*velocity.shape), like(*shape)], in...  1.98 us
    pallas_call x1, Pallas kernels, body(): pl.pallas_call(level_kernel, out_shape=[like(*tracers.shape), held(*veloc...  0.96 us
    ppermute x2, waiting for transfers between devices, exchange(): lax.ppermute(message, ('z', 'core'), pairs + [(j, i) for i, j in pairs])  0.82 us
  transfers between devices with their start and end apart: 3, of which 2 were waited for; matrix products, arithmetic and copies ran while one was open for 0% of the time, Pallas kernels for 0%

profile of v8, /device:TPU:0, one launch (start us, length us, event | category | flops | bytes accessed | tf_op | source)
XLA Modules:
  0.0 35.0 jit_solution(5474526438829575167)
XLA Ops:
  0.6 2.0 %shard_map.76 = (f32[81,128]{1,0:T(8,128)S(1)}, f32[81,128]{1,0:T(8,128)S(1)}, f32[32,16,128]{2,1,0:T(8,128)}, f32[2,20,8,128]{3,2,1,0:T(8,128)S(1)}, f32[2,20,8...) custom-call(f32[2,20,8,128]{3,2,1,0:T(8,128)} %tracers_in.1, f32[2,20,8,128]{3,2,1,0:T(8,128)} %velocity_in.1, ...), custom_call_target="tpu_custom_call" | custom-call | tf_op jit(solution)/shard_map/pallas_call | solution.py:390
  2.6 7.3 %all-to-all-start = ((f32[32,16,128]{2,1,0:T(8,128)}), f32[32,16,128]{2,1,0:T(8,128)S(1)}, u32[]{:S(2)}, u32[]{:S(2)}) async-start(f32[32,16,128]{2,1,0:T(8,128)} %get-tuple-element.21), calls=%async_computation | async-start | bytes 524288 | tf_op jit(solution)/shard_map/all_to_all | solution.py:408
  10.0 0.7 %collective-permute-start = (f32[81,128]{1,0:T(8,128)S(1)}, f32[81,128]{1,0:T(8,128)S(1)}, u32[]{:S(2)}, u32[]{:S(2)}) collective-permute-start(f32[81,128]{1,0:T(8,128)S(1)} %get-tuple-element.19), channel_id=1, source_target_pairs={{4,8},{12,16},{20,24},{8,4},{16,12},{24,20},{5,9},{13,17},{21,25},... | collective-permute-start | bytes 124424 | tf_op jit(solution)/shard_map/ppermute | solution.py:405
  10.6 3.2 %collective-permute-start.1 = (f32[81,128]{1,0:T(8,128)S(1)}, f32[81,128]{1,0:T(8,128)S(1)}, u32[]{:S(2)}, u32[]{:S(2)}) collective-permute-start(f32[81,128]{1,0:T(8,128)S(1)} %get-tuple-element.20), channel_id=1, source_target_pairs={{0,4},{8,12},{16,20},{24,28},{4,0},{12,8},{20,16},{28,24},{1,5},{9... | collective-permute-start | bytes 124424 | tf_op jit(solution)/shard_map/ppermute | solution.py:405
  13.9 0.0 collective-permute-done.rows_b
  13.9 0.8 %collective-permute-done.1.rows_a = f32[81,128]{1,0:T(8,128)S(1)} collective-permute-done((f32[81,128]{1,0:T(8,128)S(1)}, f32[81,128]{1,0:T(8,128)S(1)}, u32[]{:S(2)}, u32[]{:S(2)}) %collective-permute-start.1) | collective-permute-done | bytes 41504 | tf_op jit(solution)/shard_map/ppermute | solution.py:405
  14.7 6.2 %all-to-all-done.early.refs_1_ = f32[32,16,128]{2,1,0:T(8,128)S(1)} async-done(((f32[32,16,128]{2,1,0:T(8,128)}), f32[32,16,128]{2,1,0:T(8,128)S(1)}, u32[]{:S(2)}, u32[]{:S(2)}) %all-to-all-start) | async-done | bytes 262176 | tf_op jit(solution)/shard_map/all_to_all | solution.py:408
  20.9 1.0 %shard_map.77 = (f32[2,20,8,128]{3,2,1,0:T(8,128)}, f32[2,20,8,128]{3,2,1,0:T(8,128)S(1)}, f32[32,11,1,128]{3,2,1,0:T(1,128)S(1)}) custom-call(f32[2,20,8,128]{3,2,1,0:T(8,128)S(1)} %get-tuple-element.15.tracers, f32[2,20,8,128]{3,2,1,0:T(8,128)S(1)} %get-tuple-element.16.velocity, s32[8,128]{1,0:T(8,128)S(1)} %get-tuple-element.17.wet.refs_3_, ...), custom_call_target="tpu_custom_call" | custom-call | tf_op jit(solution)/shard_map/pallas_call | solution.py:413
  21.9 11.1 %all_to_all.10 = f32[32,11,1,128]{3,2,1,0:T(1,128)S(1)} all-to-all(f32[32,11,1,128]{3,2,1,0:T(1,128)S(1)} %get-tuple-element.23), channel_id=1, replica_groups=mesh['z'=4,'core'=2,'by'=4] {'z','core','by'}, dimensions={0} | all-to-all | bytes 360448 | tf_op jit(solution)/shard_map/all_to_all | solution.py:428
  33.0 2.0 %shard_map.78 = (f32[2,20,8,128]{3,2,1,0:T(8,128)}, f32[8,128]{1,0:T(8,128)}) custom-call(f32[352,128]{1,0:T(8,128)S(1)} %bitcast.1, f32[32,16,128]{2,1,0:T(8,128)S(1)} %all-to-all-done.early.refs_1_, f32[2,20,8,128]{3,2,1,0:T(8,128)S(1)} %get-tuple-element.24.refs_2_, s32[8,128]{1,0:T(8,128)S(1)} %get-tuple-element.17.wet.refs_3_), custom_call_target="tpu_custom_call" | custom-call | tf_op jit(solution)/shard_map/pallas_call | solution.py:434
  (1 shorter events, 0.0 us)
Async XLA Ops:
  2.6 18.3 %all-to-all-start = ((f32[32,16,128]{2,1,0:T(8,128)}), f32[32,16,128]{2,1,0:T(8,128)S(1)}, u32[]{:S(2)}, u32[]{:S(2)}) async-start(f32[32,16,128]{2,1,0:T(8,128)} %get-tuple-element.21), calls=%async_computation | async-start | bytes 524288 | tf_op jit(solution)/shard_map/all_to_all | solution.py:408
  10.0 3.9 %collective-permute-start = (f32[81,128]{1,0:T(8,128)S(1)}, f32[81,128]{1,0:T(8,128)S(1)}, u32[]{:S(2)}, u32[]{:S(2)}) collective-permute-start(f32[81,128]{1,0:T(8,128)S(1)} %get-tuple-element.19), channel_id=1, source_target_pairs={{4,8},{12,16},{20,24},{8,4},{16,12},{24,20},{5,9},{13,17},{21,25},... | collective-permute-start | bytes 124424 | tf_op jit(solution)/shard_map/ppermute | solution.py:405
  10.6 4.1 %collective-permute-start.1 = (f32[81,128]{1,0:T(8,128)S(1)}, f32[81,128]{1,0:T(8,128)S(1)}, u32[]{:S(2)}, u32[]{:S(2)}) collective-permute-start(f32[81,128]{1,0:T(8,128)S(1)} %get-tuple-element.20), channel_id=1, source_target_pairs={{0,4},{8,12},{16,20},{24,28},{4,0},{12,8},{20,16},{28,24},{1,5},{9... | collective-permute-start | bytes 124424 | tf_op jit(solution)/shard_map/ppermute | solution.py:405

commit v9 on v6

--- a/solution.py
+++ b/solution.py
@@ -174,7 +174,7 @@
 
 
 def solve_kernel(
-    blocks_x, blocks_y, gathered, swapped, moved_velocity, wet,
+    blocks_x, blocks_y, gathered, moved_velocity, wet,
     new_velocity, pressure,
     residual, inverses, lifted_0, lifted_1, smooth_0, smooth_1, smooth_2, image_0, direction_1,
 ):
@@ -227,14 +227,10 @@
 
     height = 2 * cols_x + 3
 
-    def start_from(by_core):
+    def start_all():
         def rows_of(row, column, first, count):
-            if isinstance(row, int):
-                place = (row // 2 * blocks_y + column) * height + first
-                return by_core[row % 2][place : place + count, :]
-            place = (row // 2 * blocks_y + column) * height + first
-            found = [blocks[pl.ds(place, count), :] for blocks in by_core]
-            return jnp.where(row % 2 == 0, *found)
+            place = (row * blocks_y + column) * height + first
+            return gathered[pl.ds(place, count), :]
 
         def edge_row(which, row, column):
             if isinstance(row, int):
@@ -289,9 +285,7 @@
         inner, curvature = each_row(step, (zero, zero))
         return total(inner), total(curvature)
 
-    own_core = lax.axis_index("core")
-    pl.when(own_core == 0)(lambda: start_from((gathered, swapped)))
-    pl.when(own_core == 1)(lambda: start_from((swapped, gathered)))
+    start_all()
     inner_0, curvature_0 = operate(lifted_0, smooth_0, image_0)
     step_0 = inner_0 / curvature_0
 
@@ -368,6 +362,7 @@
     blocks_x = chips_z * cores
     shape = (cols_x, rows_y)
     height = 2 * cols_x + 3
+    blocks = blocks_x * blocks_y
     rim_rows = 4 * levels + 1
 
     def like(*dims):
@@ -410,7 +405,7 @@
         level_kernel,
         out_shape=[
             like(*tracers.shape), held(*velocity.shape),
-            held(chips_z * blocks_y, height, 1, rows_y),
+            held(blocks, height, 1, rows_y),
         ],
         in_specs=[VMEM] * 10,
         out_specs=[ANY, VMEM, VMEM],
@@ -421,22 +416,20 @@
         ],
     )(*block, kept(latitude), kept(rows_b), kept(rows_a), kept(cols_b), kept(cols_a))
 
-    gathered = lax.all_to_all(surface, ("z", "by"), split_axis=0, concat_axis=0, tiled=True)
-    swapped = lax.ppermute(gathered, "core", [(0, 1), (1, 0)])
-    gathered, swapped = (array.reshape(-1, rows_y) for array in (gathered, swapped))
+    gathered = lax.all_to_all(surface, ("z", "core", "by"), split_axis=0, concat_axis=0, tiled=True)
+    gathered = gathered.reshape(-1, rows_y)
 
     def solve(*refs):
         solve_kernel(blocks_x, blocks_y, *refs)
 
-    blocks = blocks_x * blocks_y
     new_velocity, pressure = pl.pallas_call(
         solve,
         out_shape=[like(*velocity.shape), like(*shape)],
-        in_specs=[VMEM] * 4,
+        in_specs=[VMEM] * 3,
         out_specs=[VMEM] * 2,
         scratch_shapes=[pltpu.VMEM((blocks, *shape), jnp.float32)] * 9,
         compiler_params=pltpu.CompilerParams(vmem_limit_bytes=(4 + 52 * blocks // 1024) * 2**20),
-    )(kept(gathered), kept(swapped), kept(moved_velocity), block[2])
+    )(kept(gathered), kept(moved_velocity), block[2])
     return new_tracers, new_velocity, pressure
 
 

time: 32.5 us -> 33.6 us (1.034)
  blocking collectives: 14.4 us -> 17.4 us
  waiting for transfers between devices: 2.18 us -> 0.8 us
  Pallas kernels: 4.99 us -> 4.4 us
    all_to_all x1, blocking collectives: 14.4 us -> 17.4 us  [body(): lax.all_to_all(surface, ('z', 'core', 'by'), split_axis=0, concat_axis=0,...]
    ppermute x1 -> x0, waiting for transfers between devices: 1.38 us -> none  [body(): swapped = lax.ppermute(gathered, 'core', [(0, 1), (1, 0)])]
    pallas_call x1, Pallas kernels: 2.56 us -> 1.97 us  [body(): pl.pallas_call(solve, out_shape=[like(*velocity.shape), like(*shape)], in...]
  transfers between devices with their start and end apart: 5 -> 4, of which waited for: 2 -> 1; matrix products, arithmetic and copies ran while one was open for 0% -> 0% of each run, Pallas kernels for 0% -> 0%
where the time goes in v9:
time: 33.6 us; the launch traced here: 33.4 us
  blocking collectives  17.4 us (52%)
  starting transfers between devices  10.1 us (30%)
  Pallas kernels  4.4 us (13%)
  waiting for transfers between devices  0.8 us (2%)
  between operations  0.69 us (2%)
    all_to_all x1, blocking collectives, body(): lax.all_to_all(surface, ('z', 'core', 'by'), split_axis=0, concat_axis=0,...  17.4 us
    ppermute x4, starting transfers between devices, exchange(): return lax.ppermute(message, axes, pairs + [(j, i) for i, j in pairs])  10.1 us
    pallas_call x1, Pallas kernels, body(): pl.pallas_call(solve, out_shape=[like(*velocity.shape), like(*shape)], in...  1.97 us
    pallas_call x1, Pallas kernels, body(): pl.pallas_call(pack_rims, out_shape=[held(rim_rows, rows_y), held(rim_row...  1.29 us
    pallas_call x1, Pallas kernels, body(): pl.pallas_call(level_kernel, out_shape=[like(*tracers.shape), held(*veloc...  1.14 us
    ppermute x4, waiting for transfers between devices, exchange(): return lax.ppermute(message, axes, pairs + [(j, i) for i, j in pairs])  0.8 us
  transfers between devices with their start and end apart: 4, of which 1 were waited for; matrix products, arithmetic and copies ran while one was open for 0% of the time, Pallas kernels for 0%

profile of v9, /device:TPU:0, one launch (start us, length us, event | category | flops | bytes accessed | tf_op | source)
XLA Modules:
  0.0 33.4 jit_solution(13785589164065142062)
XLA Ops:
  0.6 1.3 %shard_map.76 = (f32[81,128]{1,0:T(8,128)S(1)}, f32[81,128]{1,0:T(8,128)S(1)}, f32[8,128]{1,0:T(8,128)S(1)}, f32[8,128]{1,0:T(8,128)S(1)}, f32[2,20,8,128]{3,2,1...) custom-call(f32[2,20,8,128]{3,2,1,0:T(8,128)} %tracers_in.1, ...), custom_call_target="tpu_custom_call" | custom-call | tf_op jit(solution)/shard_map/pallas_call | solution.py:380
  1.9 0.7 %collective-permute-start.2 = (f32[8,128]{1,0:T(8,128)S(1)}, f32[8,128]{1,0:T(8,128)S(1)}, u32[]{:S(2)}, u32[]{:S(2)}) collective-permute-start(f32[8,128]{1,0:T(8,128)S(1)} %get-tuple-element.24), channel_id=1, source_target_pairs={{1,2},{2,1},{5,6},{6,5},{9,10},{10,9},{13,14},{14,13},{17,18},{18,... | collective-permute-start | bytes 12296 | tf_op jit(solution)/shard_map/ppermute | solution.py:397
  2.6 5.7 %collective-permute-start.3 = (f32[8,128]{1,0:T(8,128)S(1)}, f32[8,128]{1,0:T(8,128)S(1)}, u32[]{:S(2)}, u32[]{:S(2)}) collective-permute-start(f32[8,128]{1,0:T(8,128)S(1)} %get-tuple-element.25), channel_id=1, source_target_pairs={{0,1},{2,3},{1,0},{3,2},{4,5},{6,7},{5,4},{7,6},{8,9},{10,11},{9,8... | collective-permute-start | bytes 12296 | tf_op jit(solution)/shard_map/ppermute | solution.py:397
  8.3 0.7 %collective-permute-start = (f32[81,128]{1,0:T(8,128)S(1)}, f32[81,128]{1,0:T(8,128)S(1)}, u32[]{:S(2)}, u32[]{:S(2)}) collective-permute-start(f32[81,128]{1,0:T(8,128)S(1)} %get-tuple-element.22), channel_id=1, source_target_pairs={{4,8},{12,16},{20,24},{8,4},{16,12},{24,20},{5,9},{13,17},{21,25},... | collective-permute-start | bytes 124424 | tf_op jit(solution)/shard_map/ppermute | solution.py:397
  9.0 3.0 %collective-permute-start.1 = (f32[81,128]{1,0:T(8,128)S(1)}, f32[81,128]{1,0:T(8,128)S(1)}, u32[]{:S(2)}, u32[]{:S(2)}) collective-permute-start(f32[81,128]{1,0:T(8,128)S(1)} %get-tuple-element.23), channel_id=1, source_target_pairs={{0,4},{8,12},{16,20},{24,28},{4,0},{12,8},{20,16},{28,24},{1,5},{9... | collective-permute-start | bytes 124424 | tf_op jit(solution)/shard_map/ppermute | solution.py:397
  12.1 0.0 collective-permute-done.2.cols_b
  12.1 0.0 collective-permute-done.3.cols_a
  12.1 0.0 collective-permute-done.rows_b
  12.1 0.8 %collective-permute-done.1.rows_a = f32[81,128]{1,0:T(8,128)S(1)} collective-permute-done((f32[81,128]{1,0:T(8,128)S(1)}, f32[81,128]{1,0:T(8,128)S(1)}, u32[]{:S(2)}, u32[]{:S(2)}) %collective-permute-start.1) | collective-permute-done | bytes 41504 | tf_op jit(solution)/shard_map/ppermute | solution.py:397
  12.9 1.1 %shard_map.77 = (f32[2,20,8,128]{3,2,1,0:T(8,128)}, f32[2,20,8,128]{3,2,1,0:T(8,128)S(1)}, f32[32,19,1,128]{3,2,1,0:T(1,128)S(1)}) custom-call(f32[2,20,8,128]{3,2,1,0:T(8,128)S(1)} %get-tuple-element.17.tracers, f32[2,20,8,128]{3,2,1,0:T(8,128)S(1)} %get-tuple-element.18.velocity, s32[8,128]{1,0:T(8,128)S(1)} %get-tuple-element.19.wet.refs_2_, ...), custom_call_target="tpu_custom_call" | custom-call | tf_op jit(solution)/shard_map/pallas_call | solution.py:404
  14.0 17.4 %all_to_all.5 = f32[32,19,1,128]{3,2,1,0:T(1,128)S(1)} all-to-all(f32[32,19,1,128]{3,2,1,0:T(1,128)S(1)} %get-tuple-element.27), channel_id=1, replica_groups=mesh['z'=4,'core'=2,'by'=4] {'z','core','by'}, dimensions={0} | all-to-all | bytes 622592 | tf_op jit(solution)/shard_map/all_to_all | solution.py:419
  31.4 2.0 %shard_map.78 = (f32[2,20,8,128]{3,2,1,0:T(8,128)}, f32[8,128]{1,0:T(8,128)}) custom-call(f32[608,128]{1,0:T(8,128)S(1)} %bitcast.1, f32[2,20,8,128]{3,2,1,0:T(8,128)S(1)} %get-tuple-element.28.refs_1_, s32[8,128]{1,0:T(8,128)S(1)} %get-tuple-element.19.wet.refs_2_), custom_call_target="tpu_custom_call" | custom-call | tf_op jit(solution)/shard_map/pallas_call | solution.py:425
  (1 shorter events, 0.0 us)
Async XLA Ops:
  1.9 10.1 %collective-permute-start.2 = (f32[8,128]{1,0:T(8,128)S(1)}, f32[8,128]{1,0:T(8,128)S(1)}, u32[]{:S(2)}, u32[]{:S(2)}) collective-permute-start(f32[8,128]{1,0:T(8,128)S(1)} %get-tuple-element.24), channel_id=1, source_target_pairs={{1,2},{2,1},{5,6},{6,5},{9,10},{10,9},{13,14},{14,13},{17,18},{18,... | collective-permute-start | bytes 12296 | tf_op jit(solution)/shard_map/ppermute | solution.py:397
  2.6 9.5 %collective-permute-start.3 = (f32[8,128]{1,0:T(8,128)S(1)}, f32[8,128]{1,0:T(8,128)S(1)}, u32[]{:S(2)}, u32[]{:S(2)}) collective-permute-start(f32[8,128]{1,0:T(8,128)S(1)} %get-tuple-element.25), channel_id=1, source_target_pairs={{0,1},{2,3},{1,0},{3,2},{4,5},{6,7},{5,4},{7,6},{8,9},{10,11},{9,8... | collective-permute-start | bytes 12296 | tf_op jit(solution)/shard_map/ppermute | solution.py:397
  8.3 3.7 %collective-permute-start = (f32[81,128]{1,0:T(8,128)S(1)}, f32[81,128]{1,0:T(8,128)S(1)}, u32[]{:S(2)}, u32[]{:S(2)}) collective-permute-start(f32[81,128]{1,0:T(8,128)S(1)} %get-tuple-element.22), channel_id=1, source_target_pairs={{4,8},{12,16},{20,24},{8,4},{16,12},{24,20},{5,9},{13,17},{21,25},... | collective-permute-start | bytes 124424 | tf_op jit(solution)/shard_map/ppermute | solution.py:397
  9.0 3.9 %collective-permute-start.1 = (f32[81,128]{1,0:T(8,128)S(1)}, f32[81,128]{1,0:T(8,128)S(1)}, u32[]{:S(2)}, u32[]{:S(2)}) collective-permute-start(f32[81,128]{1,0:T(8,128)S(1)} %get-tuple-element.23), channel_id=1, source_target_pairs={{0,4},{8,12},{16,20},{24,28},{4,0},{12,8},{20,16},{28,24},{1,5},{9... | collective-permute-start | bytes 124424 | tf_op jit(solution)/shard_map/ppermute | solution.py:397

commit v10 on v6

--- a/solution.py
+++ b/solution.py
@@ -76,29 +76,49 @@
     cols_b[...] = jnp.where(even_y, first, last)
 
 
+def edges_of(shape):
+    sublane, lane = (sublanes_of(shape), lanes_of(shape))
+    return sublane == 0, sublane == shape[0] - 1, lane == 0, lane == shape[1] - 1
+
+
+def neighbours_of(tile, after_row, before_row, after_col, before_col):
+    low_x, high_x, low_y, high_y = edges_of(tile.shape)
+    cols_x, rows_y = tile.shape
+    return (
+        jnp.where(high_x, after_row, pltpu.roll(tile, cols_x - 1, 0)),
+        jnp.where(low_x, before_row, pltpu.roll(tile, 1, 0)),
+        jnp.where(high_y, after_col, pltpu.roll(tile, rows_y - 1, 1)),
+        jnp.where(low_y, before_col, pltpu.roll(tile, 1, 1)),
+    )
+
+
+def laplacian(tile, others, shared, level):
+    total = jnp.zeros_like(tile)
+    for other, limit in zip(others, shared):
+        total = total + jnp.where(limit > level, other - tile, 0.0)
+    return total
+
+
+def side_columns(cols_b, cols_a):
+    even_y = lax.axis_index("by") % 2 == 0
+    a, b = (cols_a[...], cols_b[...])
+    return jnp.where(even_y, a, b), jnp.where(even_y, b, a)
+
+
 def level_kernel(
-    tracers, velocity, wet, diagonal, weights, latitude, rows_b, rows_a, cols_b, cols_a,
-    new_tracers, moved_velocity, surface,
-    next_tracers, gradients, semaphore,
+    tracers, velocity, wet, weights, latitude, cols_b, cols_a, rows_a,
+    moved_velocity, flows, inner,
 ):
     levels, cols_x, rows_y = tracers.shape[1:]
     shape = (cols_x, rows_y)
-    lane, sublane = (lanes_of(shape), sublanes_of(shape))
-    low_x, high_x = (sublane == 0, sublane == cols_x - 1)
-    low_y, high_y = (lane == 0, lane == rows_y - 1)
-    even_x, even_y = (lax.axis_index("core") == 0, lax.axis_index("by") % 2 == 0)
-    after_cols = jnp.where(even_y, cols_a[...], cols_b[...])
-    before_cols = jnp.where(even_y, cols_b[...], cols_a[...])
+    even_x = lax.axis_index("core") == 0
+    after_cols, before_cols = side_columns(cols_b, cols_a)
 
     def neighbours(tile, index):
-        row_a, row_b = (rows_a[index : index + 1, :], rows_b[index : index + 1, :])
-        after_row, before_row = (jnp.where(even_x, row_a, row_b), jnp.where(even_x, row_b, row_a))
-        return (
-            jnp.where(high_x, after_row, pltpu.roll(tile, cols_x - 1, 0)),
-            jnp.where(low_x, before_row, pltpu.roll(tile, 1, 0)),
-            jnp.where(high_y, after_cols[:, index : index + 1], pltpu.roll(tile, rows_y - 1, 1)),
-            jnp.where(low_y, before_cols[:, index : index + 1], pltpu.roll(tile, 1, 1)),
-        )
+        row = rows_a[index : index + 1, :]
+        after_row, before_row = (jnp.where(even_x, row, 0.0), jnp.where(even_x, 0.0, row))
+        sides = (after_cols[:, index : index + 1], before_cols[:, index : index + 1])
+        return neighbours_of(tile, after_row, before_row, *sides)
 
     counts = wet[...].astype(jnp.float32)
     around = neighbours(counts, 4 * levels)
@@ -106,56 +126,86 @@
     both_x = jnp.minimum(shared[0], shared[1])
     both_y = jnp.minimum(shared[2], shared[3])
     zero = jnp.zeros(shape, jnp.float32)
-
-    def laplacian(tile, others, level):
-        total = zero
-        for other, limit in zip(others, shared):
-            total = total + jnp.where(limit > level, other - tile, 0.0)
-        return total
-
-    difference_x, difference_y = (zero, zero)
+    coriolis = jnp.broadcast_to(latitude[...], shape)
+    difference_x, difference_y, flow_x, flow_y = (zero, zero, zero, zero)
     for level in range(levels):
+        here = counts > level
         weight = weights[level : level + 1, :]
-        heat, salt = (tracers[0, level], tracers[1, level])
-        heat_around = neighbours(heat, level)
-        salt_around = neighbours(salt, levels + level)
+        heat_around = neighbours(tracers[0, level], level)
+        salt_around = neighbours(tracers[1, level], levels + level)
         loads = [
             jnp.where(count > level, SALINITY_BETA * s - HEAT_ALPHA * t, 0.0)
             for count, s, t in zip(around, salt_around, heat_around)
         ]
         difference_x = difference_x + weight * (loads[0] - loads[1])
         difference_y = difference_y + weight * (loads[2] - loads[3])
-        gradients[0, level] = jnp.where(both_x > level, difference_x * 0.5, 0.0)
-        gradients[1, level] = jnp.where(both_y > level, difference_y * 0.5, 0.0)
-        diffusivity = TIME_INCREMENT * KAPPA_SPREAD
-        next_tracers[0, level] = heat + diffusivity * laplacian(heat, heat_around, level)
-        next_tracers[1, level] = salt + diffusivity * laplacian(salt, salt_around, level)
-    leaving = pltpu.make_async_copy(next_tracers, new_tracers, semaphore)
-    leaving.start()
-
-    coriolis = jnp.broadcast_to(latitude[...], shape)
-    flow_x, flow_y = (zero, zero)
-    for level in range(levels):
-        here = counts > level
-        weight = weights[level : level + 1, :]
+        inner[level : level + 1, :] = jnp.where(
+            even_x, difference_x[0:1, :], difference_x[cols_x - 1 : cols_x, :]
+        )
+        gradient_x = jnp.where(both_x > level, difference_x * 0.5, 0.0)
+        gradient_y = jnp.where(both_y > level, difference_y * 0.5, 0.0)
         zonal, merid = (velocity[0, level], velocity[1, level])
-        spread_x = laplacian(zonal, neighbours(zonal, 2 * levels + level), level)
-        spread_y = laplacian(merid, neighbours(merid, 3 * levels + level), level)
-        zonal_rate = coriolis * merid - gradients[0, level] + VISCOSITY * spread_x
-        merid_rate = -coriolis * zonal - gradients[1, level] + VISCOSITY * spread_y
+        spread_x = laplacian(zonal, neighbours(zonal, 2 * levels + level), shared, level)
+        spread_y = laplacian(merid, neighbours(merid, 3 * levels + level), shared, level)
+        zonal_rate = coriolis * merid - gradient_x + VISCOSITY * spread_x
+        merid_rate = -coriolis * zonal - gradient_y + VISCOSITY * spread_y
         next_zonal = zonal + jnp.where(here, TIME_INCREMENT * zonal_rate, 0.0)
         next_merid = merid + jnp.where(here, TIME_INCREMENT * merid_rate, 0.0)
         moved_velocity[0, level] = next_zonal
         moved_velocity[1, level] = next_merid
         flow_x = flow_x + jnp.where(here, weight * next_zonal, 0.0)
         flow_y = flow_y + jnp.where(here, weight * next_merid, 0.0)
+    flows[0] = flow_x
+    flows[1] = flow_y
+
+
+def edge_kernel(
+    own, across, inner, weights, wet, diagonal, flows,
+    surface, change,
+):
+    levels = weights.shape[0]
+    cols_x, rows_y = shape = wet.shape
+    low_x, high_x, low_y, high_y = edges_of(shape)
+    lane, sublane = (lanes_of(shape), sublanes_of(shape))
+    even_x = lax.axis_index("core") == 0
+    sign = jnp.where(even_x, -1.0, 1.0)
+    counts = wet[...].astype(jnp.float32)
+    within = jnp.where(even_x, counts[1:2, :], counts[cols_x - 2 : cols_x - 1, :])
+    count = across[4 * levels : 4 * levels + 1, :]
+    shared = jnp.minimum(count, own[4 * levels : 4 * levels + 1, :])
+    both = jnp.minimum(shared, within)
+    pressure = jnp.zeros((1, rows_y), jnp.float32)
+    added_x, added_y = (pressure, pressure)
+    for level in range(levels):
+        heat, salt, zonal, merid = (
+            across[field * levels + level : field * levels + level + 1, :] for field in range(4)
+        )
+        own_zonal, own_merid = (
+            own[field * levels + level : field * levels + level + 1, :] for field in (2, 3)
+        )
+        weight = weights[level : level + 1, :]
+        load = jnp.where(count > level, SALINITY_BETA * salt - HEAT_ALPHA * heat, 0.0)
+        pressure = pressure + weight * load
+        slope = (inner[level : level + 1, :] + sign * pressure) * 0.5
+        spread_x = jnp.where(shared > level, zonal - own_zonal, 0.0)
+        spread_y = jnp.where(shared > level, merid - own_merid, 0.0)
+        rate = VISCOSITY * spread_x - jnp.where(both > level, slope, 0.0)
+        change_x = TIME_INCREMENT * rate
+        change_y = (TIME_INCREMENT * VISCOSITY) * spread_y
+        change[0, level : level + 1, :] = change_x
+        change[1, level : level + 1, :] = change_y
+        added_x = added_x + weight * change_x
+        added_y = added_y + weight * change_y
+    edge = sublane == jnp.where(even_x, 0, cols_x - 1)
+    flow_x = flows[0] + jnp.where(edge, added_x, 0.0)
+    flow_y = flows[1] + jnp.where(edge, added_y, 0.0)
     inverse = jnp.where(counts > 0, 1.0, 0.0) / (4.0 + diagonal[...])
     ahead = jnp.where(high_x, 0.0, pltpu.roll(flow_x, cols_x - 1, 0))
     behind = jnp.where(low_x, 0.0, pltpu.roll(flow_x, 1, 0))
     slope = ahead - behind
     ahead = jnp.where(high_y, 0.0, pltpu.roll(flow_y, rows_y - 1, 1))
     behind = jnp.where(low_y, 0.0, pltpu.roll(flow_y, 1, 1))
-    inner = (slope + (ahead - behind)) * 0.5
+    divergence = (slope + (ahead - behind)) * 0.5
     edge_x = flow_x * 0.5
     edge_y = flow_y * 0.5
     first = jnp.where(lane == sublane, edge_y[:, 0:1], 0.0)
@@ -163,20 +213,48 @@
     corner = jnp.sum(first + last, axis=0, keepdims=True)
 
     def place(target):
-        surface[target, 0:cols_x, 0, :] = inner
+        surface[target, 0:cols_x, 0, :] = divergence
         surface[target, cols_x : 2 * cols_x, 0, :] = inverse
         surface[target, 2 * cols_x : 2 * cols_x + 1, 0, :] = edge_x[0:1, :]
         surface[target, 2 * cols_x + 1 : 2 * cols_x + 2, 0, :] = edge_x[cols_x - 1 : cols_x, :]
         surface[target, 2 * cols_x + 2 : 2 * cols_x + 3, 0, :] = corner
 
     pl.loop(0, surface.shape[0], unroll=8)(place)
-    leaving.wait()
+
+
+def tracer_kernel(
+    tracers, wet, moved, change, cols_b, cols_a, rows_b, rows_a, after_gather,
+    new_tracers, moved_velocity,
+):
+    del after_gather
+    levels, cols_x, rows_y = tracers.shape[1:]
+    even_x = lax.axis_index("core") == 0
+    after_cols, before_cols = side_columns(cols_b, cols_a)
+
+    def neighbours(tile, index):
+        row_a, row_b = (rows_a[index : index + 1, :], rows_b[index : index + 1, :])
+        rows = (jnp.where(even_x, row_a, row_b), jnp.where(even_x, row_b, row_a))
+        sides = (after_cols[:, index : index + 1], before_cols[:, index : index + 1])
+        return neighbours_of(tile, *rows, *sides)
+
+    counts = wet[...].astype(jnp.float32)
+    shared = [jnp.minimum(counts, other) for other in neighbours(counts, 4 * levels)]
+    diffusivity = TIME_INCREMENT * KAPPA_SPREAD
+    sublane = sublanes_of((cols_x, rows_y))
+    edge = sublane == jnp.where(even_x, 0, cols_x - 1)
+    for level in range(levels):
+        for part in range(2):
+            tile = tracers[part, level]
+            spread = laplacian(tile, neighbours(tile, part * levels + level), shared, level)
+            new_tracers[part, level] = tile + diffusivity * spread
+            added = jnp.where(edge, change[part, level : level + 1, :], 0.0)
+            moved_velocity[part, level] = moved[part, level] + added
 
 
 def solve_kernel(
     blocks_x, blocks_y, gathered, swapped, moved_velocity, wet,
     new_velocity, pressure,
-    residual, inverses, lifted_0, lifted_1, smooth_0, smooth_1, smooth_2, image_0, direction_1,
+    forcing, edges, residual, inverses, lifted_0, lifted_1, smooth_0, smooth_1, smooth_2, image_0, direction_1,
 ):
     levels, cols_x, rows_y = moved_velocity.shape[1:]
     shape = (cols_x, rows_y)
@@ -185,12 +263,15 @@
     low_y, high_y = (lane == 0, lane == rows_y - 1)
     zero = jnp.zeros(shape, jnp.float32)
 
+    def each(count, step, carry):
+        if blocks_x <= 8:
+            for number in range(count):
+                carry = step(number, carry)
+            return carry
+        return lax.fori_loop(0, count, step, carry)
+
     def each_row(step, carry):
-        if blocks_x <= 8:
-            for row in range(blocks_x):
-                carry = step(row, carry)
-            return carry
-        return lax.fori_loop(0, blocks_x, step, carry)
+        return each(blocks_x, step, carry)
 
     def guarded(load, row, column):
         if isinstance(row, int):
@@ -227,47 +308,43 @@
 
     height = 2 * cols_x + 3
 
-    def start_from(by_core):
-        def rows_of(row, column, first, count):
-            if isinstance(row, int):
-                place = (row // 2 * blocks_y + column) * height + first
-                return by_core[row % 2][place : place + count, :]
-            place = (row // 2 * blocks_y + column) * height + first
-            found = [blocks[pl.ds(place, count), :] for blocks in by_core]
-            return jnp.where(row % 2 == 0, *found)
-
-        def edge_row(which, row, column):
-            if isinstance(row, int):
-                inside = 0 <= row < blocks_x
-                return rows_of(row, column, 2 * cols_x + which, 1) if inside else 0.0
-            inside = jnp.logical_and(row >= 0, row < blocks_x).astype(jnp.float32)
-            row = jnp.clip(row, 0, blocks_x - 1)
-            return rows_of(row, column, 2 * cols_x + which, 1) * inside
-
-        def step(row, carry):
-            corners = [rows_of(row, c, 2 * cols_x + 2, 1) for c in range(blocks_y)]
-            filler = [jnp.zeros((1, rows_y), jnp.float32)] * (-blocks_y % 8)
-            corners = jnp.transpose(jnp.concatenate(corners + filler, axis=0))
-            for column in range(blocks_y):
-                index = row * blocks_y + column
-                forcing = rows_of(row, column, 0, cols_x)
-                forcing = forcing + jnp.where(high_x, edge_row(0, row + 1, column), 0.0)
-                forcing = forcing - jnp.where(low_x, edge_row(1, row - 1, column), 0.0)
-                if column + 1 < blocks_y:
-                    beyond = corners[0:cols_x, column + 1 : column + 2]
-                    forcing = forcing + jnp.where(high_y, beyond, 0.0)
-                if column > 0:
-                    beyond = corners[cols_x : 2 * cols_x, column - 1 : column]
-                    forcing = forcing - jnp.where(low_y, beyond, 0.0)
-                inverse = rows_of(row, column, cols_x, cols_x)
-                lifted = lift(inverse, forcing)
-                inverses[index] = inverse
-                residual[index] = forcing
-                lifted_0[index] = lifted
-                smooth_0[index] = inverse * lifted
-            return carry
-
-        each_row(step, 0)
+    own_core = lax.axis_index("core")
+
+    def unpack(chip, carry):
+        for column in range(blocks_y):
+            place = (chip * blocks_y + column) * height
+            for blocks, core in ((gathered, own_core), (swapped, 1 - own_core)):
+                index = (2 * chip + core) * blocks_y + column
+                forcing[index] = blocks[pl.ds(place, cols_x), :]
+                inverses[index] = blocks[pl.ds(place + cols_x, cols_x), :]
+                edges[index, 0:3] = blocks[pl.ds(place + 2 * cols_x, 3), :]
+        return carry
+
+    each(blocks_x // 2, unpack, 0)
+
+    def edge_row(which, row, column):
+        return guarded(lambda i: edges[i, which : which + 1], row, column)
+
+    def begin(row, carry):
+        corners = [edges[row * blocks_y + c, 2:3] for c in range(blocks_y)]
+        filler = [jnp.zeros((1, rows_y), jnp.float32)] * (-blocks_y % 8)
+        corners = jnp.transpose(jnp.concatenate(corners + filler, axis=0))
+        for column in range(blocks_y):
+            index = row * blocks_y + column
+            whole = forcing[index]
+            whole = whole + jnp.where(high_x, edge_row(0, row + 1, column), 0.0)
+            whole = whole - jnp.where(low_x, edge_row(1, row - 1, column), 0.0)
+            if column + 1 < blocks_y:
+                whole = whole + jnp.where(high_y, corners[0:cols_x, column + 1 : column + 2], 0.0)
+            if column > 0:
+                beyond = corners[cols_x : 2 * cols_x, column - 1 : column]
+                whole = whole - jnp.where(low_y, beyond, 0.0)
+            inverse = inverses[index]
+            lifted = lift(inverse, whole)
+            residual[index] = whole
+            lifted_0[index] = lifted
+            smooth_0[index] = inverse * lifted
+        return carry
 
     def operate(lifted, smooth, image):
         def load(index, rows=slice(None)):
@@ -289,9 +366,7 @@
         inner, curvature = each_row(step, (zero, zero))
         return total(inner), total(curvature)
 
-    own_core = lax.axis_index("core")
-    pl.when(own_core == 0)(lambda: start_from((gathered, swapped)))
-    pl.when(own_core == 1)(lambda: start_from((swapped, gathered)))
+    each_row(begin, 0)
     inner_0, curvature_0 = operate(lifted_0, smooth_0, image_0)
     step_0 = inner_0 / curvature_0
 
@@ -401,28 +476,36 @@
         axes = ("z", "core") if axis == "bx" else axis
         return lax.ppermute(message, axes, pairs + [(j, i) for i, j in pairs])
 
+    sent = rows_b
     rows_b, rows_a = (exchange(rows_b, "bx", 1), exchange(rows_a, "bx", 0))
     cols_b, cols_a = (exchange(cols_b, "by", 1), exchange(cols_a, "by", 0))
     positions = (lax.axis_index("by") * rows_y + jnp.arange(rows_y, dtype=jnp.int32)).astype(jnp.float32)
     latitude = latitude_rate(positions, blocks_y * rows_y)[None]
 
-    new_tracers, moved_velocity, surface = pl.pallas_call(
+    tracers, velocity, wet, diagonal, weights = block
+    sent = kept(sent)
+    rows_a, rows_b, cols_a, cols_b = (kept(array) for array in (rows_a, rows_b, cols_a, cols_b))
+    moved, flows, inner = pl.pallas_call(
         level_kernel,
-        out_shape=[
-            like(*tracers.shape), held(*velocity.shape),
-            held(chips_z * blocks_y, height, 1, rows_y),
-        ],
-        in_specs=[VMEM] * 10,
-        out_specs=[ANY, VMEM, VMEM],
-        scratch_shapes=[
-            pltpu.VMEM(tracers.shape, jnp.float32),
-            pltpu.VMEM((2, levels, *shape), jnp.float32),
-            pltpu.SemaphoreType.DMA,
-        ],
-    )(*block, kept(latitude), kept(rows_b), kept(rows_a), kept(cols_b), kept(cols_a))
+        out_shape=[held(*velocity.shape), held(2, *shape), held(levels, rows_y)],
+        in_specs=[VMEM] * 8,
+        out_specs=[VMEM] * 3,
+    )(tracers, velocity, wet, weights, kept(latitude), cols_b, cols_a, rows_a)
+    surface, change = pl.pallas_call(
+        edge_kernel,
+        out_shape=[held(chips_z * blocks_y, height, 1, rows_y), held(2, levels, rows_y)],
+        in_specs=[VMEM] * 7,
+        out_specs=[VMEM] * 2,
+    )(sent, rows_b, kept(inner), weights, wet, diagonal, kept(flows))
 
     gathered = lax.all_to_all(surface, ("z", "by"), split_axis=0, concat_axis=0, tiled=True)
     swapped = lax.ppermute(gathered, "core", [(0, 1), (1, 0)])
+    new_tracers, moved_velocity = pl.pallas_call(
+        tracer_kernel,
+        out_shape=[like(*tracers.shape), held(*velocity.shape)],
+        in_specs=[VMEM] * 8 + [ANY],
+        out_specs=[VMEM] * 2,
+    )(tracers, wet, kept(moved), kept(change), cols_b, cols_a, rows_b, rows_a, gathered)
     gathered, swapped = (array.reshape(-1, rows_y) for array in (gathered, swapped))
 
     def solve(*refs):
@@ -434,9 +517,9 @@
         out_shape=[like(*velocity.shape), like(*shape)],
         in_specs=[VMEM] * 4,
         out_specs=[VMEM] * 2,
-        scratch_shapes=[pltpu.VMEM((blocks, *shape), jnp.float32)] * 9,
+        scratch_shapes=[pltpu.VMEM((blocks, *shape), jnp.float32)] * 11,
         compiler_params=pltpu.CompilerParams(vmem_limit_bytes=(4 + 52 * blocks // 1024) * 2**20),
-    )(kept(gathered), kept(swapped), kept(moved_velocity), block[2])
+    )(kept(gathered), kept(swapped), kept(moved_velocity), wet)
     return new_tracers, new_velocity, pressure
 
 

time: 32.5 us -> 32.2 us (level)
  starting transfers between devices: 10.1 us -> 7.06 us
  blocking collectives: 14.4 us -> 16.8 us
  local copies, waits for them, and re-layouts: 0 us -> 1.57 us
  waiting for transfers between devices: 2.18 us -> 0.87 us
    ppermute x4, starting transfers between devices: 10.1 us -> 7.06 us  [exchange(): return lax.ppermute(message, axes, pairs + [(j, i) for i, j in pairs])]
    all_to_all x1, blocking collectives: 14.4 us -> 16.8 us  [body(): lax.all_to_all(surface, ('z', 'by'), split_axis=0, concat_axis=0, tiled=T...]
    unnamed x0 -> x4, local copies, waits for them, and re-layouts: none -> 1.57 us
    ppermute x1, waiting for transfers between devices: 1.38 us -> 0.01 us  [body(): swapped = lax.ppermute(gathered, 'core', [(0, 1), (1, 0)])]
    pallas_call x1, Pallas kernels: 2.56 us -> 1.97 us  [body(): pl.pallas_call(solve, out_shape=[like(*velocity.shape), like(*shape)], in...]
    pallas_call x1 -> x3, Pallas kernels: 1.14 us -> 1.62 us  [the longest x1 0.95 us: body(): pl.pallas_call(tracer_kernel, out_shape=[like(*tracers.shape), held(*velo...]
  transfers between devices with their start and end apart: 5 -> 5, of which waited for: 2 -> 1; matrix products, arithmetic and copies ran while one was open for 0% -> 0% of each run, Pallas kernels for 0% -> 4%
where the time goes in v10:
time: 32.2 us; the launch traced here: 32 us
  blocking collectives  16.8 us (52%)
  starting transfers between devices  7.06 us (22%)
  Pallas kernels  4.88 us (15%)
  local copies, waits for them, and re-layouts  1.57 us (5%)
  waiting for transfers between devices  0.87 us (3%)
  between operations  0.69 us (2%)
    all_to_all x1, blocking collectives, body(): lax.all_to_all(surface, ('z', 'by'), split_axis=0, concat_axis=0, tiled=T...  16.8 us
    ppermute x4, starting transfers between devices, exchange(): return lax.ppermute(message, axes, pairs + [(j, i) for i, j in pairs])  7.06 us
    pallas_call x1, Pallas kernels, body(): pl.pallas_call(solve, out_shape=[like(*velocity.shape), like(*shape)], in...  1.97 us
    unnamed x4, local copies, waits for them, and re-layouts  1.57 us
    pallas_call x1, Pallas kernels, body(): pl.pallas_call(pack_rims, out_shape=[held(rim_rows, rows_y), held(rim_row...  1.29 us
    pallas_call x1, Pallas kernels, body(): pl.pallas_call(tracer_kernel, out_shape=[like(*tracers.shape), held(*velo...  0.95 us
    ppermute x4, waiting for transfers between devices, exchange(): return lax.ppermute(message, axes, pairs + [(j, i) for i, j in pairs])  0.87 us
  transfers between devices with their start and end apart: 5, of which 1 were waited for; matrix products, arithmetic and copies ran while one was open for 0% of the time, Pallas kernels for 4%

profile of v10, /device:TPU:0, one launch (start us, length us, event | category | flops | bytes accessed | tf_op | source)
XLA Modules:
  0.0 32.0 jit_solution(10932849041820253473)
XLA Ops:
  0.6 1.3 %shard_map.76 = (f32[81,128]{1,0:T(8,128)S(1)}, f32[81,128]{1,0:T(8,128)S(1)}, f32[8,128]{1,0:T(8,128)S(1)}, f32[8,128]{1,0:T(8,128)S(1)}, f32[2,20,8,128]{3,2,1...) custom-call(f32[2,20,8,128]{3,2,1,0:T(8,128)} %tracers_in.1, ...), custom_call_target="tpu_custom_call" | custom-call | tf_op jit(solution)/shard_map/pallas_call | solution.py:460
  1.9 0.7 %collective-permute-start = (f32[8,128]{1,0:T(8,128)S(1)}, f32[8,128]{1,0:T(8,128)S(1)}, u32[]{:S(2)}, u32[]{:S(2)}) collective-permute-start(f32[8,128]{1,0:T(8,128)S(1)} %get-tuple-element.25), channel_id=1, source_target_pairs={{1,2},{2,1},{5,6},{6,5},{9,10},{10,9},{13,14},{14,13},{17,18},{18,... | collective-permute-start | bytes 12296 | tf_op jit(solution)/shard_map/ppermute | solution.py:477
  2.6 5.7 %collective-permute-start.1 = (f32[8,128]{1,0:T(8,128)S(1)}, f32[8,128]{1,0:T(8,128)S(1)}, u32[]{:S(2)}, u32[]{:S(2)}) collective-permute-start(f32[8,128]{1,0:T(8,128)S(1)} %get-tuple-element.26), channel_id=1, source_target_pairs={{0,1},{2,3},{1,0},{3,2},{4,5},{6,7},{5,4},{7,6},{8,9},{10,11},{9,8... | collective-permute-start | bytes 12296 | tf_op jit(solution)/shard_map/ppermute | solution.py:477
  8.3 0.0 collective-permute-start.2
  8.3 0.7 %collective-permute-start.3 = (f32[81,128]{1,0:T(8,128)S(1)}, f32[81,128]{1,0:T(8,128)S(1)}, u32[]{:S(2)}, u32[]{:S(2)}) collective-permute-start(f32[81,128]{1,0:T(8,128)S(1)} %get-tuple-element.29.own), channel_id=1, source_target_pairs={{4,8},{12,16},{20,24},{8,4},{16,12},{24,20},{5,9},{13,17},{21,25},... | collective-permute-start | bytes 124424 | tf_op jit(solution)/shard_map/ppermute | solution.py:477
  9.1 0.0 collective-permute-done.cols_b
  9.1 0.9 %collective-permute-done.1.cols_a = f32[8,128]{1,0:T(8,128)S(1)} collective-permute-done((f32[8,128]{1,0:T(8,128)S(1)}, f32[8,128]{1,0:T(8,128)S(1)}, u32[]{:S(2)}, u32[]{:S(2)}) %collective-permute-start.1) | collective-permute-done | bytes 4128 | tf_op jit(solution)/shard_map/ppermute | solution.py:477
  9.9 0.0 collective-permute-done.2.rows_a
  9.9 0.5 %shard_map.77 = (f32[2,20,8,128]{3,2,1,0:T(8,128)S(1)}, f32[2,8,128]{2,1,0:T(8,128)S(1)}, f32[20,128]{1,0:T(8,128)S(1)}) custom-call(f32[2,20,8,128]{3,2,1,0:T(8,128)S(1)} %get-tuple-element.21.tracers, f32[2,20,8,128]{3,2,1,0:T(8,128)S(1)} %get-tuple-element.23.velocity, s32[8,128]{1,0:T(8,128)S(1)} %get-tuple-element.22.wet.refs_3_, ...), custom_call_target="tpu_custom_call" | custom-call | tf_op jit(solution)/shard_map/pallas_call | solution.py:488
  10.4 0.0 collective-permute-done.3.across.rows_b
  10.4 0.2 shard_map.78
  10.6 16.8 %all_to_all.5.after_gather = f32[16,19,1,128]{3,2,1,0:T(1,128)S(1)} all-to-all(f32[16,19,1,128]{3,2,1,0:T(1,128)S(1)} %get-tuple-element.34), channel_id=1, replica_groups=mesh['z'=4,'core'=2,'by'=4] {'z','by'}, dimensions={0} | all-to-all | bytes 311296 | tf_op jit(solution)/shard_map/all_to_all | solution.py:501
  27.4 0.0 copy-start
  27.4 0.0 collective-permute-start.4
  27.5 0.7 %copy-done = f32[16,19,1,128]{3,2,1,0:T(1,128)} copy-done((f32[16,19,1,128]{3,2,1,0:T(1,128)}, f32[16,19,1,128]{3,2,1,0:T(1,128)S(1)}, u32[]{:S(2)}) %copy-start) | copy-done | bytes 155672
  28.1 1.0 %shard_map.79 = (f32[2,20,8,128]{3,2,1,0:T(8,128)}, f32[2,20,8,128]{3,2,1,0:T(8,128)S(1)}) custom-call(f32[2,20,8,128]{3,2,1,0:T(8,128)S(1)} %get-tuple-element.21.tracers, s32[8,128]{1,0:T(8,128)S(1)} %get-tuple-element.22.wet.refs_3_, f32[2,20,8,128]{3,2,1,0:T(8,128)S(1)} %get-tuple-element.28.moved, f32[2,20,128]{2,1,0:T(8,128)S(1)} %get-tuple-element.33.change, ...), custom_call_target="tpu_custom_call" | custom-call | tf_op jit(solution)/shard_map/pallas_call | solution.py:503
  29.1 0.0 collective-permute-done.4
  29.1 0.0 copy-start.1
  29.1 0.9 %copy-done.1 = f32[16,19,1,128]{3,2,1,0:T(1,128)S(1)} copy-done((f32[16,19,1,128]{3,2,1,0:T(1,128)S(1)}, f32[16,19,1,128]{3,2,1,0:T(1,128)}, u32[]{:S(2)}) %copy-start.1) | copy-done | bytes 155672
  30.0 2.0 %shard_map.80 = (f32[2,20,8,128]{3,2,1,0:T(8,128)}, f32[8,128]{1,0:T(8,128)}) custom-call(f32[304,128]{1,0:T(8,128)S(1)} %bitcast.2, f32[304,128]{1,0:T(8,128)S(1)} %bitcast.3, f32[2,20,8,128]{3,2,1,0:T(8,128)S(1)} %get-tuple-element.36.refs_2_, s32[8,128]{1,0:T(8,128)S(1)} %get-tuple-element.22.wet.refs_3_), custom_call_target="tpu_custom_call" | custom-call | tf_op jit(solution)/shard_map/pallas_call | solution.py:515
  (1 shorter events, 0.0 us)
Async XLA Ops:
  1.9 7.1 %collective-permute-start = (f32[8,128]{1,0:T(8,128)S(1)}, f32[8,128]{1,0:T(8,128)S(1)}, u32[]{:S(2)}, u32[]{:S(2)}) collective-permute-start(f32[8,128]{1,0:T(8,128)S(1)} %get-tuple-element.25), channel_id=1, source_target_pairs={{1,2},{2,1},{5,6},{6,5},{9,10},{10,9},{13,14},{14,13},{17,18},{18,... | collective-permute-start | bytes 12296 | tf_op jit(solution)/shard_map/ppermute | solution.py:477
  2.6 7.3 %collective-permute-start.1 = (f32[8,128]{1,0:T(8,128)S(1)}, f32[8,128]{1,0:T(8,128)S(1)}, u32[]{:S(2)}, u32[]{:S(2)}) collective-permute-start(f32[8,128]{1,0:T(8,128)S(1)} %get-tuple-element.26), channel_id=1, source_target_pairs={{0,1},{2,3},{1,0},{3,2},{4,5},{6,7},{5,4},{7,6},{8,9},{10,11},{9,8... | collective-permute-start | bytes 12296 | tf_op jit(solution)/shard_map/ppermute | solution.py:477
  8.3 1.6 %collective-permute-start.2 = (f32[81,128]{1,0:T(8,128)S(1)}, f32[81,128]{1,0:T(8,128)S(1)}, u32[]{:S(2)}, u32[]{:S(2)}) collective-permute-start(f32[81,128]{1,0:T(8,128)S(1)} %get-tuple-element.27), channel_id=1, source_target_pairs={{0,4},{8,12},{16,20},{24,28},{4,0},{12,8},{20,16},{28,24},{1,5},{9... | collective-permute-start | bytes 124424 | tf_op jit(solution)/shard_map/ppermute | solution.py:477
  8.3 2.1 %collective-permute-start.3 = (f32[81,128]{1,0:T(8,128)S(1)}, f32[81,128]{1,0:T(8,128)S(1)}, u32[]{:S(2)}, u32[]{:S(2)}) collective-permute-start(f32[81,128]{1,0:T(8,128)S(1)} %get-tuple-element.29.own), channel_id=1, source_target_pairs={{4,8},{12,16},{20,24},{8,4},{16,12},{24,20},{5,9},{13,17},{21,25},... | collective-permute-start | bytes 124424 | tf_op jit(solution)/shard_map/ppermute | solution.py:477
  27.4 0.7 %copy-start = (f32[16,19,1,128]{3,2,1,0:T(1,128)}, f32[16,19,1,128]{3,2,1,0:T(1,128)S(1)}, u32[]{:S(2)}) copy-start(f32[16,19,1,128]{3,2,1,0:T(1,128)S(1)} %all_to_all.5.after_gather) | copy-start | bytes 466948
  27.4 1.6 %collective-permute-start.4 = (f32[16,19,1,128]{3,2,1,0:T(1,128)S(1)}, f32[16,19,1,128]{3,2,1,0:T(1,128)S(1)}, u32[]{:S(2)}, u32[]{:S(2)}) collective-permute-start(f32[16,19,1,128]{3,2,1,0:T(1,128)S(1)} %all_to_all.5.after_gather), channel_id=1, source_target_pairs={{0,4},{4,0},{1,5},{5,1},{2,6},{6,2},{3,7},{7,3},{8,12},{12,8},{9,1... | collective-permute-start | bytes 466952 | tf_op jit(solution)/shard_map/ppermute | solution.py:502
  29.1 0.9 %copy-start.1 = (f32[16,19,1,128]{3,2,1,0:T(1,128)S(1)}, f32[16,19,1,128]{3,2,1,0:T(1,128)}, u32[]{:S(2)}) copy-start(f32[16,19,1,128]{3,2,1,0:T(1,128)} %copy-done) | copy-start | bytes 466948

commit v11 on v10

--- a/solution.py
+++ b/solution.py
@@ -503,9 +503,9 @@
     new_tracers, moved_velocity = pl.pallas_call(
         tracer_kernel,
         out_shape=[like(*tracers.shape), held(*velocity.shape)],
-        in_specs=[VMEM] * 8 + [ANY],
+        in_specs=[VMEM] * 9,
         out_specs=[VMEM] * 2,
-    )(tracers, wet, kept(moved), kept(change), cols_b, cols_a, rows_b, rows_a, gathered)
+    )(tracers, wet, kept(moved), kept(change), cols_b, cols_a, rows_b, rows_a, kept(gathered))
     gathered, swapped = (array.reshape(-1, rows_y) for array in (gathered, swapped))
 
     def solve(*refs):

time: 32.2 us -> 31 us (0.963)
  local copies, waits for them, and re-layouts: 1.57 us -> 0 us
  waiting for transfers between devices: 0.87 us -> 1.3 us
    unnamed x4 -> x0, local copies, waits for them, and re-layouts: 1.57 us -> none
    ppermute x1, waiting for transfers between devices: 0.01 us -> 0.43 us  [body(): swapped = lax.ppermute(gathered, 'core', [(0, 1), (1, 0)])]
  transfers between devices with their start and end apart: 5 -> 5, of which waited for: 1 -> 2; matrix products, arithmetic and copies ran while one was open for 0% -> 0% of each run, Pallas kernels for 4% -> 5%
where the time goes in v11:
time: 31 us; the launch traced here: 30.8 us
  blocking collectives  16.8 us (54%)
  starting transfers between devices  7.06 us (23%)
  Pallas kernels  4.89 us (16%)
  waiting for transfers between devices  1.3 us (4%)
  between operations  0.69 us (2%)
    all_to_all x1, blocking collectives, body(): lax.all_to_all(surface, ('z', 'by'), split_axis=0, concat_axis=0, tiled=T...  16.8 us
    ppermute x4, starting transfers between devices, exchange(): return lax.ppermute(message, axes, pairs + [(j, i) for i, j in pairs])  7.06 us
    pallas_call x1, Pallas kernels, body(): pl.pallas_call(solve, out_shape=[like(*velocity.shape), like(*shape)], in...  1.97 us
    pallas_call x1, Pallas kernels, body(): pl.pallas_call(pack_rims, out_shape=[held(rim_rows, rows_y), held(rim_row...  1.29 us
    pallas_call x1, Pallas kernels, body(): pl.pallas_call(tracer_kernel, out_shape=[like(*tracers.shape), held(*velo...  0.95 us
    ppermute x4, waiting for transfers between devices, exchange(): return lax.ppermute(message, axes, pairs + [(j, i) for i, j in pairs])  0.87 us
  transfers between devices with their start and end apart: 5, of which 2 were waited for; matrix products, arithmetic and copies ran while one was open for 0% of the time, Pallas kernels for 5%

profile of v11, /device:TPU:0, one launch (start us, length us, event | category | flops | bytes accessed | tf_op | source)
XLA Modules:
  0.0 30.8 jit_solution(13958530076932376513)
XLA Ops:
  0.6 1.3 %shard_map.76 = (f32[81,128]{1,0:T(8,128)S(1)}, f32[81,128]{1,0:T(8,128)S(1)}, f32[8,128]{1,0:T(8,128)S(1)}, f32[8,128]{1,0:T(8,128)S(1)}, f32[2,20,8,128]{3,2,1...) custom-call(f32[2,20,8,128]{3,2,1,0:T(8,128)} %tracers_in.1, ...), custom_call_target="tpu_custom_call" | custom-call | tf_op jit(solution)/shard_map/pallas_call | solution.py:460
  1.9 0.7 %collective-permute-start = (f32[8,128]{1,0:T(8,128)S(1)}, f32[8,128]{1,0:T(8,128)S(1)}, u32[]{:S(2)}, u32[]{:S(2)}) collective-permute-start(f32[8,128]{1,0:T(8,128)S(1)} %get-tuple-element.25), channel_id=1, source_target_pairs={{1,2},{2,1},{5,6},{6,5},{9,10},{10,9},{13,14},{14,13},{17,18},{18,... | collective-permute-start | bytes 12296 | tf_op jit(solution)/shard_map/ppermute | solution.py:477
  2.6 5.7 %collective-permute-start.1 = (f32[8,128]{1,0:T(8,128)S(1)}, f32[8,128]{1,0:T(8,128)S(1)}, u32[]{:S(2)}, u32[]{:S(2)}) collective-permute-start(f32[8,128]{1,0:T(8,128)S(1)} %get-tuple-element.26), channel_id=1, source_target_pairs={{0,1},{2,3},{1,0},{3,2},{4,5},{6,7},{5,4},{7,6},{8,9},{10,11},{9,8... | collective-permute-start | bytes 12296 | tf_op jit(solution)/shard_map/ppermute | solution.py:477
  8.3 0.0 collective-permute-start.2
  8.3 0.7 %collective-permute-start.3 = (f32[81,128]{1,0:T(8,128)S(1)}, f32[81,128]{1,0:T(8,128)S(1)}, u32[]{:S(2)}, u32[]{:S(2)}) collective-permute-start(f32[81,128]{1,0:T(8,128)S(1)} %get-tuple-element.29.own), channel_id=1, source_target_pairs={{4,8},{12,16},{20,24},{8,4},{16,12},{24,20},{5,9},{13,17},{21,25},... | collective-permute-start | bytes 124424 | tf_op jit(solution)/shard_map/ppermute | solution.py:477
  9.1 0.0 collective-permute-done.cols_b
  9.1 0.9 %collective-permute-done.1.cols_a = f32[8,128]{1,0:T(8,128)S(1)} collective-permute-done((f32[8,128]{1,0:T(8,128)S(1)}, f32[8,128]{1,0:T(8,128)S(1)}, u32[]{:S(2)}, u32[]{:S(2)}) %collective-permute-start.1) | collective-permute-done | bytes 4128 | tf_op jit(solution)/shard_map/ppermute | solution.py:477
  9.9 0.0 collective-permute-done.2.rows_a
  9.9 0.5 %shard_map.77 = (f32[2,20,8,128]{3,2,1,0:T(8,128)S(1)}, f32[2,8,128]{2,1,0:T(8,128)S(1)}, f32[20,128]{1,0:T(8,128)S(1)}) custom-call(f32[2,20,8,128]{3,2,1,0:T(8,128)S(1)} %get-tuple-element.21.tracers, f32[2,20,8,128]{3,2,1,0:T(8,128)S(1)} %get-tuple-element.23.velocity, s32[8,128]{1,0:T(8,128)S(1)} %get-tuple-element.22.wet.refs_3_, ...), custom_call_target="tpu_custom_call" | custom-call | tf_op jit(solution)/shard_map/pallas_call | solution.py:488
  10.4 0.0 collective-permute-done.3.across.rows_b
  10.4 0.2 shard_map.78
  10.6 16.8 %all_to_all.5.after_gather = f32[16,19,1,128]{3,2,1,0:T(1,128)S(1)} all-to-all(f32[16,19,1,128]{3,2,1,0:T(1,128)S(1)} %get-tuple-element.34), channel_id=1, replica_groups=mesh['z'=4,'core'=2,'by'=4] {'z','by'}, dimensions={0} | all-to-all | bytes 311296 | tf_op jit(solution)/shard_map/all_to_all | solution.py:501
  27.4 0.0 collective-permute-start.4
  27.5 1.0 %shard_map.79 = (f32[2,20,8,128]{3,2,1,0:T(8,128)}, f32[2,20,8,128]{3,2,1,0:T(8,128)S(1)}) custom-call(f32[2,20,8,128]{3,2,1,0:T(8,128)S(1)} %get-tuple-element.21.tracers, s32[8,128]{1,0:T(8,128)S(1)} %get-tuple-element.22.wet.refs_3_, f32[2,20,8,128]{3,2,1,0:T(8,128)S(1)} %get-tuple-element.28.moved, f32[2,20,128]{2,1,0:T(8,128)S(1)} %get-tuple-element.33.change, ...), custom_call_target="tpu_custom_call" | custom-call | tf_op jit(solution)/shard_map/pallas_call | solution.py:503
  28.4 0.4 %collective-permute-done.4 = f32[16,19,1,128]{3,2,1,0:T(1,128)S(1)} collective-permute-done((f32[16,19,1,128]{3,2,1,0:T(1,128)S(1)}, f32[16,19,1,128]{3,2,1,0:T(1,128)S(1)}, u32[]{:S(2)}, u32[]{:S(2)}) %collective-permute-start.4) | collective-permute-done | bytes 155680 | tf_op jit(solution)/shard_map/ppermute | solution.py:502
  28.8 2.0 %shard_map.80 = (f32[2,20,8,128]{3,2,1,0:T(8,128)}, f32[8,128]{1,0:T(8,128)}) custom-call(f32[304,128]{1,0:T(8,128)S(1)} %bitcast.2, f32[304,128]{1,0:T(8,128)S(1)} %bitcast.3, f32[2,20,8,128]{3,2,1,0:T(8,128)S(1)} %get-tuple-element.36.refs_2_, s32[8,128]{1,0:T(8,128)S(1)} %get-tuple-element.22.wet.refs_3_), custom_call_target="tpu_custom_call" | custom-call | tf_op jit(solution)/shard_map/pallas_call | solution.py:515
  (1 shorter events, 0.0 us)
Async XLA Ops:
  1.9 7.1 %collective-permute-start = (f32[8,128]{1,0:T(8,128)S(1)}, f32[8,128]{1,0:T(8,128)S(1)}, u32[]{:S(2)}, u32[]{:S(2)}) collective-permute-start(f32[8,128]{1,0:T(8,128)S(1)} %get-tuple-element.25), channel_id=1, source_target_pairs={{1,2},{2,1},{5,6},{6,5},{9,10},{10,9},{13,14},{14,13},{17,18},{18,... | collective-permute-start | bytes 12296 | tf_op jit(solution)/shard_map/ppermute | solution.py:477
  2.6 7.3 %collective-permute-start.1 = (f32[8,128]{1,0:T(8,128)S(1)}, f32[8,128]{1,0:T(8,128)S(1)}, u32[]{:S(2)}, u32[]{:S(2)}) collective-permute-start(f32[8,128]{1,0:T(8,128)S(1)} %get-tuple-element.26), channel_id=1, source_target_pairs={{0,1},{2,3},{1,0},{3,2},{4,5},{6,7},{5,4},{7,6},{8,9},{10,11},{9,8... | collective-permute-start | bytes 12296 | tf_op jit(solution)/shard_map/ppermute | solution.py:477
  8.3 1.6 %collective-permute-start.2 = (f32[81,128]{1,0:T(8,128)S(1)}, f32[81,128]{1,0:T(8,128)S(1)}, u32[]{:S(2)}, u32[]{:S(2)}) collective-permute-start(f32[81,128]{1,0:T(8,128)S(1)} %get-tuple-element.27), channel_id=1, source_target_pairs={{0,4},{8,12},{16,20},{24,28},{4,0},{12,8},{20,16},{28,24},{1,5},{9... | collective-permute-start | bytes 124424 | tf_op jit(solution)/shard_map/ppermute | solution.py:477
  8.3 2.1 %collective-permute-start.3 = (f32[81,128]{1,0:T(8,128)S(1)}, f32[81,128]{1,0:T(8,128)S(1)}, u32[]{:S(2)}, u32[]{:S(2)}) collective-permute-start(f32[81,128]{1,0:T(8,128)S(1)} %get-tuple-element.29.own), channel_id=1, source_target_pairs={{4,8},{12,16},{20,24},{8,4},{16,12},{24,20},{5,9},{13,17},{21,25},... | collective-permute-start | bytes 124424 | tf_op jit(solution)/shard_map/ppermute | solution.py:477
  27.4 1.4 %collective-permute-start.4 = (f32[16,19,1,128]{3,2,1,0:T(1,128)S(1)}, f32[16,19,1,128]{3,2,1,0:T(1,128)S(1)}, u32[]{:S(2)}, u32[]{:S(2)}) collective-permute-start(f32[16,19,1,128]{3,2,1,0:T(1,128)S(1)} %all_to_all.5.after_gather), channel_id=1, source_target_pairs={{0,4},{4,0},{1,5},{5,1},{2,6},{6,2},{3,7},{7,3},{8,12},{12,8},{9,1... | collective-permute-start | bytes 466952 | tf_op jit(solution)/shard_map/ppermute | solution.py:502

commit v12 on v11

--- a/solution.py
+++ b/solution.py
@@ -106,8 +106,8 @@
 
 
 def level_kernel(
-    tracers, velocity, wet, weights, latitude, cols_b, cols_a, rows_a,
-    moved_velocity, flows, inner,
+    tracers, velocity, wet, weights, latitude, cols_b, cols_a,
+    moved_velocity, flows, inner_b, inner_a,
 ):
     levels, cols_x, rows_y = tracers.shape[1:]
     shape = (cols_x, rows_y)
@@ -115,10 +115,8 @@
     after_cols, before_cols = side_columns(cols_b, cols_a)
 
     def neighbours(tile, index):
-        row = rows_a[index : index + 1, :]
-        after_row, before_row = (jnp.where(even_x, row, 0.0), jnp.where(even_x, 0.0, row))
         sides = (after_cols[:, index : index + 1], before_cols[:, index : index + 1])
-        return neighbours_of(tile, after_row, before_row, *sides)
+        return neighbours_of(tile, 0.0, 0.0, *sides)
 
     counts = wet[...].astype(jnp.float32)
     around = neighbours(counts, 4 * levels)
@@ -139,9 +137,9 @@
         ]
         difference_x = difference_x + weight * (loads[0] - loads[1])
         difference_y = difference_y + weight * (loads[2] - loads[3])
-        inner[level : level + 1, :] = jnp.where(
-            even_x, difference_x[0:1, :], difference_x[cols_x - 1 : cols_x, :]
-        )
+        low, high = (difference_x[0:1, :], difference_x[cols_x - 1 : cols_x, :])
+        inner_b[level : level + 1, :] = jnp.where(even_x, low, high)
+        inner_a[level : level + 1, :] = jnp.where(even_x, high, low)
         gradient_x = jnp.where(both_x > level, difference_x * 0.5, 0.0)
         gradient_y = jnp.where(both_y > level, difference_y * 0.5, 0.0)
         zonal, merid = (velocity[0, level], velocity[1, level])
@@ -159,18 +157,8 @@
     flows[1] = flow_y
 
 
-def edge_kernel(
-    own, across, inner, weights, wet, diagonal, flows,
-    surface, change,
-):
-    levels = weights.shape[0]
-    cols_x, rows_y = shape = wet.shape
-    low_x, high_x, low_y, high_y = edges_of(shape)
-    lane, sublane = (lanes_of(shape), sublanes_of(shape))
-    even_x = lax.axis_index("core") == 0
-    sign = jnp.where(even_x, -1.0, 1.0)
-    counts = wet[...].astype(jnp.float32)
-    within = jnp.where(even_x, counts[1:2, :], counts[cols_x - 2 : cols_x - 1, :])
+def edge_change(own, across, inner, within, weights, sign, change):
+    levels, rows_y = weights.shape
     count = across[4 * levels : 4 * levels + 1, :]
     shared = jnp.minimum(count, own[4 * levels : 4 * levels + 1, :])
     both = jnp.minimum(shared, within)
@@ -196,9 +184,36 @@
         change[1, level : level + 1, :] = change_y
         added_x = added_x + weight * change_x
         added_y = added_y + weight * change_y
-    edge = sublane == jnp.where(even_x, 0, cols_x - 1)
-    flow_x = flows[0] + jnp.where(edge, added_x, 0.0)
-    flow_y = flows[1] + jnp.where(edge, added_y, 0.0)
+    return added_x, added_y
+
+
+def edge_masks(shape):
+    even_x = lax.axis_index("core") == 0
+    sublane = sublanes_of(shape)
+    last = shape[0] - 1
+    return sublane == jnp.where(even_x, 0, last), sublane == jnp.where(even_x, last, 0)
+
+
+def edge_kernel(
+    own_b, across_b, inner_b, own_a, across_a, inner_a, weights, wet, diagonal, flows,
+    surface, change_b, change_a,
+):
+    cols_x, rows_y = shape = wet.shape
+    low_x, high_x, low_y, high_y = edges_of(shape)
+    lane, sublane = (lanes_of(shape), sublanes_of(shape))
+    even_x = lax.axis_index("core") == 0
+    sign = jnp.where(even_x, -1.0, 1.0)
+    counts = wet[...].astype(jnp.float32)
+    second, last_but_one = (counts[1:2, :], counts[cols_x - 2 : cols_x - 1, :])
+    within_b = jnp.where(even_x, second, last_but_one)
+    within_a = jnp.where(even_x, last_but_one, second)
+    added_b = edge_change(own_b, across_b, inner_b, within_b, weights, sign, change_b)
+    added_a = edge_change(own_a, across_a, inner_a, within_a, weights, -sign, change_a)
+    edge_b, edge_a = edge_masks(shape)
+    flow_x, flow_y = (
+        flows[part] + jnp.where(edge_b, added_b[part], 0.0) + jnp.where(edge_a, added_a[part], 0.0)
+        for part in range(2)
+    )
     inverse = jnp.where(counts > 0, 1.0, 0.0) / (4.0 + diagonal[...])
     ahead = jnp.where(high_x, 0.0, pltpu.roll(flow_x, cols_x - 1, 0))
     behind = jnp.where(low_x, 0.0, pltpu.roll(flow_x, 1, 0))
@@ -223,7 +238,7 @@
 
 
 def tracer_kernel(
-    tracers, wet, moved, change, cols_b, cols_a, rows_b, rows_a, after_gather,
+    tracers, wet, moved, change_b, change_a, cols_b, cols_a, rows_b, rows_a, after_gather,
     new_tracers, moved_velocity,
 ):
     del after_gather
@@ -240,14 +255,14 @@
     counts = wet[...].astype(jnp.float32)
     shared = [jnp.minimum(counts, other) for other in neighbours(counts, 4 * levels)]
     diffusivity = TIME_INCREMENT * KAPPA_SPREAD
-    sublane = sublanes_of((cols_x, rows_y))
-    edge = sublane == jnp.where(even_x, 0, cols_x - 1)
+    edge_b, edge_a = edge_masks((cols_x, rows_y))
     for level in range(levels):
         for part in range(2):
             tile = tracers[part, level]
             spread = laplacian(tile, neighbours(tile, part * levels + level), shared, level)
             new_tracers[part, level] = tile + diffusivity * spread
-            added = jnp.where(edge, change[part, level : level + 1, :], 0.0)
+            added = jnp.where(edge_b, change_b[part, level : level + 1, :], 0.0)
+            added = added + jnp.where(edge_a, change_a[part, level : level + 1, :], 0.0)
             moved_velocity[part, level] = moved[part, level] + added
 
 
@@ -476,36 +491,40 @@
         axes = ("z", "core") if axis == "bx" else axis
         return lax.ppermute(message, axes, pairs + [(j, i) for i, j in pairs])
 
-    sent = rows_b
+    sent_b, sent_a = (rows_b, rows_a)
     rows_b, rows_a = (exchange(rows_b, "bx", 1), exchange(rows_a, "bx", 0))
     cols_b, cols_a = (exchange(cols_b, "by", 1), exchange(cols_a, "by", 0))
     positions = (lax.axis_index("by") * rows_y + jnp.arange(rows_y, dtype=jnp.int32)).astype(jnp.float32)
     latitude = latitude_rate(positions, blocks_y * rows_y)[None]
 
     tracers, velocity, wet, diagonal, weights = block
-    sent = kept(sent)
+    sent_b, sent_a = (kept(sent_b), kept(sent_a))
     rows_a, rows_b, cols_a, cols_b = (kept(array) for array in (rows_a, rows_b, cols_a, cols_b))
-    moved, flows, inner = pl.pallas_call(
+    moved, flows, inner_b, inner_a = pl.pallas_call(
         level_kernel,
-        out_shape=[held(*velocity.shape), held(2, *shape), held(levels, rows_y)],
-        in_specs=[VMEM] * 8,
+        out_shape=[held(*velocity.shape), held(2, *shape)] + [held(levels, rows_y)] * 2,
+        in_specs=[VMEM] * 7,
+        out_specs=[VMEM] * 4,
+    )(tracers, velocity, wet, weights, kept(latitude), cols_b, cols_a)
+    inner_b, inner_a, flows = (kept(inner_b), kept(inner_a), kept(flows))
+    surface, change_b, change_a = pl.pallas_call(
+        edge_kernel,
+        out_shape=[held(chips_z * blocks_y, height, 1, rows_y)] + [held(2, levels, rows_y)] * 2,
+        in_specs=[VMEM] * 10,
         out_specs=[VMEM] * 3,
-    )(tracers, velocity, wet, weights, kept(latitude), cols_b, cols_a, rows_a)
-    surface, change = pl.pallas_call(
-        edge_kernel,
-        out_shape=[held(chips_z * blocks_y, height, 1, rows_y), held(2, levels, rows_y)],
-        in_specs=[VMEM] * 7,
-        out_specs=[VMEM] * 2,
-    )(sent, rows_b, kept(inner), weights, wet, diagonal, kept(flows))
+    )(sent_b, rows_b, inner_b, sent_a, rows_a, inner_a, weights, wet, diagonal, flows)
 
     gathered = lax.all_to_all(surface, ("z", "by"), split_axis=0, concat_axis=0, tiled=True)
     swapped = lax.ppermute(gathered, "core", [(0, 1), (1, 0)])
     new_tracers, moved_velocity = pl.pallas_call(
         tracer_kernel,
         out_shape=[like(*tracers.shape), held(*velocity.shape)],
-        in_specs=[VMEM] * 9,
+        in_specs=[VMEM] * 10,
         out_specs=[VMEM] * 2,
-    )(tracers, wet, kept(moved), kept(change), cols_b, cols_a, rows_b, rows_a, kept(gathered))
+    )(
+        tracers, wet, kept(moved), kept(change_b), kept(change_a),
+        cols_b, cols_a, rows_b, rows_a, kept(gathered),
+    )
     gathered, swapped = (array.reshape(-1, rows_y) for array in (gathered, swapped))
 
     def solve(*refs):

time: 31 us -> 31.1 us (level)
  starting transfers between devices: 7.06 us -> 10.1 us
  blocking collectives: 16.8 us -> 14.4 us
  waiting for transfers between devices: 1.3 us -> 0.75 us
    ppermute x4, starting transfers between devices: 7.06 us -> 10.1 us  [exchange(): return lax.ppermute(message, axes, pairs + [(j, i) for i, j in pairs])]
    all_to_all x1, blocking collectives: 16.8 us -> 14.4 us  [body(): lax.all_to_all(surface, ('z', 'by'), split_axis=0, concat_axis=0, tiled=T...]
    ppermute x4, waiting for transfers between devices: 0.87 us -> 0.32 us  [exchange(): return lax.ppermute(message, axes, pairs + [(j, i) for i, j in pairs])]
where the time goes in v12:
time: 31.1 us; the launch traced here: 30.9 us
  blocking collectives  14.4 us (46%)
  starting transfers between devices  10.1 us (32%)
  Pallas kernels  4.95 us (16%)
  waiting for transfers between devices  0.75 us (2%)
  between operations  0.69 us (2%)
    all_to_all x1, blocking collectives, body(): lax.all_to_all(surface, ('z', 'by'), split_axis=0, concat_axis=0, tiled=T...  14.4 us
    ppermute x4, starting transfers between devices, exchange(): return lax.ppermute(message, axes, pairs + [(j, i) for i, j in pairs])  10.1 us
    pallas_call x1, Pallas kernels, body(): pl.pallas_call(solve, out_shape=[like(*velocity.shape), like(*shape)], in...  1.97 us
    pallas_call x1, Pallas kernels, body(): pl.pallas_call(pack_rims, out_shape=[held(rim_rows, rows_y), held(rim_row...  1.29 us
    pallas_call x1, Pallas kernels, body(): pl.pallas_call(tracer_kernel, out_shape=[like(*tracers.shape), held(*velo...  0.95 us
  transfers between devices with their start and end apart: 5, of which 2 were waited for; matrix products, arithmetic and copies ran while one was open for 0% of the time, Pallas kernels for 5%

profile of v12, /device:TPU:0, one launch (start us, length us, event | category | flops | bytes accessed | tf_op | source)
XLA Modules:
  0.0 30.9 jit_solution(17523058542143114772)
XLA Ops:
  0.6 1.3 %shard_map.76 = (f32[81,128]{1,0:T(8,128)S(1)}, f32[81,128]{1,0:T(8,128)S(1)}, f32[8,128]{1,0:T(8,128)S(1)}, f32[8,128]{1,0:T(8,128)S(1)}, f32[2,20,8,128]{3,2,1...) custom-call(f32[2,20,8,128]{3,2,1,0:T(8,128)} %tracers_in.1, ...), custom_call_target="tpu_custom_call" | custom-call | tf_op jit(solution)/shard_map/pallas_call | solution.py:475
  1.9 0.7 %collective-permute-start = (f32[8,128]{1,0:T(8,128)S(1)}, f32[8,128]{1,0:T(8,128)S(1)}, u32[]{:S(2)}, u32[]{:S(2)}) collective-permute-start(f32[8,128]{1,0:T(8,128)S(1)} %get-tuple-element.27), channel_id=1, source_target_pairs={{1,2},{2,1},{5,6},{6,5},{9,10},{10,9},{13,14},{14,13},{17,18},{18,... | collective-permute-start | bytes 12296 | tf_op jit(solution)/shard_map/ppermute | solution.py:492
  2.6 5.7 %collective-permute-start.1 = (f32[8,128]{1,0:T(8,128)S(1)}, f32[8,128]{1,0:T(8,128)S(1)}, u32[]{:S(2)}, u32[]{:S(2)}) collective-permute-start(f32[8,128]{1,0:T(8,128)S(1)} %get-tuple-element.28), channel_id=1, source_target_pairs={{0,1},{2,3},{1,0},{3,2},{4,5},{6,7},{5,4},{7,6},{8,9},{10,11},{9,8... | collective-permute-start | bytes 12296 | tf_op jit(solution)/shard_map/ppermute | solution.py:492
  8.3 0.7 %collective-permute-start.2 = (f32[81,128]{1,0:T(8,128)S(1)}, f32[81,128]{1,0:T(8,128)S(1)}, u32[]{:S(2)}, u32[]{:S(2)}) collective-permute-start(f32[81,128]{1,0:T(8,128)S(1)} %get-tuple-element.30.own_b), channel_id=1, source_target_pairs={{4,8},{12,16},{20,24},{8,4},{16,12},{24,20},{5,9},{13,17},{21,25},... | collective-permute-start | bytes 124424 | tf_op jit(solution)/shard_map/ppermute | solution.py:492
  9.0 3.0 %collective-permute-start.3 = (f32[81,128]{1,0:T(8,128)S(1)}, f32[81,128]{1,0:T(8,128)S(1)}, u32[]{:S(2)}, u32[]{:S(2)}) collective-permute-start(f32[81,128]{1,0:T(8,128)S(1)} %get-tuple-element.32.own_a), channel_id=1, source_target_pairs={{0,4},{8,12},{16,20},{24,28},{4,0},{12,8},{20,16},{28,24},{1,5},{9... | collective-permute-start | bytes 124424 | tf_op jit(solution)/shard_map/ppermute | solution.py:492
  12.1 0.0 collective-permute-done.cols_b
  12.1 0.0 collective-permute-done.1.cols_a
  12.1 0.5 %shard_map.77 = (f32[2,20,8,128]{3,2,1,0:T(8,128)S(1)}, f32[2,8,128]{2,1,0:T(8,128)S(1)}, f32[20,128]{1,0:T(8,128)S(1)}, f32[20,128]{1,0:T(8,128)S(1)}) custom-call(f32[2,20,8,128]{3,2,1,0:T(8,128)S(1)} %get-tuple-element.23.tracers, f32[2,20,8,128]{3,2,1,0:T(8,128)S(1)} %get-tuple-element.25.velocity, s32[8,128]{1,0:T(8,128)S(1)} %get-tuple-element.24.wet.refs_3_, ...), custom_call_target="tpu_custom_call" | custom-call | tf_op jit(solution)/shard_map/pallas_call | solution.py:503
  12.6 0.0 collective-permute-done.2.across_b.rows_b
  12.6 0.3 %collective-permute-done.3.across_a.rows_a = f32[81,128]{1,0:T(8,128)S(1)} collective-permute-done((f32[81,128]{1,0:T(8,128)S(1)}, f32[81,128]{1,0:T(8,128)S(1)}, u32[]{:S(2)}, u32[]{:S(2)}) %collective-permute-start.3) | collective-permute-done | bytes 41504 | tf_op jit(solution)/shard_map/ppermute | solution.py:492
  12.9 0.3 shard_map.78
  13.1 14.4 %all_to_all.5.after_gather = f32[16,19,1,128]{3,2,1,0:T(1,128)S(1)} all-to-all(f32[16,19,1,128]{3,2,1,0:T(1,128)S(1)} %get-tuple-element.38), channel_id=1, replica_groups=mesh['z'=4,'core'=2,'by'=4] {'z','by'}, dimensions={0} | all-to-all | bytes 311296 | tf_op jit(solution)/shard_map/all_to_all | solution.py:517
  27.5 0.0 collective-permute-start.4
  27.5 1.0 %shard_map.79 = (f32[2,20,8,128]{3,2,1,0:T(8,128)}, f32[2,20,8,128]{3,2,1,0:T(8,128)S(1)}) custom-call(f32[2,20,8,128]{3,2,1,0:T(8,128)S(1)} %get-tuple-element.23.tracers, s32[8,128]{1,0:T(8,128)S(1)} %get-tuple-element.24.wet.refs_3_, f32[2,20,8,128]{3,2,1,0:T(8,128)S(1)} %get-tuple-element.29.moved, f32[2,20,128]{2,1,0:T(8,128)S(1)} %get-tuple-element.36.change_b, ...), custom_call_target="tpu_custom_call" | custom-call | tf_op jit(solution)/shard_map/pallas_call | solution.py:519
  28.5 0.4 %collective-permute-done.4 = f32[16,19,1,128]{3,2,1,0:T(1,128)S(1)} collective-permute-done((f32[16,19,1,128]{3,2,1,0:T(1,128)S(1)}, f32[16,19,1,128]{3,2,1,0:T(1,128)S(1)}, u32[]{:S(2)}, u32[]{:S(2)}) %collective-permute-start.4) | collective-permute-done | bytes 155680 | tf_op jit(solution)/shard_map/ppermute | solution.py:518
  28.9 2.0 %shard_map.80 = (f32[2,20,8,128]{3,2,1,0:T(8,128)}, f32[8,128]{1,0:T(8,128)}) custom-call(f32[304,128]{1,0:T(8,128)S(1)} %bitcast.2, f32[304,128]{1,0:T(8,128)S(1)} %bitcast.3, f32[2,20,8,128]{3,2,1,0:T(8,128)S(1)} %get-tuple-element.40.refs_2_, s32[8,128]{1,0:T(8,128)S(1)} %get-tuple-element.24.wet.refs_3_), custom_call_target="tpu_custom_call" | custom-call | tf_op jit(solution)/shard_map/pallas_call | solution.py:534
  (1 shorter events, 0.0 us)
Async XLA Ops:
  1.9 10.1 %collective-permute-start = (f32[8,128]{1,0:T(8,128)S(1)}, f32[8,128]{1,0:T(8,128)S(1)}, u32[]{:S(2)}, u32[]{:S(2)}) collective-permute-start(f32[8,128]{1,0:T(8,128)S(1)} %get-tuple-element.27), channel_id=1, source_target_pairs={{1,2},{2,1},{5,6},{6,5},{9,10},{10,9},{13,14},{14,13},{17,18},{18,... | collective-permute-start | bytes 12296 | tf_op jit(solution)/shard_map/ppermute | solution.py:492
  2.6 9.5 %collective-permute-start.1 = (f32[8,128]{1,0:T(8,128)S(1)}, f32[8,128]{1,0:T(8,128)S(1)}, u32[]{:S(2)}, u32[]{:S(2)}) collective-permute-start(f32[8,128]{1,0:T(8,128)S(1)} %get-tuple-element.28), channel_id=1, source_target_pairs={{0,1},{2,3},{1,0},{3,2},{4,5},{6,7},{5,4},{7,6},{8,9},{10,11},{9,8... | collective-permute-start | bytes 12296 | tf_op jit(solution)/shard_map/ppermute | solution.py:492
  8.3 4.2 %collective-permute-start.2 = (f32[81,128]{1,0:T(8,128)S(1)}, f32[81,128]{1,0:T(8,128)S(1)}, u32[]{:S(2)}, u32[]{:S(2)}) collective-permute-start(f32[81,128]{1,0:T(8,128)S(1)} %get-tuple-element.30.own_b), channel_id=1, source_target_pairs={{4,8},{12,16},{20,24},{8,4},{16,12},{24,20},{5,9},{13,17},{21,25},... | collective-permute-start | bytes 124424 | tf_op jit(solution)/shard_map/ppermute | solution.py:492
  9.0 3.9 %collective-permute-start.3 = (f32[81,128]{1,0:T(8,128)S(1)}, f32[81,128]{1,0:T(8,128)S(1)}, u32[]{:S(2)}, u32[]{:S(2)}) collective-permute-start(f32[81,128]{1,0:T(8,128)S(1)} %get-tuple-element.32.own_a), channel_id=1, source_target_pairs={{0,4},{8,12},{16,20},{24,28},{4,0},{12,8},{20,16},{28,24},{1,5},{9... | collective-permute-start | bytes 124424 | tf_op jit(solution)/shard_map/ppermute | solution.py:492
  27.5 1.4 %collective-permute-start.4 = (f32[16,19,1,128]{3,2,1,0:T(1,128)S(1)}, f32[16,19,1,128]{3,2,1,0:T(1,128)S(1)}, u32[]{:S(2)}, u32[]{:S(2)}) collective-permute-start(f32[16,19,1,128]{3,2,1,0:T(1,128)S(1)} %all_to_all.5.after_gather), channel_id=1, source_target_pairs={{0,4},{4,0},{1,5},{5,1},{2,6},{6,2},{3,7},{7,3},{8,12},{12,8},{9,1... | collective-permute-start | bytes 466952 | tf_op jit(solution)/shard_map/ppermute | solution.py:518

commit v13 on v12

--- a/solution.py
+++ b/solution.py
@@ -327,7 +327,7 @@
 
     def unpack(chip, carry):
         for column in range(blocks_y):
-            place = (chip * blocks_y + column) * height
+            place = (column * (blocks_x // 2) + chip) * height
             for blocks, core in ((gathered, own_core), (swapped, 1 - own_core)):
                 index = (2 * chip + core) * blocks_y + column
                 forcing[index] = blocks[pl.ds(place, cols_x), :]
@@ -340,10 +340,18 @@
     def edge_row(which, row, column):
         return guarded(lambda i: edges[i, which : which + 1], row, column)
 
+    def columns_of(first, count):
+        corners = [edges[first + number, 2:3] for number in range(count)]
+        filler = [jnp.zeros((1, rows_y), jnp.float32)] * (-count % 8)
+        return jnp.transpose(jnp.concatenate(corners + filler, axis=0))[0 : 2 * cols_x]
+
+    turned = columns_of(0, blocks_x * blocks_y) if blocks_x <= 8 else None
+
     def begin(row, carry):
-        corners = [edges[row * blocks_y + c, 2:3] for c in range(blocks_y)]
-        filler = [jnp.zeros((1, rows_y), jnp.float32)] * (-blocks_y % 8)
-        corners = jnp.transpose(jnp.concatenate(corners + filler, axis=0))
+        if turned is None:
+            corners = columns_of(row * blocks_y, blocks_y)
+        else:
+            corners = turned[:, row * blocks_y : (row + 1) * blocks_y]
         for column in range(blocks_y):
             index = row * blocks_y + column
             whole = forcing[index]
@@ -514,7 +522,7 @@
         out_specs=[VMEM] * 3,
     )(sent_b, rows_b, inner_b, sent_a, rows_a, inner_a, weights, wet, diagonal, flows)
 
-    gathered = lax.all_to_all(surface, ("z", "by"), split_axis=0, concat_axis=0, tiled=True)
+    gathered = lax.all_to_all(surface, ("by", "z"), split_axis=0, concat_axis=0, tiled=True)
     swapped = lax.ppermute(gathered, "core", [(0, 1), (1, 0)])
     new_tracers, moved_velocity = pl.pallas_call(
         tracer_kernel,

time: 31.1 us -> 30.9 us (level)
  no operation moved by 1% of the time
where the time goes in v13:
time: 30.9 us; the launch traced here: 30.7 us
  blocking collectives  14.2 us (46%)
  starting transfers between devices  10.1 us (33%)
  Pallas kernels  4.99 us (16%)
  waiting for transfers between devices  0.75 us (2%)
  between operations  0.69 us (2%)
    all_to_all x1, blocking collectives, body(): lax.all_to_all(surface, ('by', 'z'), split_axis=0, concat_axis=0, tiled=T...  14.2 us
    ppermute x4, starting transfers between devices, exchange(): return lax.ppermute(message, axes, pairs + [(j, i) for i, j in pairs])  10.1 us
    pallas_call x1, Pallas kernels, body(): pl.pallas_call(solve, out_shape=[like(*velocity.shape), like(*shape)], in...  2.01 us
    pallas_call x1, Pallas kernels, body(): pl.pallas_call(pack_rims, out_shape=[held(rim_rows, rows_y), held(rim_row...  1.29 us
    pallas_call x1, Pallas kernels, body(): pl.pallas_call(tracer_kernel, out_shape=[like(*tracers.shape), held(*velo...  0.95 us
  transfers between devices with their start and end apart: 5, of which 2 were waited for; matrix products, arithmetic and copies ran while one was open for 0% of the time, Pallas kernels for 5%

profile of v13, /device:TPU:0, one launch (start us, length us, event | category | flops | bytes accessed | tf_op | source)
XLA Modules:
  0.0 30.7 jit_solution(13713869475525727328)
XLA Ops:
  0.6 1.3 %shard_map.76 = (f32[81,128]{1,0:T(8,128)S(1)}, f32[81,128]{1,0:T(8,128)S(1)}, f32[8,128]{1,0:T(8,128)S(1)}, f32[8,128]{1,0:T(8,128)S(1)}, f32[2,20,8,128]{3,2,1...) custom-call(f32[2,20,8,128]{3,2,1,0:T(8,128)} %tracers_in.1, ...), custom_call_target="tpu_custom_call" | custom-call | tf_op jit(solution)/shard_map/pallas_call | solution.py:483
  1.9 0.7 %collective-permute-start = (f32[8,128]{1,0:T(8,128)S(1)}, f32[8,128]{1,0:T(8,128)S(1)}, u32[]{:S(2)}, u32[]{:S(2)}) collective-permute-start(f32[8,128]{1,0:T(8,128)S(1)} %get-tuple-element.27), channel_id=1, source_target_pairs={{1,2},{2,1},{5,6},{6,5},{9,10},{10,9},{13,14},{14,13},{17,18},{18,... | collective-permute-start | bytes 12296 | tf_op jit(solution)/shard_map/ppermute | solution.py:500
  2.6 5.7 %collective-permute-start.1 = (f32[8,128]{1,0:T(8,128)S(1)}, f32[8,128]{1,0:T(8,128)S(1)}, u32[]{:S(2)}, u32[]{:S(2)}) collective-permute-start(f32[8,128]{1,0:T(8,128)S(1)} %get-tuple-element.28), channel_id=1, source_target_pairs={{0,1},{2,3},{1,0},{3,2},{4,5},{6,7},{5,4},{7,6},{8,9},{10,11},{9,8... | collective-permute-start | bytes 12296 | tf_op jit(solution)/shard_map/ppermute | solution.py:500
  8.3 0.7 %collective-permute-start.2 = (f32[81,128]{1,0:T(8,128)S(1)}, f32[81,128]{1,0:T(8,128)S(1)}, u32[]{:S(2)}, u32[]{:S(2)}) collective-permute-start(f32[81,128]{1,0:T(8,128)S(1)} %get-tuple-element.30.own_b), channel_id=1, source_target_pairs={{4,8},{12,16},{20,24},{8,4},{16,12},{24,20},{5,9},{13,17},{21,25},... | collective-permute-start | bytes 124424 | tf_op jit(solution)/shard_map/ppermute | solution.py:500
  9.0 3.0 %collective-permute-start.3 = (f32[81,128]{1,0:T(8,128)S(1)}, f32[81,128]{1,0:T(8,128)S(1)}, u32[]{:S(2)}, u32[]{:S(2)}) collective-permute-start(f32[81,128]{1,0:T(8,128)S(1)} %get-tuple-element.32.own_a), channel_id=1, source_target_pairs={{0,4},{8,12},{16,20},{24,28},{4,0},{12,8},{20,16},{28,24},{1,5},{9... | collective-permute-start | bytes 124424 | tf_op jit(solution)/shard_map/ppermute | solution.py:500
  12.1 0.0 collective-permute-done.cols_b
  12.1 0.0 collective-permute-done.1.cols_a
  12.1 0.5 %shard_map.77 = (f32[2,20,8,128]{3,2,1,0:T(8,128)S(1)}, f32[2,8,128]{2,1,0:T(8,128)S(1)}, f32[20,128]{1,0:T(8,128)S(1)}, f32[20,128]{1,0:T(8,128)S(1)}) custom-call(f32[2,20,8,128]{3,2,1,0:T(8,128)S(1)} %get-tuple-element.23.tracers, f32[2,20,8,128]{3,2,1,0:T(8,128)S(1)} %get-tuple-element.25.velocity, s32[8,128]{1,0:T(8,128)S(1)} %get-tuple-element.24.wet.refs_3_, ...), custom_call_target="tpu_custom_call" | custom-call | tf_op jit(solution)/shard_map/pallas_call | solution.py:511
  12.6 0.0 collective-permute-done.2.across_b.rows_b
  12.6 0.3 %collective-permute-done.3.across_a.rows_a = f32[81,128]{1,0:T(8,128)S(1)} collective-permute-done((f32[81,128]{1,0:T(8,128)S(1)}, f32[81,128]{1,0:T(8,128)S(1)}, u32[]{:S(2)}, u32[]{:S(2)}) %collective-permute-start.3) | collective-permute-done | bytes 41504 | tf_op jit(solution)/shard_map/ppermute | solution.py:500
  12.9 0.3 shard_map.78
  13.1 14.2 %all_to_all.5.after_gather = f32[16,19,1,128]{3,2,1,0:T(1,128)S(1)} all-to-all(f32[16,19,1,128]{3,2,1,0:T(1,128)S(1)} %get-tuple-element.38), channel_id=1, replica_groups=mesh['z'=4,'core'=2,'by'=4] {'by','z'}, dimensions={0} | all-to-all | bytes 311296 | tf_op jit(solution)/shard_map/all_to_all | solution.py:525
  27.3 0.0 collective-permute-start.4
  27.3 1.0 %shard_map.79 = (f32[2,20,8,128]{3,2,1,0:T(8,128)}, f32[2,20,8,128]{3,2,1,0:T(8,128)S(1)}) custom-call(f32[2,20,8,128]{3,2,1,0:T(8,128)S(1)} %get-tuple-element.23.tracers, s32[8,128]{1,0:T(8,128)S(1)} %get-tuple-element.24.wet.refs_3_, f32[2,20,8,128]{3,2,1,0:T(8,128)S(1)} %get-tuple-element.29.moved, f32[2,20,128]{2,1,0:T(8,128)S(1)} %get-tuple-element.36.change_b, ...), custom_call_target="tpu_custom_call" | custom-call | tf_op jit(solution)/shard_map/pallas_call | solution.py:527
  28.3 0.4 %collective-permute-done.4 = f32[16,19,1,128]{3,2,1,0:T(1,128)S(1)} collective-permute-done((f32[16,19,1,128]{3,2,1,0:T(1,128)S(1)}, f32[16,19,1,128]{3,2,1,0:T(1,128)S(1)}, u32[]{:S(2)}, u32[]{:S(2)}) %collective-permute-start.4) | collective-permute-done | bytes 155680 | tf_op jit(solution)/shard_map/ppermute | solution.py:526
  28.7 2.0 %shard_map.80 = (f32[2,20,8,128]{3,2,1,0:T(8,128)}, f32[8,128]{1,0:T(8,128)}) custom-call(f32[304,128]{1,0:T(8,128)S(1)} %bitcast.2, f32[304,128]{1,0:T(8,128)S(1)} %bitcast.3, f32[2,20,8,128]{3,2,1,0:T(8,128)S(1)} %get-tuple-element.40.refs_2_, s32[8,128]{1,0:T(8,128)S(1)} %get-tuple-element.24.wet.refs_3_), custom_call_target="tpu_custom_call" | custom-call | tf_op jit(solution)/shard_map/pallas_call | solution.py:542
  (1 shorter events, 0.0 us)
Async XLA Ops:
  1.9 10.1 %collective-permute-start = (f32[8,128]{1,0:T(8,128)S(1)}, f32[8,128]{1,0:T(8,128)S(1)}, u32[]{:S(2)}, u32[]{:S(2)}) collective-permute-start(f32[8,128]{1,0:T(8,128)S(1)} %get-tuple-element.27), channel_id=1, source_target_pairs={{1,2},{2,1},{5,6},{6,5},{9,10},{10,9},{13,14},{14,13},{17,18},{18,... | collective-permute-start | bytes 12296 | tf_op jit(solution)/shard_map/ppermute | solution.py:500
  2.6 9.5 %collective-permute-start.1 = (f32[8,128]{1,0:T(8,128)S(1)}, f32[8,128]{1,0:T(8,128)S(1)}, u32[]{:S(2)}, u32[]{:S(2)}) collective-permute-start(f32[8,128]{1,0:T(8,128)S(1)} %get-tuple-element.28), channel_id=1, source_target_pairs={{0,1},{2,3},{1,0},{3,2},{4,5},{6,7},{5,4},{7,6},{8,9},{10,11},{9,8... | collective-permute-start | bytes 12296 | tf_op jit(solution)/shard_map/ppermute | solution.py:500
  8.3 4.2 %collective-permute-start.2 = (f32[81,128]{1,0:T(8,128)S(1)}, f32[81,128]{1,0:T(8,128)S(1)}, u32[]{:S(2)}, u32[]{:S(2)}) collective-permute-start(f32[81,128]{1,0:T(8,128)S(1)} %get-tuple-element.30.own_b), channel_id=1, source_target_pairs={{4,8},{12,16},{20,24},{8,4},{16,12},{24,20},{5,9},{13,17},{21,25},... | collective-permute-start | bytes 124424 | tf_op jit(solution)/shard_map/ppermute | solution.py:500
  9.0 3.9 %collective-permute-start.3 = (f32[81,128]{1,0:T(8,128)S(1)}, f32[81,128]{1,0:T(8,128)S(1)}, u32[]{:S(2)}, u32[]{:S(2)}) collective-permute-start(f32[81,128]{1,0:T(8,128)S(1)} %get-tuple-element.32.own_a), channel_id=1, source_target_pairs={{0,4},{8,12},{16,20},{24,28},{4,0},{12,8},{20,16},{28,24},{1,5},{9... | collective-permute-start | bytes 124424 | tf_op jit(solution)/shard_map/ppermute | solution.py:500
  27.3 1.4 %collective-permute-start.4 = (f32[16,19,1,128]{3,2,1,0:T(1,128)S(1)}, f32[16,19,1,128]{3,2,1,0:T(1,128)S(1)}, u32[]{:S(2)}, u32[]{:S(2)}) collective-permute-start(f32[16,19,1,128]{3,2,1,0:T(1,128)S(1)} %all_to_all.5.after_gather), channel_id=1, source_target_pairs={{0,4},{4,0},{1,5},{5,1},{2,6},{6,2},{3,7},{7,3},{8,12},{12,8},{9,1... | collective-permute-start | bytes 466952 | tf_op jit(solution)/shard_map/ppermute | solution.py:526

commit v14 on v13

--- a/solution.py
+++ b/solution.py
@@ -380,10 +380,27 @@
             for column in range(blocks_y):
                 index = row * blocks_y + column
                 result = lifted[index] - (along_x(load, row, column) + beside[column])
-                if image is not None:
-                    image[index] = result
+                image[index] = result
                 inner = inner + residual[index] * tiles[column]
                 curvature = curvature + tiles[column] * result
+            return inner, curvature
+
+        inner, curvature = each_row(step, (zero, zero))
+        return total(inner), total(curvature)
+
+    def measure_last(lifted, smooth):
+        def step(row, carry):
+            inner, curvature = carry
+            tiles = [smooth[row * blocks_y + c] for c in range(blocks_y)]
+            ahead = [pltpu.roll(tile, rows_y - 1, 1) for tile in tiles] + [0.0]
+            for column in range(blocks_y):
+                index = row * blocks_y + column
+                tile = tiles[column]
+                other = guarded(lambda i: smooth[i, 0:1], row + 1, column)
+                near = jnp.where(high_x, other, pltpu.roll(tile, cols_x - 1, 0))
+                near = near + jnp.where(high_y, ahead[column + 1], ahead[column])
+                inner = inner + residual[index] * tile
+                curvature = curvature + tile * (lifted[index] - 2.0 * near)
             return inner, curvature
 
         inner, curvature = each_row(step, (zero, zero))
@@ -423,7 +440,7 @@
         return carry
 
     each_row(advance_1, 0)
-    inner_2, curvature_2 = operate(lifted_0, smooth_2, None)
+    inner_2, curvature_2 = measure_last(lifted_0, smooth_2)
     turn_2 = inner_2 / inner_1
     step_2 = inner_2 / (curvature_2 - turn_2 * inner_2 / step_1)
 

time: 30.9 us -> 30.9 us (level)
  no operation moved by 1% of the time
where the time goes in v14:
time: 30.9 us; the launch traced here: 30.7 us
  blocking collectives  14.2 us (46%)
  starting transfers between devices  10.1 us (33%)
  Pallas kernels  4.99 us (16%)
  waiting for transfers between devices  0.75 us (2%)
  between operations  0.69 us (2%)
    all_to_all x1, blocking collectives, body(): lax.all_to_all(surface, ('by', 'z'), split_axis=0, concat_axis=0, tiled=T...  14.2 us
    ppermute x4, starting transfers between devices, exchange(): return lax.ppermute(message, axes, pairs + [(j, i) for i, j in pairs])  10.1 us
    pallas_call x1, Pallas kernels, body(): pl.pallas_call(solve, out_shape=[like(*velocity.shape), like(*shape)], in...  2.01 us
    pallas_call x1, Pallas kernels, body(): pl.pallas_call(pack_rims, out_shape=[held(rim_rows, rows_y), held(rim_row...  1.29 us
    pallas_call x1, Pallas kernels, body(): pl.pallas_call(tracer_kernel, out_shape=[like(*tracers.shape), held(*velo...  0.95 us
  transfers between devices with their start and end apart: 5, of which 2 were waited for; matrix products, arithmetic and copies ran while one was open for 0% of the time, Pallas kernels for 5%

profile of v14, /device:TPU:0, one launch (start us, length us, event | category | flops | bytes accessed | tf_op | source)
XLA Modules:
  0.0 30.7 jit_solution(9759109048414251674)
XLA Ops:
  0.6 1.3 %shard_map.76 = (f32[81,128]{1,0:T(8,128)S(1)}, f32[81,128]{1,0:T(8,128)S(1)}, f32[8,128]{1,0:T(8,128)S(1)}, f32[8,128]{1,0:T(8,128)S(1)}, f32[2,20,8,128]{3,2,1...) custom-call(f32[2,20,8,128]{3,2,1,0:T(8,128)} %tracers_in.1, ...), custom_call_target="tpu_custom_call" | custom-call | tf_op jit(solution)/shard_map/pallas_call | solution.py:500
  1.9 0.7 %collective-permute-start = (f32[8,128]{1,0:T(8,128)S(1)}, f32[8,128]{1,0:T(8,128)S(1)}, u32[]{:S(2)}, u32[]{:S(2)}) collective-permute-start(f32[8,128]{1,0:T(8,128)S(1)} %get-tuple-element.27), channel_id=1, source_target_pairs={{1,2},{2,1},{5,6},{6,5},{9,10},{10,9},{13,14},{14,13},{17,18},{18,... | collective-permute-start | bytes 12296 | tf_op jit(solution)/shard_map/ppermute | solution.py:517
  2.6 5.7 %collective-permute-start.1 = (f32[8,128]{1,0:T(8,128)S(1)}, f32[8,128]{1,0:T(8,128)S(1)}, u32[]{:S(2)}, u32[]{:S(2)}) collective-permute-start(f32[8,128]{1,0:T(8,128)S(1)} %get-tuple-element.28), channel_id=1, source_target_pairs={{0,1},{2,3},{1,0},{3,2},{4,5},{6,7},{5,4},{7,6},{8,9},{10,11},{9,8... | collective-permute-start | bytes 12296 | tf_op jit(solution)/shard_map/ppermute | solution.py:517
  8.3 0.7 %collective-permute-start.2 = (f32[81,128]{1,0:T(8,128)S(1)}, f32[81,128]{1,0:T(8,128)S(1)}, u32[]{:S(2)}, u32[]{:S(2)}) collective-permute-start(f32[81,128]{1,0:T(8,128)S(1)} %get-tuple-element.30.own_b), channel_id=1, source_target_pairs={{4,8},{12,16},{20,24},{8,4},{16,12},{24,20},{5,9},{13,17},{21,25},... | collective-permute-start | bytes 124424 | tf_op jit(solution)/shard_map/ppermute | solution.py:517
  9.0 3.0 %collective-permute-start.3 = (f32[81,128]{1,0:T(8,128)S(1)}, f32[81,128]{1,0:T(8,128)S(1)}, u32[]{:S(2)}, u32[]{:S(2)}) collective-permute-start(f32[81,128]{1,0:T(8,128)S(1)} %get-tuple-element.32.own_a), channel_id=1, source_target_pairs={{0,4},{8,12},{16,20},{24,28},{4,0},{12,8},{20,16},{28,24},{1,5},{9... | collective-permute-start | bytes 124424 | tf_op jit(solution)/shard_map/ppermute | solution.py:517
  12.1 0.0 collective-permute-done.cols_b
  12.1 0.0 collective-permute-done.1.cols_a
  12.1 0.5 %shard_map.77 = (f32[2,20,8,128]{3,2,1,0:T(8,128)S(1)}, f32[2,8,128]{2,1,0:T(8,128)S(1)}, f32[20,128]{1,0:T(8,128)S(1)}, f32[20,128]{1,0:T(8,128)S(1)}) custom-call(f32[2,20,8,128]{3,2,1,0:T(8,128)S(1)} %get-tuple-element.23.tracers, f32[2,20,8,128]{3,2,1,0:T(8,128)S(1)} %get-tuple-element.25.velocity, s32[8,128]{1,0:T(8,128)S(1)} %get-tuple-element.24.wet.refs_3_, ...), custom_call_target="tpu_custom_call" | custom-call | tf_op jit(solution)/shard_map/pallas_call | solution.py:528
  12.6 0.0 collective-permute-done.2.across_b.rows_b
  12.6 0.3 %collective-permute-done.3.across_a.rows_a = f32[81,128]{1,0:T(8,128)S(1)} collective-permute-done((f32[81,128]{1,0:T(8,128)S(1)}, f32[81,128]{1,0:T(8,128)S(1)}, u32[]{:S(2)}, u32[]{:S(2)}) %collective-permute-start.3) | collective-permute-done | bytes 41504 | tf_op jit(solution)/shard_map/ppermute | solution.py:517
  12.9 0.3 shard_map.78
  13.1 14.2 %all_to_all.5.after_gather = f32[16,19,1,128]{3,2,1,0:T(1,128)S(1)} all-to-all(f32[16,19,1,128]{3,2,1,0:T(1,128)S(1)} %get-tuple-element.38), channel_id=1, replica_groups=mesh['z'=4,'core'=2,'by'=4] {'by','z'}, dimensions={0} | all-to-all | bytes 311296 | tf_op jit(solution)/shard_map/all_to_all | solution.py:542
  27.3 0.0 collective-permute-start.4
  27.3 1.0 %shard_map.79 = (f32[2,20,8,128]{3,2,1,0:T(8,128)}, f32[2,20,8,128]{3,2,1,0:T(8,128)S(1)}) custom-call(f32[2,20,8,128]{3,2,1,0:T(8,128)S(1)} %get-tuple-element.23.tracers, s32[8,128]{1,0:T(8,128)S(1)} %get-tuple-element.24.wet.refs_3_, f32[2,20,8,128]{3,2,1,0:T(8,128)S(1)} %get-tuple-element.29.moved, f32[2,20,128]{2,1,0:T(8,128)S(1)} %get-tuple-element.36.change_b, ...), custom_call_target="tpu_custom_call" | custom-call | tf_op jit(solution)/shard_map/pallas_call | solution.py:544
  28.3 0.4 %collective-permute-done.4 = f32[16,19,1,128]{3,2,1,0:T(1,128)S(1)} collective-permute-done((f32[16,19,1,128]{3,2,1,0:T(1,128)S(1)}, f32[16,19,1,128]{3,2,1,0:T(1,128)S(1)}, u32[]{:S(2)}, u32[]{:S(2)}) %collective-permute-start.4) | collective-permute-done | bytes 155680 | tf_op jit(solution)/shard_map/ppermute | solution.py:543
  28.7 2.0 %shard_map.80 = (f32[2,20,8,128]{3,2,1,0:T(8,128)}, f32[8,128]{1,0:T(8,128)}) custom-call(f32[304,128]{1,0:T(8,128)S(1)} %bitcast.2, f32[304,128]{1,0:T(8,128)S(1)} %bitcast.3, f32[2,20,8,128]{3,2,1,0:T(8,128)S(1)} %get-tuple-element.40.refs_2_, s32[8,128]{1,0:T(8,128)S(1)} %get-tuple-element.24.wet.refs_3_), custom_call_target="tpu_custom_call" | custom-call | tf_op jit(solution)/shard_map/pallas_call | solution.py:559
  (1 shorter events, 0.0 us)
Async XLA Ops:
  1.9 10.1 %collective-permute-start = (f32[8,128]{1,0:T(8,128)S(1)}, f32[8,128]{1,0:T(8,128)S(1)}, u32[]{:S(2)}, u32[]{:S(2)}) collective-permute-start(f32[8,128]{1,0:T(8,128)S(1)} %get-tuple-element.27), channel_id=1, source_target_pairs={{1,2},{2,1},{5,6},{6,5},{9,10},{10,9},{13,14},{14,13},{17,18},{18,... | collective-permute-start | bytes 12296 | tf_op jit(solution)/shard_map/ppermute | solution.py:517
  2.6 9.5 %collective-permute-start.1 = (f32[8,128]{1,0:T(8,128)S(1)}, f32[8,128]{1,0:T(8,128)S(1)}, u32[]{:S(2)}, u32[]{:S(2)}) collective-permute-start(f32[8,128]{1,0:T(8,128)S(1)} %get-tuple-element.28), channel_id=1, source_target_pairs={{0,1},{2,3},{1,0},{3,2},{4,5},{6,7},{5,4},{7,6},{8,9},{10,11},{9,8... | collective-permute-start | bytes 12296 | tf_op jit(solution)/shard_map/ppermute | solution.py:517
  8.3 4.2 %collective-permute-start.2 = (f32[81,128]{1,0:T(8,128)S(1)}, f32[81,128]{1,0:T(8,128)S(1)}, u32[]{:S(2)}, u32[]{:S(2)}) collective-permute-start(f32[81,128]{1,0:T(8,128)S(1)} %get-tuple-element.30.own_b), channel_id=1, source_target_pairs={{4,8},{12,16},{20,24},{8,4},{16,12},{24,20},{5,9},{13,17},{21,25},... | collective-permute-start | bytes 124424 | tf_op jit(solution)/shard_map/ppermute | solution.py:517
  9.0 3.9 %collective-permute-start.3 = (f32[81,128]{1,0:T(8,128)S(1)}, f32[81,128]{1,0:T(8,128)S(1)}, u32[]{:S(2)}, u32[]{:S(2)}) collective-permute-start(f32[81,128]{1,0:T(8,128)S(1)} %get-tuple-element.32.own_a), channel_id=1, source_target_pairs={{0,4},{8,12},{16,20},{24,28},{4,0},{12,8},{20,16},{28,24},{1,5},{9... | collective-permute-start | bytes 124424 | tf_op jit(solution)/shard_map/ppermute | solution.py:517
  27.3 1.4 %collective-permute-start.4 = (f32[16,19,1,128]{3,2,1,0:T(1,128)S(1)}, f32[16,19,1,128]{3,2,1,0:T(1,128)S(1)}, u32[]{:S(2)}, u32[]{:S(2)}) collective-permute-start(f32[16,19,1,128]{3,2,1,0:T(1,128)S(1)} %all_to_all.5.after_gather), channel_id=1, source_target_pairs={{0,4},{4,0},{1,5},{5,1},{2,6},{6,2},{3,7},{7,3},{8,12},{12,8},{9,1... | collective-permute-start | bytes 466952 | tf_op jit(solution)/shard_map/ppermute | solution.py:543

commit v15 on v14

--- a/solution.py
+++ b/solution.py
@@ -55,14 +55,15 @@
         copy.start()
     even_x, even_y = (lax.axis_index("core") == 0, lax.axis_index("by") % 2 == 0)
     lane = lanes_of((cols_x, rows_y))
-    for copy in copies:
-        copy.wait()
-    for level in range(levels):
-        weights[level : level + 1, :] = jnp.full((1, rows_y), thickness[level], jnp.float32)
+    of_tracers, of_velocity, of_wet, *others = copies
+    of_wet.wait()
+    of_tracers.wait()
     counts = wet[...].astype(jnp.float32)
     first, last = jnp.zeros_like(counts), jnp.zeros_like(counts)
     for index in range(4 * levels + 1):
         field, level = divmod(index, levels)
+        if index == 2 * levels:
+            of_velocity.wait()
         if field < 4:
             tile = (tracers if field < 2 else velocity)[field % 2, level]
         else:
@@ -74,6 +75,10 @@
         last = jnp.where(lane == index, tile[:, rows_y - 1 : rows_y], last)
     cols_a[...] = jnp.where(even_y, last, first)
     cols_b[...] = jnp.where(even_y, first, last)
+    for copy in others:
+        copy.wait()
+    for level in range(levels):
+        weights[level : level + 1, :] = jnp.full((1, rows_y), thickness[level], jnp.float32)
 
 
 def edges_of(shape):

time: 30.9 us -> 30.9 us (level)
  no operation moved by 1% of the time
where the time goes in v15:
time: 30.9 us; the launch traced here: 30.7 us
  blocking collectives  14.2 us (46%)
  starting transfers between devices  10.1 us (33%)
  Pallas kernels  4.99 us (16%)
  waiting for transfers between devices  0.75 us (2%)
  between operations  0.69 us (2%)
    all_to_all x1, blocking collectives, body(): lax.all_to_all(surface, ('by', 'z'), split_axis=0, concat_axis=0, tiled=T...  14.2 us
    ppermute x4, starting transfers between devices, exchange(): return lax.ppermute(message, axes, pairs + [(j, i) for i, j in pairs])  10.1 us
    pallas_call x1, Pallas kernels, body(): pl.pallas_call(solve, out_shape=[like(*velocity.shape), like(*shape)], in...  2.01 us
    pallas_call x1, Pallas kernels, body(): pl.pallas_call(pack_rims, out_shape=[held(rim_rows, rows_y), held(rim_row...  1.29 us
    pallas_call x1, Pallas kernels, body(): pl.pallas_call(tracer_kernel, out_shape=[like(*tracers.shape), held(*velo...  0.95 us
  transfers between devices with their start and end apart: 5, of which 2 were waited for; matrix products, arithmetic and copies ran while one was open for 0% of the time, Pallas kernels for 5%

profile of v15, /device:TPU:0, one launch (start us, length us, event | category | flops | bytes accessed | tf_op | source)
XLA Modules:
  0.0 30.7 jit_solution(13449915312126996374)
XLA Ops:
  0.6 1.3 %shard_map.76 = (f32[81,128]{1,0:T(8,128)S(1)}, f32[81,128]{1,0:T(8,128)S(1)}, f32[8,128]{1,0:T(8,128)S(1)}, f32[8,128]{1,0:T(8,128)S(1)}, f32[2,20,8,128]{3,2,1...) custom-call(f32[2,20,8,128]{3,2,1,0:T(8,128)} %tracers_in.1, ...), custom_call_target="tpu_custom_call" | custom-call | tf_op jit(solution)/shard_map/pallas_call | solution.py:505
  1.9 0.7 %collective-permute-start = (f32[8,128]{1,0:T(8,128)S(1)}, f32[8,128]{1,0:T(8,128)S(1)}, u32[]{:S(2)}, u32[]{:S(2)}) collective-permute-start(f32[8,128]{1,0:T(8,128)S(1)} %get-tuple-element.27), channel_id=1, source_target_pairs={{1,2},{2,1},{5,6},{6,5},{9,10},{10,9},{13,14},{14,13},{17,18},{18,... | collective-permute-start | bytes 12296 | tf_op jit(solution)/shard_map/ppermute | solution.py:522
  2.6 5.7 %collective-permute-start.1 = (f32[8,128]{1,0:T(8,128)S(1)}, f32[8,128]{1,0:T(8,128)S(1)}, u32[]{:S(2)}, u32[]{:S(2)}) collective-permute-start(f32[8,128]{1,0:T(8,128)S(1)} %get-tuple-element.28), channel_id=1, source_target_pairs={{0,1},{2,3},{1,0},{3,2},{4,5},{6,7},{5,4},{7,6},{8,9},{10,11},{9,8... | collective-permute-start | bytes 12296 | tf_op jit(solution)/shard_map/ppermute | solution.py:522
  8.3 0.7 %collective-permute-start.2 = (f32[81,128]{1,0:T(8,128)S(1)}, f32[81,128]{1,0:T(8,128)S(1)}, u32[]{:S(2)}, u32[]{:S(2)}) collective-permute-start(f32[81,128]{1,0:T(8,128)S(1)} %get-tuple-element.30.own_b), channel_id=1, source_target_pairs={{4,8},{12,16},{20,24},{8,4},{16,12},{24,20},{5,9},{13,17},{21,25},... | collective-permute-start | bytes 124424 | tf_op jit(solution)/shard_map/ppermute | solution.py:522
  9.0 3.0 %collective-permute-start.3 = (f32[81,128]{1,0:T(8,128)S(1)}, f32[81,128]{1,0:T(8,128)S(1)}, u32[]{:S(2)}, u32[]{:S(2)}) collective-permute-start(f32[81,128]{1,0:T(8,128)S(1)} %get-tuple-element.32.own_a), channel_id=1, source_target_pairs={{0,4},{8,12},{16,20},{24,28},{4,0},{12,8},{20,16},{28,24},{1,5},{9... | collective-permute-start | bytes 124424 | tf_op jit(solution)/shard_map/ppermute | solution.py:522
  12.1 0.0 collective-permute-done.cols_b
  12.1 0.0 collective-permute-done.1.cols_a
  12.1 0.5 %shard_map.77 = (f32[2,20,8,128]{3,2,1,0:T(8,128)S(1)}, f32[2,8,128]{2,1,0:T(8,128)S(1)}, f32[20,128]{1,0:T(8,128)S(1)}, f32[20,128]{1,0:T(8,128)S(1)}) custom-call(f32[2,20,8,128]{3,2,1,0:T(8,128)S(1)} %get-tuple-element.23.tracers, f32[2,20,8,128]{3,2,1,0:T(8,128)S(1)} %get-tuple-element.25.velocity, s32[8,128]{1,0:T(8,128)S(1)} %get-tuple-element.24.wet.refs_3_, ...), custom_call_target="tpu_custom_call" | custom-call | tf_op jit(solution)/shard_map/pallas_call | solution.py:533
  12.6 0.0 collective-permute-done.2.across_b.rows_b
  12.6 0.3 %collective-permute-done.3.across_a.rows_a = f32[81,128]{1,0:T(8,128)S(1)} collective-permute-done((f32[81,128]{1,0:T(8,128)S(1)}, f32[81,128]{1,0:T(8,128)S(1)}, u32[]{:S(2)}, u32[]{:S(2)}) %collective-permute-start.3) | collective-permute-done | bytes 41504 | tf_op jit(solution)/shard_map/ppermute | solution.py:522
  12.9 0.3 shard_map.78
  13.1 14.2 %all_to_all.5.after_gather = f32[16,19,1,128]{3,2,1,0:T(1,128)S(1)} all-to-all(f32[16,19,1,128]{3,2,1,0:T(1,128)S(1)} %get-tuple-element.38), channel_id=1, replica_groups=mesh['z'=4,'core'=2,'by'=4] {'by','z'}, dimensions={0} | all-to-all | bytes 311296 | tf_op jit(solution)/shard_map/all_to_all | solution.py:547
  27.3 0.0 collective-permute-start.4
  27.3 1.0 %shard_map.79 = (f32[2,20,8,128]{3,2,1,0:T(8,128)}, f32[2,20,8,128]{3,2,1,0:T(8,128)S(1)}) custom-call(f32[2,20,8,128]{3,2,1,0:T(8,128)S(1)} %get-tuple-element.23.tracers, s32[8,128]{1,0:T(8,128)S(1)} %get-tuple-element.24.wet.refs_3_, f32[2,20,8,128]{3,2,1,0:T(8,128)S(1)} %get-tuple-element.29.moved, f32[2,20,128]{2,1,0:T(8,128)S(1)} %get-tuple-element.36.change_b, ...), custom_call_target="tpu_custom_call" | custom-call | tf_op jit(solution)/shard_map/pallas_call | solution.py:549
  28.3 0.4 %collective-permute-done.4 = f32[16,19,1,128]{3,2,1,0:T(1,128)S(1)} collective-permute-done((f32[16,19,1,128]{3,2,1,0:T(1,128)S(1)}, f32[16,19,1,128]{3,2,1,0:T(1,128)S(1)}, u32[]{:S(2)}, u32[]{:S(2)}) %collective-permute-start.4) | collective-permute-done | bytes 155680 | tf_op jit(solution)/shard_map/ppermute | solution.py:548
  28.7 2.0 %shard_map.80 = (f32[2,20,8,128]{3,2,1,0:T(8,128)}, f32[8,128]{1,0:T(8,128)}) custom-call(f32[304,128]{1,0:T(8,128)S(1)} %bitcast.2, f32[304,128]{1,0:T(8,128)S(1)} %bitcast.3, f32[2,20,8,128]{3,2,1,0:T(8,128)S(1)} %get-tuple-element.40.refs_2_, s32[8,128]{1,0:T(8,128)S(1)} %get-tuple-element.24.wet.refs_3_), custom_call_target="tpu_custom_call" | custom-call | tf_op jit(solution)/shard_map/pallas_call | solution.py:564
  (1 shorter events, 0.0 us)
Async XLA Ops:
  1.9 10.1 %collective-permute-start = (f32[8,128]{1,0:T(8,128)S(1)}, f32[8,128]{1,0:T(8,128)S(1)}, u32[]{:S(2)}, u32[]{:S(2)}) collective-permute-start(f32[8,128]{1,0:T(8,128)S(1)} %get-tuple-element.27), channel_id=1, source_target_pairs={{1,2},{2,1},{5,6},{6,5},{9,10},{10,9},{13,14},{14,13},{17,18},{18,... | collective-permute-start | bytes 12296 | tf_op jit(solution)/shard_map/ppermute | solution.py:522
  2.6 9.5 %collective-permute-start.1 = (f32[8,128]{1,0:T(8,128)S(1)}, f32[8,128]{1,0:T(8,128)S(1)}, u32[]{:S(2)}, u32[]{:S(2)}) collective-permute-start(f32[8,128]{1,0:T(8,128)S(1)} %get-tuple-element.28), channel_id=1, source_target_pairs={{0,1},{2,3},{1,0},{3,2},{4,5},{6,7},{5,4},{7,6},{8,9},{10,11},{9,8... | collective-permute-start | bytes 12296 | tf_op jit(solution)/shard_map/ppermute | solution.py:522
  8.3 4.2 %collective-permute-start.2 = (f32[81,128]{1,0:T(8,128)S(1)}, f32[81,128]{1,0:T(8,128)S(1)}, u32[]{:S(2)}, u32[]{:S(2)}) collective-permute-start(f32[81,128]{1,0:T(8,128)S(1)} %get-tuple-element.30.own_b), channel_id=1, source_target_pairs={{4,8},{12,16},{20,24},{8,4},{16,12},{24,20},{5,9},{13,17},{21,25},... | collective-permute-start | bytes 124424 | tf_op jit(solution)/shard_map/ppermute | solution.py:522
  9.0 3.9 %collective-permute-start.3 = (f32[81,128]{1,0:T(8,128)S(1)}, f32[81,128]{1,0:T(8,128)S(1)}, u32[]{:S(2)}, u32[]{:S(2)}) collective-permute-start(f32[81,128]{1,0:T(8,128)S(1)} %get-tuple-element.32.own_a), channel_id=1, source_target_pairs={{0,4},{8,12},{16,20},{24,28},{4,0},{12,8},{20,16},{28,24},{1,5},{9... | collective-permute-start | bytes 124424 | tf_op jit(solution)/shard_map/ppermute | solution.py:522
  27.3 1.4 %collective-permute-start.4 = (f32[16,19,1,128]{3,2,1,0:T(1,128)S(1)}, f32[16,19,1,128]{3,2,1,0:T(1,128)S(1)}, u32[]{:S(2)}, u32[]{:S(2)}) collective-permute-start(f32[16,19,1,128]{3,2,1,0:T(1,128)S(1)} %all_to_all.5.after_gather), channel_id=1, source_target_pairs={{0,4},{4,0},{1,5},{5,1},{2,6},{6,2},{3,7},{7,3},{8,12},{12,8},{9,1... | collective-permute-start | bytes 466952 | tf_op jit(solution)/shard_map/ppermute | solution.py:548
